TPU v7x, 128 devices: a whole 4x4x4 slice. The times are simulated.
128 devices in a mesh: ctx: 8 (over z, core), fsdp: 16 (over y, x).
Axes of the slice: x: 4, y: 4, z: 4, core: 2. Of those that a mesh axis runs over, the one named last changes fastest.
Arguments:
- tokens: bfloat16 [16, 1024, 2048], P('fsdp', 'ctx'), may hold values from -6 to 6
- segments: int32 [16, 1024], P('fsdp', 'ctx'), may hold values from 0 to 3, as said below
- ln_gain: bfloat16 [2048], P('fsdp'), may hold values from 0.5 to 1.5
- ln_shift: bfloat16 [2048], P('fsdp'), may hold values from -3 to 3
- qkv_weight: bfloat16 [2048, 6144], P('fsdp'), may hold values from -0.125 to 0.125
- qkv_bias: bfloat16 [6144], P('fsdp'), may hold values from -3 to 3
- proj_weight: bfloat16 [2048, 2048], P('fsdp'), may hold values from -1 to 1
- proj_bias: bfloat16 [2048], P('fsdp'), may hold values from -3 to 3
- up_weight: bfloat16 [2048, 8192], P('fsdp'), may hold values from -0.125 to 0.125
- up_bias: bfloat16 [8192], P('fsdp'), may hold values from -3 to 3
- down_weight: bfloat16 [8192, 2048], P('fsdp'), may hold values from -0.0625 to 0.0625
- down_bias: bfloat16 [2048], P('fsdp'), may hold values from -3 to 3
- cotangent: bfloat16 [16, 1024, 2048], P('fsdp', 'ctx'), may hold values from -6 to 6
Outputs:
- block_out: bfloat16 [16, 1024, 2048], P('fsdp', 'ctx')
- token_grad: bfloat16 [16, 1024, 2048], P('fsdp', 'ctx')
- log_sums: float32 [16, 32, 1024], P('fsdp', None, 'ctx')
- gain_grad: float32 [2048], P('fsdp')
- shift_grad: float32 [2048], P('fsdp')
- qkv_weight_grad: float32 [2048, 6144], P('fsdp')
- qkv_bias_grad: float32 [6144], P('fsdp')
- proj_weight_grad: float32 [2048, 2048], P('fsdp')
- proj_bias_grad: float32 [2048], P('fsdp')
- up_weight_grad: float32 [2048, 8192], P('fsdp')
- up_bias_grad: float32 [8192], P('fsdp')
- down_weight_grad: float32 [8192, 2048], P('fsdp')
- down_bias_grad: float32 [2048], P('fsdp')
Inputs may be any that keep to these rules, and one draw needn't show every extreme that they name: `segments`: along each sequence the ids never fall and every id from 0 to 3 forms one contiguous run; the run of id 1 begins at position 64 or earlier and ends within the last 128 positions.
All inputs are finite; a program needn't handle non-finite values.
Results may differ from a plain program's by a relative error of at most 0.02.
Values may be sent and summed in bfloat16 or wider, within the bound.
A program may use at most 640 MiB of HBM per device.

v0:
```python
from functools import partial
import math

import jax
import jax.numpy as jnp
from jax import lax
from jax.sharding import PartitionSpec as P

HEAD = 64
ROT_DIMS = 32
DOCS = 4


epsilon = 1e-05
masked_score = -1e30


def from_root(block, axis, source):
    block = jnp.where(lax.axis_index(axis) == source, block, jnp.zeros_like(block))
    return lax.psum(block, axis)


def passed_along(block, axis, distance):
    devices = range(lax.axis_size(axis))
    route = [(i - distance, i) for i in devices if i - distance in devices]
    return lax.ppermute(block, axis, route)


def passed_along_2(shard, axis, by):
    devices = lax.axis_size(axis)
    return lax.ppermute(shard, axis, [(i, (i + by) % devices) for i in range(devices)])


def gelu_tanh(values):
    inner_arg = 0.7978845608028654 * (values + 0.044715 * values * values * values)
    return 0.5 * values * (1.0 + jnp.tanh(inner_arg))


def rotate_heads(fields, cosine_table, sine_table):
    half = ROT_DIMS // 2
    first_half = fields[..., :half]
    second_half = fields[..., half:ROT_DIMS]
    return jnp.concatenate(
        [
            first_half * cosine_table - second_half * sine_table,
            second_half * cosine_table + first_half * sine_table,
            fields[..., ROT_DIMS:],
        ],
        axis=-1,
    )


def standardize(inputs):
    average = jnp.mean(inputs, axis=-1, keepdims=True)
    centered = inputs - average
    variance = jnp.mean(centered * centered, axis=-1, keepdims=True)
    return centered * lax.rsqrt(variance + epsilon)


def local(
    tokens,
    segments,
    ln_gain,
    ln_shift,
    qkv_weight,
    qkv_bias,
    proj_weight,
    proj_bias,
    up_weight,
    up_bias,
    down_weight,
    down_bias,
    cotangent,
):
    float_type = jnp.float32
    brain_type = jnp.bfloat16
    row_count = tokens.shape[1]
    width = tokens.shape[2]
    hidden_width = up_weight.shape[1]
    ratio = hidden_width // width
    head_count = width // HEAD
    shard_rows = ln_gain.shape[0]
    cycle_size = lax.axis_size("ctx")
    shards = lax.axis_size("fsdp")
    cycle_place = lax.axis_index("ctx")
    local_rows = jnp.arange(row_count, dtype=jnp.int32)
    row_index = cycle_place * row_count + local_rows
    score_scale = 1.0 / math.sqrt(HEAD)
    doc_kinds = jnp.arange(DOCS, dtype=jnp.int32)
    onehot = (segments[0][:, None] == doc_kinds[None, :]).astype(jnp.int32)
    beyond = jnp.int32(cycle_size * row_count)
    local_first = jnp.min(jnp.where(onehot == 1, row_index[:, None], beyond), axis=0)
    root_first = from_root(local_first, "ctx", 0)
    starts = jnp.minimum(local_first, root_first)
    begins = jnp.sum(onehot * starts[None, :], axis=1)
    positions = row_index - begins
    inverse = jnp.exp(
        jnp.arange(ROT_DIMS // 2, dtype=float_type) * (-math.log(10000.0) / (ROT_DIMS // 2))
    )
    angles = positions.astype(float_type)[:, None, None] * inverse
    cosine_table = jnp.cos(angles)
    sine_table = jnp.sin(angles)
    inputs = tokens[0].astype(float_type)
    standard, standard_pull = jax.vjp(standardize, inputs)
    gain_piece = lax.all_gather(ln_gain, "fsdp", axis=0, tiled=True)
    shift_piece = lax.all_gather(ln_shift, "fsdp", axis=0, tiled=True)
    qkv_piece = lax.all_gather(qkv_weight, "fsdp", axis=0, tiled=True)
    up_piece = lax.all_gather(up_weight, "fsdp", axis=0, tiled=True)
    qkv_bias_piece = lax.all_gather(qkv_bias.reshape(shard_rows, 3), "fsdp", axis=0, tiled=True)
    up_bias_piece = lax.all_gather(up_bias.reshape(shard_rows, ratio), "fsdp", axis=0, tiled=True)
    amount = gain_piece.shape[0]
    normed_piece = (
        standard * gain_piece.astype(float_type) + shift_piece.astype(float_type)
    ).astype(brain_type)
    mixed_sum = jnp.dot(normed_piece, qkv_piece, preferred_element_type=float_type)
    hidden_sum = jnp.dot(normed_piece, up_piece, preferred_element_type=float_type)
    normed, mixed_sum, hidden_sum, full_gain, full_shift, full_qkv_bias, full_up_bias = (
        normed_piece,
        mixed_sum,
        hidden_sum,
        gain_piece,
        shift_piece,
        qkv_bias_piece,
        up_bias_piece,
    )
    projected = mixed_sum + full_qkv_bias.reshape(3 * width).astype(float_type)
    hidden = hidden_sum + full_up_bias.reshape(hidden_width).astype(float_type)
    grouped = projected.reshape(row_count, 3, head_count, HEAD)
    turner = partial(rotate_heads, cosine_table=cosine_table, sine_table=sine_table)
    queries_wide, query_pull = jax.vjp(turner, grouped[:, 0])
    key_wide, key_pull = jax.vjp(turner, grouped[:, 1])
    queries = queries_wide.astype(brain_type)
    key_rows = key_wide.astype(brain_type)
    values = grouped[:, 2].astype(brain_type)

    def masked_scores(key_block, key_index):
        scores = (
            jnp.einsum("qhd,khd->hqk", queries, key_block, preferred_element_type=float_type)
            * score_scale
        )
        allowed = (key_index[None, :] <= row_index[:, None]) & (
            key_index[None, :] >= begins[:, None]
        )
        return jnp.where(allowed[None], scores, masked_score)

    def attend_block(running, moving, key_index):
        highest, totals, accum = running
        key_block, value_block = moving
        scores = masked_scores(key_block, key_index)
        new_high = jnp.maximum(highest, jnp.max(scores, axis=-1))
        factor = jnp.exp(highest - new_high)
        weights = jnp.exp(scores - new_high[..., None])
        totals = totals * factor + jnp.sum(weights, axis=-1)
        update = jnp.einsum(
            "hqk,khd->qhd",
            weights.astype(brain_type),
            value_block,
            preferred_element_type=float_type,
        )
        accum = accum * jnp.transpose(factor)[:, :, None] + update
        return (new_high, totals, accum)

    def forward_step(step, carried):
        running, moving = carried
        source = cycle_place - step
        running = attend_block(running, moving, source * row_count + local_rows)
        moving = passed_along((moving[0], moving[1]), "ctx", 1)
        return (running, moving)

    initial = (
        jnp.full((head_count, row_count), masked_score, float_type),
        jnp.zeros((head_count, row_count), float_type),
        jnp.zeros((row_count, head_count, HEAD), float_type),
    )
    running, moving = lax.fori_loop(0, cycle_size - 1, forward_step, (initial, (key_rows, values)))
    last_source = cycle_place - (cycle_size - 1)
    highest, totals, accum = attend_block(running, moving, last_source * row_count + local_rows)
    logsum = highest + jnp.log(totals)
    context_wide = accum / jnp.transpose(totals)[:, :, None]
    context = context_wide.reshape(row_count, width).astype(brain_type)
    active_wide, active_pull = jax.vjp(gelu_tanh, hidden)
    active = active_wide.astype(brain_type)
    down_grouped = down_weight.reshape(shard_rows, ratio, width)
    proj_piece = lax.all_gather(proj_weight, "fsdp", axis=0, tiled=True)
    down_piece = lax.all_gather(down_grouped, "fsdp", axis=0, tiled=True)
    proj_bias_piece = lax.all_gather(proj_bias, "fsdp", axis=0, tiled=True)
    down_bias_piece = lax.all_gather(down_bias, "fsdp", axis=0, tiled=True)
    amount = proj_piece.shape[0]
    out_sum = jnp.dot(context, proj_piece, preferred_element_type=float_type)
    out_sum = out_sum + jnp.dot(
        active, down_piece.reshape(amount * ratio, width), preferred_element_type=float_type
    )
    out_sum, full_proj_bias, full_down_bias = (out_sum, proj_bias_piece, down_bias_piece)
    block_out = (
        inputs + out_sum + full_proj_bias.astype(float_type) + full_down_bias.astype(float_type)
    ).astype(brain_type)
    upstream = cotangent[0]
    upstream_wide = upstream.astype(float_type)
    contract_last = (((1,), (1,)), ((), ()))
    proj_piece = lax.all_gather(proj_weight, "fsdp", axis=0, tiled=True)
    down_piece = lax.all_gather(down_grouped, "fsdp", axis=0, tiled=True)
    context_part = lax.dot_general(
        upstream, proj_piece, contract_last, preferred_element_type=float_type
    )
    down_part = jnp.einsum("rd,cjd->jrc", upstream, down_piece, preferred_element_type=float_type)
    fresh = jnp.concatenate([context_part[None], down_part], axis=0)
    back_cols = fresh
    d_active = jnp.transpose(back_cols[1:], (1, 2, 0)).reshape(row_count, hidden_width)
    d_hidden = active_pull(d_active)[0].astype(brain_type)
    d_context = back_cols[0].astype(brain_type).reshape(row_count, head_count, HEAD)
    delta = jnp.transpose(jnp.sum(d_context.astype(float_type) * context_wide, axis=-1))

    def grad_block(moving, key_index):
        key_block, value_block = moving
        scores = masked_scores(key_block, key_index)
        probs = jnp.exp(scores - logsum[..., None])
        d_probs = jnp.einsum(
            "qhd,khd->hqk", d_context, value_block, preferred_element_type=float_type
        )
        d_scores = (probs * (d_probs - delta[..., None])).astype(brain_type)
        query_part = (
            jnp.einsum("hqk,khd->qhd", d_scores, key_block, preferred_element_type=float_type)
            * score_scale
        )
        key_part = (
            jnp.einsum("hqk,qhd->khd", d_scores, queries, preferred_element_type=float_type)
            * score_scale
        )
        value_part = jnp.einsum(
            "hqk,qhd->khd", probs.astype(brain_type), d_context, preferred_element_type=float_type
        )
        return (query_part, key_part, value_part)

    def pass_grads(moving_grads):
        return (
            passed_along_2(moving_grads[0].astype(jnp.bfloat16), "ctx", 1).astype(jnp.float32),
            passed_along_2(moving_grads[1].astype(jnp.bfloat16), "ctx", 1).astype(jnp.float32),
        )

    def backward_step(step, carried):
        d_queries, moving, moving_grads = carried
        source = cycle_place - step
        query_part, key_part, value_part = grad_block(moving, source * row_count + local_rows)
        moving_grads = pass_grads((moving_grads[0] + key_part, moving_grads[1] + value_part))
        moving = passed_along((moving[0], moving[1]), "ctx", 1)
        return (d_queries + query_part, moving, moving_grads)

    zero_block = jnp.zeros((row_count, head_count, HEAD), float_type)
    d_queries, moving, moving_grads = lax.fori_loop(
        0, cycle_size - 1, backward_step, (zero_block, (key_rows, values), (zero_block, zero_block))
    )
    query_part, key_part, value_part = grad_block(moving, last_source * row_count + local_rows)
    d_queries = d_queries + query_part
    d_keys, d_values = pass_grads((moving_grads[0] + key_part, moving_grads[1] + value_part))
    d_projected = jnp.stack([query_pull(d_queries)[0], key_pull(d_keys)[0], d_values], axis=1)
    d_projected = d_projected.reshape(row_count, 3 * width).astype(brain_type)
    qkv_piece = lax.all_gather(qkv_weight, "fsdp", axis=0, tiled=True)
    up_piece = lax.all_gather(up_weight, "fsdp", axis=0, tiled=True)
    fresh = lax.dot_general(
        d_projected, qkv_piece, contract_last, preferred_element_type=float_type
    )
    fresh = fresh + lax.dot_general(
        d_hidden, up_piece, contract_last, preferred_element_type=float_type
    )
    d_inputs = standard_pull(fresh * full_gain.astype(float_type))[0]
    token_grad = (upstream_wide + d_inputs).astype(brain_type)
    d_gain = jnp.sum(fresh * standard, axis=0)
    d_shift = jnp.sum(fresh, axis=0)
    d_out_bias = jnp.sum(upstream_wide, axis=0)
    d_qkv_bias = jnp.sum(d_projected.astype(float_type), axis=0)
    d_up_bias = jnp.sum(d_hidden.astype(float_type), axis=0)
    vector_term = jnp.concatenate(
        [
            jnp.stack([d_gain, d_shift, d_out_bias, d_out_bias], axis=1),
            d_qkv_bias.reshape(width, 3),
            d_up_bias.reshape(width, ratio),
        ],
        axis=1,
    )

    def term_maker(normed_left, context_left, active_left):
        contract_first = (((0,), (0,)), ((), ()))

        def term_rows(offset, amount):
            grad_qkv = lax.dot_general(
                normed_left, d_projected, contract_first, preferred_element_type=float_type
            )
            grad_proj = lax.dot_general(
                context_left, upstream, contract_first, preferred_element_type=float_type
            )
            grad_up = lax.dot_general(
                normed_left, d_hidden, contract_first, preferred_element_type=float_type
            )
            grad_down = lax.dot_general(
                active_left, upstream, contract_first, preferred_element_type=float_type
            )
            return jnp.concatenate(
                [grad_qkv, grad_proj, grad_up, grad_down.reshape(amount, ratio * width)], axis=1
            )

        return term_rows

    term_rows = term_maker(normed, context, active)
    matrix_part = lax.psum_scatter(
        term_rows(jnp.int32(0), width // shards * lax.axis_size("fsdp")).astype(jnp.bfloat16),
        "fsdp",
        scatter_dimension=0,
        tiled=True,
    )
    vector_part = lax.psum_scatter(
        vector_term.astype(jnp.bfloat16), "fsdp", scatter_dimension=0, tiled=True
    )
    matrix_shard, vector_shard = (
        lax.psum(matrix_part, "ctx").astype(jnp.float32),
        lax.psum(vector_part, "ctx").astype(jnp.float32),
    )
    qkv_weight_grad = matrix_shard[:, : 3 * width]
    proj_weight_grad = matrix_shard[:, 3 * width : 4 * width]
    up_weight_grad = matrix_shard[:, 4 * width : 4 * width + hidden_width]
    down_weight_grad = matrix_shard[:, 4 * width + hidden_width :].reshape(
        shard_rows * ratio, width
    )
    return (
        block_out[None],
        token_grad[None],
        logsum[None],
        vector_shard[:, 0],
        vector_shard[:, 1],
        qkv_weight_grad,
        vector_shard[:, 4:7].reshape(3 * shard_rows),
        proj_weight_grad,
        vector_shard[:, 2],
        up_weight_grad,
        vector_shard[:, 7 : 7 + ratio].reshape(ratio * shard_rows),
        down_weight_grad,
        vector_shard[:, 3],
    )


def solution(mesh):
    in_specs = (
        P("fsdp", "ctx", None),
        P("fsdp", "ctx"),
        P("fsdp"),
        P("fsdp"),
        P("fsdp", None),
        P("fsdp"),
        P("fsdp", None),
        P("fsdp"),
        P("fsdp", None),
        P("fsdp"),
        P("fsdp", None),
        P("fsdp"),
        P("fsdp", "ctx", None),
    )
    out_specs = (
        P("fsdp", "ctx", None),
        P("fsdp", "ctx", None),
        P("fsdp", None, "ctx"),
        P("fsdp"),
        P("fsdp"),
        P("fsdp", None),
        P("fsdp"),
        P("fsdp", None),
        P("fsdp"),
        P("fsdp", None),
        P("fsdp"),
        P("fsdp", None),
        P("fsdp"),
    )
    return jax.shard_map(local, mesh=mesh, in_specs=in_specs, out_specs=out_specs, check_vma=False)
```

profile of v0, /device:TPU:1, one launch (start us, length us, event | category | flops | bytes accessed | tf_op | source)
XLA Modules:
  0.0 1614.3 jit_solution(9181833733876596031)
XLA Ops:
  21.8 18.3 %all-gather = bf16[16,1,128]{2,1,0:T(2,128)(2,1)S(1)} all-gather(bf16[1,1,128]{2,1,0:T(2,128)(2,1)S(1)} %bitcast.236), channel_id=1, replica_groups=mesh['ctx'=8,'fsdp'=16] {'fsdp'}, dimensions={0}, use_global_device_ids=true | all-gather | bytes 4352 | tf_op jit(solution)/shard_map/all_gather | solution.py:105
  40.1 15.9 all-gather.1
  56.4 19.8 %all_gather.40 = bf16[2048,4]{1,0:T(8,128)(2,1)S(1)} all-gather(bf16[128,4]{1,0:T(8,128)(2,1)S(1)} %reshape.422), channel_id=1, replica_groups=mesh['ctx'=8,'fsdp'=16] {'fsdp'}, dimensions={0}, use_global_device_ids=true | all-gather | bytes 17408 | tf_op jit(solution)/shard_map/all_gather | solution.py:110
  77.0 19.0 %all_gather.37 = bf16[2048,3]{1,0:T(8,128)(2,1)S(1)} all-gather(bf16[128,3]{1,0:T(8,128)(2,1)S(1)} %reshape.420), channel_id=1, replica_groups=mesh['ctx'=8,'fsdp'=16] {'fsdp'}, dimensions={0}, use_global_device_ids=true | all-gather | bytes 13056 | tf_op jit(solution)/shard_map/all_gather | solution.py:109
  105.6 137.8 %all-gather.9.cloned.1.call-done = bf16[2048,6144]{1,0:T(8,128)(2,1)} async-done(((bf16[128,6144]{1,0:T(8,128)(2,1)}), bf16[2048,6144]{1,0:T(8,128)(2,1)}) %all-gather.9.cloned.1.call-update) | async-done | bytes 25165840 | tf_op jit(solution)/shard_map/all_gather | solution.py:107
  243.5 13.4 convolution_add_fusion.1
  270.3 120.2 %while.44 = (s32[]{:T(128)}, f32[32,128]{1,0:T(8,128)S(1)}, f32[32,128]{1,0:T(8,128)S(1)}, f32[128,32,64]{0,2,1:T(8,128)S(1)}, bf16[128,32,64]{0,2,1:T(8,128)(2,...) while((s32[]{:T(128)}, f32[32,128]{1,0:T(8,128)S(1)}, ...), condition=%wide.region_8.9_spmd.clone, body=%wide.region_5.8_spmd.clone.sunk | while | flops 140845312 | bytes 16583425 | solution.py:175
  395.5 220.0 %while.45 = (s32[]{:T(128)}, f32[128,32,64]{0,2,1:T(8,128)}, bf16[128,32,64]{0,2,1:T(8,128)(2,1)}, bf16[128,32,64]{0,2,1:T(8,128)(2,1)}, f32[128,32,64]{0,2,1:T(...) while((s32[]{:T(128)}, f32[128,32,64]{0,2,1:T(8,128)}, ...), condition=%wide.region_13.14_spmd.clone, body=%wide.region_12.13_spmd.clone.sunk | while | flops 342409472 | bytes 40438680 | solution.py:249
  660.0 17.2 %convolution_add_fusion = f32[128,8192]{1,0:T(8,128)} fusion(bf16[2048,8192]{1,0:T(8,128)(2,1)} %all-gather.13.cloned.1.call-done, f32[8192]{0:T(1024)S(1)} %reshape.433, bf16[1,128,2048]{2,1,0:T(8,128)(2,1)S(1)} %copy-done.1, f32[2048]{0:T(1024)S(1)} %bitcast.230, f32[2048]{0:T(1024)S(1)} %bitcast.223, f32[128]{0:T(128)S(1)} %fusion.92, ...), kind=kOutput, calls=%fused_computation.46 | convolution fusion | flops 4297588736 | bytes 38323200 | tf_op jit(solution)/shard_map/dot_general | solution.py:116
  677.2 16.1 convolution_convert_fusion.1
  693.3 45.8 %reshape.424 = bf16[8192,2048]{1,0:T(8,128)(2,1)} reshape(bf16[2048,4,2048]{2,1,0:T(4,128)(2,1)} %all-gather.15.cloned.1.call-done) | data formatting | bytes 67108864 | tf_op jit(solution)/shard_map/reshape | solution.py:191
  739.1 19.9 %fusion.106 = (bf16[8192]{0:T(1024)(128)(2,1)S(1)}, bf16[128,8192]{1,0:T(8,128)(2,1)}) fusion(f32[128,8192]{1,0:T(8,128)} %convolution_add_fusion, bf16[8192,2048]{1,0:T(8,128)(2,1)} %reshape.424, bf16[1,128,2048]{2,1,0:T(8,128)(2,1)S(1)} %copy-done.10), kind=kOutput, calls=%fused_computation.180 | convolution fusion | flops 4321173504 | bytes 40386560 | tf_op jit(solution)/shard_map/rd,cjd->jrc/dot_general | solution.py:205
  759.0 55.1 %reshape.428 = bf16[2048,8192]{1,0:T(8,128)(2,1)} reshape(bf16[8192,2048]{1,0:T(8,128)(2,1)} %convolution_convert_fusion.1) | data formatting | bytes 67108864 | tf_op jit(solution)/shard_map/reshape | solution.py:298
  814.0 15.8 convolution_convert_fusion
  829.9 65.9 %pad_maximum_fusion = bf16[2048,24576]{1,0:T(8,128)(2,1)} fusion(bf16[2048,8192]{1,0:T(8,128)(2,1)} %reshape.428, bf16[2048,8192]{1,0:T(8,128)(2,1)} %convolution_convert_fusion, bf16[2048,2048]{1,0:T(8,128)(2,1)} %copy.101, bf16[2048,6144]{1,0:T(8,128)(2,1)} %convolution_convert_fusion.2), kind=kLoop, calls=%fused_computation.42 | loop fusion | flops 402653184 | bytes 201326592 | tf_op jit(solution)/shard_map/concatenate | solution.py:297
  897.8 17.6 %fusion.108 = f32[128,2048]{1,0:T(8,128)} fusion(bf16[128,8192]{1,0:T(8,128)(2,1)} %get-tuple-element.618, bf16[2048,8192]{1,0:T(8,128)(2,1)} %all-gather.13.cloned.1.call-done), kind=kOutput, calls=%fused_computation.182 | convolution fusion | flops 4294967296 | bytes 36700160 | tf_op jit(solution)/shard_map/dot_general | solution.py:262
  915.5 15.1 fusion.103
  935.2 19.0 %all-gather.2 = bf16[16,1,128]{2,1,0:T(2,128)(2,1)S(1)} all-gather(bf16[1,1,128]{2,1,0:T(2,128)(2,1)S(1)} %bitcast.238), channel_id=1, replica_groups=mesh['ctx'=8,'fsdp'=16] {'fsdp'}, dimensions={0}, use_global_device_ids=true | all-gather | bytes 4352 | tf_op jit(solution)/shard_map/all_gather | solution.py:186
  954.2 17.2 %all-gather.3 = bf16[16,1,128]{2,1,0:T(2,128)(2,1)S(1)} all-gather(bf16[1,1,128]{2,1,0:T(2,128)(2,1)S(1)} %bitcast.239), channel_id=1, replica_groups=mesh['ctx'=8,'fsdp'=16] {'fsdp'}, dimensions={0}, use_global_device_ids=true | all-gather | bytes 4352 | tf_op jit(solution)/shard_map/all_gather | solution.py:187
  971.4 456.7 %reduce-scatter.5.cloned.1.call-done = bf16[128,24576]{1,0:T(8,128)(2,1)} async-done(((bf16[2048,24576]{1,0:T(8,128)(2,1)}), bf16[128,24576]{1,0:T(8,128)(2,1)}) %reduce-scatter.5.cloned.1.call-update) | async-done | bytes 6291472 | tf_op jit(solution)/shard_map/reduce_scatter | solution.py:304
  1434.2 17.9 %fusion.41 = bf16[1,128,2048]{2,1,0:T(8,128)(2,1)} fusion(f32[128,2048]{1,0:T(8,128)S(1)} %fusion.107, bf16[8192,2048]{1,0:T(8,128)(2,1)} %reshape.424, bf16[1,128,2048]{2,1,0:T(8,128)(2,1)S(1)} %copy-done.1, f32[2048]{0:T(1024)S(1)} %bitcast.235, f32[2048]{0:T(1024)S(1)} %bitcast.234, f32[128,8192]{1,0:T(8,128)} %convolution_add_fusion), kind=kOutput, calls=%fused_computation.69 | convolution fusion | flops 4305977344 | bytes 39862272 | tf_op jit(solution)/shard_map/dot_general | solution.py:190
  1452.1 50.2 %reduce-scatter.7.cloned.1.call-done = bf16[128,11]{1,0:T(8,128)(2,1)} async-done(((bf16[2048,11]{1,0:T(8,128)(2,1)}), bf16[128,11]{1,0:T(8,128)(2,1)}) %reduce-scatter.7.cloned.1.call-update) | async-done | bytes 2832
  1503.1 14.2 psum.22
  1519.6 70.1 %all-reduce.8.cloned.1.call-done = bf16[128,24576]{1,0:T(8,128)(2,1)} async-done(((bf16[128,24576]{1,0:T(8,128)(2,1)}), bf16[128,24576]{1,0:T(8,128)(2,1)}) %all-reduce.8.cloned.1.call-update) | async-done | bytes 6291472 | tf_op jit(solution)/shard_map/psum | solution.py:314
  (439 shorter events, 459.4 us)
Async XLA Ops:
  7.2 90.9 %all-gather.11.cloned.1.call-start = ((), (), s32[]{:S(2)}) async-start(), calls=%async_computation.3 | async-start | bytes 8912896 | tf_op jit(solution)/shard_map/all_gather | solution.py:184
  7.9 235.6 %all-gather.9.cloned.1.call-start = ((), (), s32[]{:S(2)}) async-start(), calls=%async_computation.2 | async-start | bytes 26738688 | tf_op jit(solution)/shard_map/all_gather | solution.py:107
  8.7 651.2 %all-gather.13.cloned.1.call-start = ((), (), s32[]{:S(2)}) async-start(), calls=%async_computation.4 | async-start | bytes 35651584 | tf_op jit(solution)/shard_map/all_gather | solution.py:108
  9.5 683.8 %all-gather.15.cloned.1.call-start = ((), (), s32[]{:S(2)}) async-start(), calls=%async_computation.5 | async-start | bytes 35651584 | tf_op jit(solution)/shard_map/all_gather | solution.py:185
  11.8 1416.4 %reduce-scatter.5.cloned.1.call-start = ((), (), s32[]{:S(2)}) async-start(), calls=%async_computation.6 | async-start | bytes 106954752 | tf_op jit(solution)/shard_map/reduce_scatter | solution.py:304
  404.9 16.3 %collective-permute-start.3 = (bf16[128,32,64]{0,2,1:T(8,128)(2,1)S(1)}, bf16[128,32,64]{0,2,1:T(8,128)(2,1)}, u32[]{:S(2)}, u32[]{:S(2)}) collective-permute-start(bf16[128,32,64]{0,2,1:T(8,128)(2,1)S(1)} %copy.140), channel_id=1, source_target_pairs={{0,16},{16,32},{32,48},{48,64},{64,80},{80,96},{96,112},{1,17},{17... | collective-permute-start | bytes 1572872 | tf_op jit(solution)/shard_map/while/body/eval_jaxpr/ppermute | solution.py:26
  408.5 18.4 %collective-permute-start.2 = (bf16[128,32,64]{0,2,1:T(8,128)(2,1)S(1)}, bf16[128,32,64]{0,2,1:T(8,128)(2,1)}, u32[]{:S(2)}, u32[]{:S(2)}) collective-permute-start(bf16[128,32,64]{0,2,1:T(8,128)(2,1)S(1)} %copy.139), channel_id=1, source_target_pairs={{0,16},{16,32},{32,48},{48,64},{64,80},{80,96},{96,112},{1,17},{17... | collective-permute-start | bytes 1572872 | tf_op jit(solution)/shard_map/while/body/eval_jaxpr/ppermute | solution.py:26
  436.2 16.3 %collective-permute-start.3 = (bf16[128,32,64]{0,2,1:T(8,128)(2,1)S(1)}, bf16[128,32,64]{0,2,1:T(8,128)(2,1)}, u32[]{:S(2)}, u32[]{:S(2)}) collective-permute-start(bf16[128,32,64]{0,2,1:T(8,128)(2,1)S(1)} %copy.140), channel_id=1, source_target_pairs={{0,16},{16,32},{32,48},{48,64},{64,80},{80,96},{96,112},{1,17},{17... | collective-permute-start | bytes 1572872 | tf_op jit(solution)/shard_map/while/body/eval_jaxpr/ppermute | solution.py:26
  439.8 18.4 %collective-permute-start.2 = (bf16[128,32,64]{0,2,1:T(8,128)(2,1)S(1)}, bf16[128,32,64]{0,2,1:T(8,128)(2,1)}, u32[]{:S(2)}, u32[]{:S(2)}) collective-permute-start(bf16[128,32,64]{0,2,1:T(8,128)(2,1)S(1)} %copy.139), channel_id=1, source_target_pairs={{0,16},{16,32},{32,48},{48,64},{64,80},{80,96},{96,112},{1,17},{17... | collective-permute-start | bytes 1572872 | tf_op jit(solution)/shard_map/while/body/eval_jaxpr/ppermute | solution.py:26
  467.6 16.3 %collective-permute-start.3 = (bf16[128,32,64]{0,2,1:T(8,128)(2,1)S(1)}, bf16[128,32,64]{0,2,1:T(8,128)(2,1)}, u32[]{:S(2)}, u32[]{:S(2)}) collective-permute-start(bf16[128,32,64]{0,2,1:T(8,128)(2,1)S(1)} %copy.140), channel_id=1, source_target_pairs={{0,16},{16,32},{32,48},{48,64},{64,80},{80,96},{96,112},{1,17},{17... | collective-permute-start | bytes 1572872 | tf_op jit(solution)/shard_map/while/body/eval_jaxpr/ppermute | solution.py:26
  471.2 18.4 %collective-permute-start.2 = (bf16[128,32,64]{0,2,1:T(8,128)(2,1)S(1)}, bf16[128,32,64]{0,2,1:T(8,128)(2,1)}, u32[]{:S(2)}, u32[]{:S(2)}) collective-permute-start(bf16[128,32,64]{0,2,1:T(8,128)(2,1)S(1)} %copy.139), channel_id=1, source_target_pairs={{0,16},{16,32},{32,48},{48,64},{64,80},{80,96},{96,112},{1,17},{17... | collective-permute-start | bytes 1572872 | tf_op jit(solution)/shard_map/while/body/eval_jaxpr/ppermute | solution.py:26
  495.2 12.7 collective-permute-start.4
  499.0 16.3 %collective-permute-start.3 = (bf16[128,32,64]{0,2,1:T(8,128)(2,1)S(1)}, bf16[128,32,64]{0,2,1:T(8,128)(2,1)}, u32[]{:S(2)}, u32[]{:S(2)}) collective-permute-start(bf16[128,32,64]{0,2,1:T(8,128)(2,1)S(1)} %copy.140), channel_id=1, source_target_pairs={{0,16},{16,32},{32,48},{48,64},{64,80},{80,96},{96,112},{1,17},{17... | collective-permute-start | bytes 1572872 | tf_op jit(solution)/shard_map/while/body/eval_jaxpr/ppermute | solution.py:26
  502.6 18.4 %collective-permute-start.2 = (bf16[128,32,64]{0,2,1:T(8,128)(2,1)S(1)}, bf16[128,32,64]{0,2,1:T(8,128)(2,1)}, u32[]{:S(2)}, u32[]{:S(2)}) collective-permute-start(bf16[128,32,64]{0,2,1:T(8,128)(2,1)S(1)} %copy.139), channel_id=1, source_target_pairs={{0,16},{16,32},{32,48},{48,64},{64,80},{80,96},{96,112},{1,17},{17... | collective-permute-start | bytes 1572872 | tf_op jit(solution)/shard_map/while/body/eval_jaxpr/ppermute | solution.py:26
  530.4 16.3 %collective-permute-start.3 = (bf16[128,32,64]{0,2,1:T(8,128)(2,1)S(1)}, bf16[128,32,64]{0,2,1:T(8,128)(2,1)}, u32[]{:S(2)}, u32[]{:S(2)}) collective-permute-start(bf16[128,32,64]{0,2,1:T(8,128)(2,1)S(1)} %copy.140), channel_id=1, source_target_pairs={{0,16},{16,32},{32,48},{48,64},{64,80},{80,96},{96,112},{1,17},{17... | collective-permute-start | bytes 1572872 | tf_op jit(solution)/shard_map/while/body/eval_jaxpr/ppermute | solution.py:26
  533.9 18.4 %collective-permute-start.2 = (bf16[128,32,64]{0,2,1:T(8,128)(2,1)S(1)}, bf16[128,32,64]{0,2,1:T(8,128)(2,1)}, u32[]{:S(2)}, u32[]{:S(2)}) collective-permute-start(bf16[128,32,64]{0,2,1:T(8,128)(2,1)S(1)} %copy.139), channel_id=1, source_target_pairs={{0,16},{16,32},{32,48},{48,64},{64,80},{80,96},{96,112},{1,17},{17... | collective-permute-start | bytes 1572872 | tf_op jit(solution)/shard_map/while/body/eval_jaxpr/ppermute | solution.py:26
  561.8 16.3 %collective-permute-start.3 = (bf16[128,32,64]{0,2,1:T(8,128)(2,1)S(1)}, bf16[128,32,64]{0,2,1:T(8,128)(2,1)}, u32[]{:S(2)}, u32[]{:S(2)}) collective-permute-start(bf16[128,32,64]{0,2,1:T(8,128)(2,1)S(1)} %copy.140), channel_id=1, source_target_pairs={{0,16},{16,32},{32,48},{48,64},{64,80},{80,96},{96,112},{1,17},{17... | collective-permute-start | bytes 1572872 | tf_op jit(solution)/shard_map/while/body/eval_jaxpr/ppermute | solution.py:26
  565.3 18.4 %collective-permute-start.2 = (bf16[128,32,64]{0,2,1:T(8,128)(2,1)S(1)}, bf16[128,32,64]{0,2,1:T(8,128)(2,1)}, u32[]{:S(2)}, u32[]{:S(2)}) collective-permute-start(bf16[128,32,64]{0,2,1:T(8,128)(2,1)S(1)} %copy.139), channel_id=1, source_target_pairs={{0,16},{16,32},{32,48},{48,64},{64,80},{80,96},{96,112},{1,17},{17... | collective-permute-start | bytes 1572872 | tf_op jit(solution)/shard_map/while/body/eval_jaxpr/ppermute | solution.py:26
  593.1 16.3 %collective-permute-start.3 = (bf16[128,32,64]{0,2,1:T(8,128)(2,1)S(1)}, bf16[128,32,64]{0,2,1:T(8,128)(2,1)}, u32[]{:S(2)}, u32[]{:S(2)}) collective-permute-start(bf16[128,32,64]{0,2,1:T(8,128)(2,1)S(1)} %copy.140), channel_id=1, source_target_pairs={{0,16},{16,32},{32,48},{48,64},{64,80},{80,96},{96,112},{1,17},{17... | collective-permute-start | bytes 1572872 | tf_op jit(solution)/shard_map/while/body/eval_jaxpr/ppermute | solution.py:26
  596.7 18.4 %collective-permute-start.2 = (bf16[128,32,64]{0,2,1:T(8,128)(2,1)S(1)}, bf16[128,32,64]{0,2,1:T(8,128)(2,1)}, u32[]{:S(2)}, u32[]{:S(2)}) collective-permute-start(bf16[128,32,64]{0,2,1:T(8,128)(2,1)S(1)} %copy.139), channel_id=1, source_target_pairs={{0,16},{16,32},{32,48},{48,64},{64,80},{80,96},{96,112},{1,17},{17... | collective-permute-start | bytes 1572872 | tf_op jit(solution)/shard_map/while/body/eval_jaxpr/ppermute | solution.py:26
  620.8 23.8 %collective-permute-start.6 = (bf16[128,32,64]{0,2,1:T(8,128)(2,1)}, bf16[128,32,64]{0,2,1:T(8,128)(2,1)S(1)}, u32[]{:S(2)}, u32[]{:S(2)}) collective-permute-start(bf16[128,32,64]{0,2,1:T(8,128)(2,1)} %fusion.58), channel_id=1, source_target_pairs={{0,16},{16,32},{32,48},{48,64},{64,80},{80,96},{96,112},{112,0},{1... | collective-permute-start | bytes 1572872 | tf_op jit(solution)/shard_map/ppermute | solution.py:31
  625.1 20.1 %collective-permute-start.7 = (bf16[128,32,64]{0,2,1:T(8,128)(2,1)}, bf16[128,32,64]{0,2,1:T(8,128)(2,1)}, u32[]{:S(2)}, u32[]{:S(2)}) collective-permute-start(bf16[128,32,64]{0,2,1:T(8,128)(2,1)} %fusion.57), channel_id=1, source_target_pairs={{0,16},{16,32},{32,48},{48,64},{64,80},{80,96},{96,112},{112,0},{1... | collective-permute-start | bytes 1572872 | tf_op jit(solution)/shard_map/ppermute | solution.py:31
  895.8 606.5 %reduce-scatter.7.cloned.1.call-start = ((), (), s32[]{:S(2)}) async-start(), calls=%async_computation.8 | async-start | bytes 557056
  935.1 654.6 %all-reduce.8.cloned.1.call-start = ((), (), s32[]{:S(2)}) async-start(), calls=%async_computation.7 | async-start | bytes 12582912 | tf_op jit(solution)/shard_map/psum | solution.py:314
  (69 other events, 1323.0 us)
Sparse Core Ops, SparseCore 0:
  10.2 76.3 all-gather.10
  88.7 154.7 all-gather.8
  245.6 196.6 all-gather.12
  444.9 196.6 all-gather.14
  895.9 532.1 reduce-scatter.4
  1432.1 70.1 reduce-scatter.6
  1504.7 84.9 all-reduce.7
where the time goes:
time: 1630 us; the launch traced here: 1610 us
  waiting for transfers between devices  828 us (51%)
  matrix products  237 us (15%)
  local copies, waits for them, and re-layouts  186 us (11%)
  blocking collectives  133 us (8%)
  other arithmetic  110 us (7%)
  starting transfers between devices  103 us (6%)
    reduce_scatter x1, waiting for transfers between devices, local(): lax.psum_scatter(term_rows(jnp.int32(0), width // shards * lax.axis_size(...  457 us
    all_gather x1, waiting for transfers between devices, local(): qkv_piece = lax.all_gather(qkv_weight, 'fsdp', axis=0, tiled=True)  138 us
    ppermute x28, waiting for transfers between devices, passed_along(): return lax.ppermute(block, axis, route)  109 us
    ppermute x28, starting transfers between devices, passed_along(): return lax.ppermute(block, axis, route)  82.5 us
    psum x1, waiting for transfers between devices, local(): lax.psum(matrix_part, 'ctx').astype(jnp.float32)  70.1 us
    concatenate x1, other arithmetic, term_rows(): jnp.concatenate([grad_qkv, grad_proj, grad_up, grad_down.reshape(amount,...  65.9 us
    reshape x1, local copies, waits for them, and re-layouts, term_rows(): grad_down.reshape(amount, ratio * width)  55.1 us
    unnamed x8, waiting for transfers between devices  52.3 us
  transfers between devices with their start and end apart: 51, of which 38 were waited for; matrix products, arithmetic and copies ran while one was open for 19% of the time, Pallas kernels for 0%

commit v1 on v0

v1 whole, which is shorter than its diff:
```python
from functools import partial
import math

import jax
import jax.numpy as jnp
from jax import lax
from jax.sharding import PartitionSpec as P

HEAD = 64
ROT_DIMS = 32
DOCS = 4

epsilon = 1e-05
masked_score = -1e30
f32 = jnp.float32
bf16 = jnp.bfloat16


def gelu_tanh(values):
    inner_arg = 0.7978845608028654 * (values + 0.044715 * values * values * values)
    return 0.5 * values * (1.0 + jnp.tanh(inner_arg))


def rotate_heads(fields, cosine_table, sine_table):
    half = ROT_DIMS // 2
    first_half = fields[..., :half]
    second_half = fields[..., half:ROT_DIMS]
    return jnp.concatenate(
        [
            first_half * cosine_table - second_half * sine_table,
            second_half * cosine_table + first_half * sine_table,
            fields[..., ROT_DIMS:],
        ],
        axis=-1,
    )


def standardize(inputs):
    average = jnp.mean(inputs, axis=-1, keepdims=True)
    centered = inputs - average
    variance = jnp.mean(centered * centered, axis=-1, keepdims=True)
    return centered * lax.rsqrt(variance + epsilon)


def dot(a, b, ca, cb):
    return lax.dot_general(a, b, (((ca,), (cb,)), ((), ())), preferred_element_type=f32)


def local(
    tokens,
    segments,
    ln_gain,
    ln_shift,
    qkv_weight,
    qkv_bias,
    proj_weight,
    proj_bias,
    up_weight,
    up_bias,
    down_weight,
    down_bias,
    cotangent,
):
    rows = tokens.shape[1]
    width = tokens.shape[2]
    shard = ln_gain.shape[0]
    ring = lax.axis_size("ctx")
    shards = lax.axis_size("fsdp")
    c = lax.axis_index("ctx")
    f = lax.axis_index("fsdp")
    heads = width // HEAD
    own_heads = heads // ring
    cols = width // ring
    hidden_width = up_weight.shape[1]
    ratio = hidden_width // width
    strip = hidden_width // (shards * ring)
    seq = rows * ring

    packed = jnp.concatenate([ln_gain, ln_shift, proj_bias, down_bias, qkv_bias, up_bias])
    packed = lax.all_gather(packed, "fsdp", axis=0, tiled=False)
    gain = packed[:, :shard].reshape(width).astype(f32)
    shift = packed[:, shard : 2 * shard].reshape(width).astype(f32)
    proj_b = packed[:, 2 * shard : 3 * shard].reshape(width).astype(f32)
    down_b = packed[:, 3 * shard : 4 * shard].reshape(width).astype(f32)
    qkv_b = packed[:, 4 * shard : 7 * shard].reshape(3, ring, cols).astype(f32)
    up_b = packed[:, 7 * shard :].reshape(shards, ring, strip).astype(f32)
    qkv_b = lax.dynamic_index_in_dim(qkv_b, c, 1, False).reshape(3 * cols)
    up_b = lax.dynamic_index_in_dim(up_b, c, 1, False).reshape(shards * strip)

    own_qkv = lax.dynamic_index_in_dim(qkv_weight.reshape(shard, 3, ring, cols), c, 2, False)
    own_up = lax.dynamic_index_in_dim(up_weight.reshape(shard, shards, ring, strip), c, 2, False)
    own_down = lax.dynamic_index_in_dim(down_weight.reshape(ring, strip, width), c, 0, False)
    own_proj = jnp.where(
        (jnp.arange(cols // shard) + c * (cols // shard) == f)[:, None, None],
        proj_weight[None],
        jnp.zeros((), bf16),
    )
    qkv_w = lax.all_gather(own_qkv.reshape(shard, 3 * cols), "fsdp", axis=0, tiled=True)
    up_w = lax.all_gather(own_up.reshape(shard, shards * strip), "fsdp", axis=0, tiled=True)
    down_w = lax.all_gather(own_down, "fsdp", axis=0, tiled=True)
    proj_w = lax.psum(own_proj, "fsdp").reshape(cols, width)

    both = jnp.concatenate([tokens[0], cotangent[0]], axis=1)
    both = lax.all_gather(both, "ctx", axis=0, tiled=True)
    all_tokens, upstream = both[:, :width], both[:, width:]
    seg = lax.all_gather(segments[0], "ctx", axis=0, tiled=True)

    row_index = jnp.arange(seq, dtype=jnp.int32)
    begins = jnp.sum((seg[None, :] < seg[:, None]).astype(jnp.int32), axis=1)
    positions = row_index - begins
    inverse = jnp.exp(
        jnp.arange(ROT_DIMS // 2, dtype=f32) * (-math.log(10000.0) / (ROT_DIMS // 2))
    )
    angles = positions.astype(f32)[:, None, None] * inverse
    cosine_table = jnp.cos(angles)
    sine_table = jnp.sin(angles)

    normed = (standardize(all_tokens.astype(f32)) * gain + shift).astype(bf16)
    projected = dot(normed, qkv_w, 1, 0) + qkv_b
    hidden = dot(normed, up_w, 1, 0) + up_b
    grouped = projected.reshape(seq, 3, own_heads, HEAD)
    turner = partial(rotate_heads, cosine_table=cosine_table, sine_table=sine_table)
    queries_wide, query_pull = jax.vjp(turner, grouped[:, 0])
    key_wide, key_pull = jax.vjp(turner, grouped[:, 1])
    queries = queries_wide.astype(bf16)
    keys = key_wide.astype(bf16)
    values = grouped[:, 2].astype(bf16)
    scale = 1.0 / math.sqrt(HEAD)

    allowed = (row_index[None, :] <= row_index[:, None]) & (seg[None, :] == seg[:, None])
    scores = jnp.einsum("qhd,khd->hqk", queries, keys, preferred_element_type=f32) * scale
    scores = jnp.where(allowed[None], scores, masked_score)
    logsum = jax.nn.logsumexp(scores, axis=-1)
    probs = jnp.exp(scores - logsum[..., None])
    probs_low = probs.astype(bf16)
    context = jnp.einsum("hqk,khd->qhd", probs_low, values, preferred_element_type=f32)
    context = context.astype(bf16).reshape(seq, cols)
    active_wide, active_pull = jax.vjp(gelu_tanh, hidden)
    active = active_wide.astype(bf16)
    out_part = dot(context, proj_w, 1, 0) + dot(active, down_w, 1, 0)
    out_sum = lax.psum_scatter(out_part.astype(bf16), "ctx", scatter_dimension=0, tiled=True)
    inputs = tokens[0].astype(f32)
    block_out = (inputs + out_sum.astype(f32) + proj_b + down_b).astype(bf16)

    d_active = dot(upstream, down_w, 1, 1)
    d_context = dot(upstream, proj_w, 1, 1).astype(bf16).reshape(seq, own_heads, HEAD)
    d_hidden = active_pull(d_active)[0].astype(bf16)
    d_probs = jnp.einsum("qhd,khd->hqk", d_context, values, preferred_element_type=f32)
    delta = jnp.sum(probs * d_probs, axis=-1, keepdims=True)
    d_scores = (probs * (d_probs - delta)).astype(bf16)
    d_queries = jnp.einsum("hqk,khd->qhd", d_scores, keys, preferred_element_type=f32) * scale
    d_keys = jnp.einsum("hqk,qhd->khd", d_scores, queries, preferred_element_type=f32) * scale
    d_values = jnp.einsum("hqk,qhd->khd", probs_low, d_context, preferred_element_type=f32)
    d_projected = jnp.stack([query_pull(d_queries)[0], key_pull(d_keys)[0], d_values], axis=1)
    d_projected = d_projected.reshape(seq, 3 * cols).astype(bf16)

    d_normed = dot(d_projected, qkv_w, 1, 1) + dot(d_hidden, up_w, 1, 1)
    d_normed = lax.psum_scatter(d_normed.astype(bf16), "ctx", scatter_dimension=0, tiled=True)
    d_normed = d_normed.astype(f32)
    standard, standard_pull = jax.vjp(standardize, inputs)
    upstream_own = cotangent[0].astype(f32)
    token_grad = (upstream_own + standard_pull(d_normed * gain)[0]).astype(bf16)

    grad_down = dot(active, upstream, 0, 0).astype(bf16)
    grad_up = dot(normed, d_hidden, 0, 0).astype(bf16)
    grad_qkv = dot(normed, d_projected, 0, 0).astype(bf16)
    grad_proj = dot(context, upstream, 0, 0).astype(bf16)
    wide = jnp.concatenate([grad_qkv, grad_up], axis=1)
    wide = lax.psum_scatter(wide, "fsdp", scatter_dimension=0, tiled=True)
    grad_down = lax.psum_scatter(grad_down, "fsdp", scatter_dimension=0, tiled=True)
    grad_proj = lax.psum(grad_proj, "fsdp").reshape(cols // shard, shard, width)
    grad_proj = lax.dynamic_index_in_dim(grad_proj, f % (cols // shard), 0, False)
    grad_proj = jnp.where(c == f // (cols // shard), grad_proj, jnp.zeros((), bf16))
    proj_weight_grad = lax.psum(grad_proj, "ctx").astype(f32)
    wide = lax.all_gather(wide, "ctx", axis=0, tiled=False)
    down_weight_grad = lax.all_gather(grad_down, "ctx", axis=0, tiled=True).astype(f32)
    qkv_weight_grad = (
        jnp.transpose(wide[:, :, : 3 * cols].reshape(ring, shard, 3, cols), (1, 2, 0, 3))
        .reshape(shard, 3 * width)
        .astype(f32)
    )
    up_weight_grad = (
        jnp.transpose(wide[:, :, 3 * cols :].reshape(ring, shard, shards, strip), (1, 2, 0, 3))
        .reshape(shard, hidden_width)
        .astype(f32)
    )

    d_qkv_b = jnp.sum(d_projected.astype(f32), axis=0).reshape(3, 1, cols)
    d_up_b = jnp.sum(d_hidden.astype(f32), axis=0).reshape(shards, 1, strip)
    here = (jnp.arange(ring) == c)[None, :, None]
    d_out_b = jnp.sum(upstream_own, axis=0)
    vectors = jnp.concatenate(
        [
            jnp.sum(d_normed * standard, axis=0).reshape(shards, -1),
            jnp.sum(d_normed, axis=0).reshape(shards, -1),
            d_out_b.reshape(shards, -1),
            jnp.where(here, d_qkv_b, 0.0).reshape(shards, -1),
            jnp.where(here, d_up_b, 0.0).reshape(shards, -1),
        ],
        axis=1,
    )
    vectors = lax.psum(vectors, ("ctx", "fsdp"))
    vectors = lax.dynamic_index_in_dim(vectors, f, 0, False)
    return (
        block_out[None],
        token_grad[None],
        lax.all_to_all(
            logsum.reshape(1, own_heads, seq), "ctx", split_axis=2, concat_axis=1, tiled=True
        ),
        vectors[:shard],
        vectors[shard : 2 * shard],
        qkv_weight_grad,
        vectors[3 * shard : 6 * shard],
        proj_weight_grad,
        vectors[2 * shard : 3 * shard],
        up_weight_grad,
        vectors[6 * shard :],
        down_weight_grad,
        vectors[2 * shard : 3 * shard],
    )


def solution(mesh):
    in_specs = (
        P("fsdp", "ctx", None),
        P("fsdp", "ctx"),
        P("fsdp"),
        P("fsdp"),
        P("fsdp", None),
        P("fsdp"),
        P("fsdp", None),
        P("fsdp"),
        P("fsdp", None),
        P("fsdp"),
        P("fsdp", None),
        P("fsdp"),
        P("fsdp", "ctx", None),
    )
    out_specs = (
        P("fsdp", "ctx", None),
        P("fsdp", "ctx", None),
        P("fsdp", None, "ctx"),
        P("fsdp"),
        P("fsdp"),
        P("fsdp", None),
        P("fsdp"),
        P("fsdp", None),
        P("fsdp"),
        P("fsdp", None),
        P("fsdp"),
        P("fsdp", None),
        P("fsdp"),
    )
    return jax.shard_map(local, mesh=mesh, in_specs=in_specs, out_specs=out_specs, check_vma=False)
```

time: 1630 us -> 931 us (0.57)
  waiting for transfers between devices: 828 us -> 625 us
  matrix products: 237 us -> 114 us
  local copies, waits for them, and re-layouts: 186 us -> 64.6 us
  blocking collectives: 133 us -> 37 us
  starting transfers between devices: 103 us -> 7.28 us
  other arithmetic: 110 us -> 62.2 us
    reduce_scatter x1 -> x4, waiting for transfers between devices: 457 us -> 182 us  [the longest x1 86 us: local(): wide = lax.psum_scatter(wide, 'fsdp', scatter_dimension=0, tiled=True)]
    psum x1 -> x3, waiting for transfers between devices: 70.1 us -> 268 us  [the longest x1 143 us: local(): vectors = lax.psum(vectors, ('ctx', 'fsdp'))]
    dot_general x68 -> x18, matrix products: 237 us -> 114 us  [the longest x12 82.2 us: dot(): lax.dot_general(a, b, (((ca,), (cb,)), ((), ())), preferred_element_type=...]
    reshape x12 -> x0, local copies, waits for them, and re-layouts: 113 us -> none  [the longest x1 55.1 us: term_rows(): grad_down.reshape(amount, ratio * width)]
    ppermute x44 -> x0, waiting for transfers between devices: 111 us -> none  [the longest x28 109 us: passed_along(): return lax.ppermute(block, axis, route)]
    ppermute x44 -> x0, starting transfers between devices: 103 us -> none  [the longest x28 82.5 us: passed_along(): return lax.ppermute(block, axis, route)]
    all_gather x6 -> x2, blocking collectives: 109 us -> 37 us  [the longest x1 21.4 us: local(): packed = lax.all_gather(packed, 'fsdp', axis=0, tiled=False)]
    concatenate x2 -> x3, other arithmetic: 66.8 us -> 8.41 us  [the longest x1 6 us: local(): wide = jnp.concatenate([grad_qkv, grad_up], axis=1)]
  transfers between devices with their start and end apart: 51 -> 14, of which waited for: 38 -> 13; matrix products, arithmetic and copies ran while one was open for 19% -> 16% of each run, Pallas kernels for 0% -> 0%
where the time goes in v1:
time: 931 us; the launch traced here: 925 us
  waiting for transfers between devices  625 us (67%)
  matrix products  114 us (12%)
  local copies, waits for them, and re-layouts  64.6 us (7%)
  other arithmetic  62.2 us (7%)
  blocking collectives  37 us (4%)
  between operations  15.2 us (2%)
    psum x1, waiting for transfers between devices, local(): vectors = lax.psum(vectors, ('ctx', 'fsdp'))  143 us
    reduce_scatter x1, waiting for transfers between devices, local(): wide = lax.psum_scatter(wide, 'fsdp', scatter_dimension=0, tiled=True)  86 us
    dot_general x12, matrix products, dot(): lax.dot_general(a, b, (((ca,), (cb,)), ((), ())), preferred_element_type=...  82.2 us
    psum x1, waiting for transfers between devices, local(): proj_w = lax.psum(own_proj, 'fsdp').reshape(cols, width)  79.7 us
    reduce_scatter x1, waiting for transfers between devices, local(): lax.psum_scatter(grad_down, 'fsdp', scatter_dimension=0, tiled=True)  77.8 us
    psum x1, waiting for transfers between devices, local(): proj_weight_grad = lax.psum(grad_proj, 'ctx').astype(f32)  45.2 us
    all_gather x1, waiting for transfers between devices, local(): lax.all_gather(own_qkv.reshape(shard, 3 * cols), 'fsdp', axis=0, tiled=True)  44 us
    all_gather x1, waiting for transfers between devices, local(): down_w = lax.all_gather(own_down, 'fsdp', axis=0, tiled=True)  43.7 us
  transfers between devices with their start and end apart: 14, of which 13 were waited for; matrix products, arithmetic and copies ran while one was open for 16% of the time, Pallas kernels for 0%

profile of v1, /device:TPU:1, one launch (start us, length us, event | category | flops | bytes accessed | tf_op | source)
XLA Modules:
  0.0 925.4 jit_solution(10895820620294388671)
XLA Ops:
  22.2 21.4 %all-gather.4 = bf16[16,1,1408]{2,1,0:T(2,128)(2,1)S(1)} all-gather(bf16[1,1,1408]{2,1,0:T(2,128)(2,1)S(1)} %reshape.367), channel_id=2, replica_groups=mesh['ctx'=8,'fsdp'=16] {'fsdp'}, dimensions={0}, use_global_device_ids=true | all-gather | bytes 47872 | tf_op jit(solution)/shard_map/all_gather | solution.py:80
  44.2 15.6 %all-gather.1 = s32[1,1024]{1,0:T(1,128)S(1)} all-gather(s32[1,128]{1,0:T(1,128)S(1)} %copy-done.40), channel_id=3, replica_groups=mesh['ctx'=8,'fsdp'=16] {'ctx'}, dimensions={1}, use_global_device_ids=true | all-gather | bytes 4608 | tf_op jit(solution)/shard_map/all_gather | solution.py:106
  73.9 44.0 %all-gather.14.cloned.1.call-done = bf16[2048,768]{0,1:T(8,128)(2,1)} async-done(((bf16[128,768]{0,1:T(8,128)(2,1)}), bf16[2048,768]{0,1:T(8,128)(2,1)}) %all-gather.14.cloned.1.call-update) | async-done | bytes 3145744 | tf_op jit(solution)/shard_map/all_gather | solution.py:98
  117.8 6.2 convolution_add_fusion
  143.6 33.8 %all-gather.16.cloned.1.call-done = bf16[2048,1024]{0,1:T(8,128)(2,1)} async-done(((bf16[128,1024]{0,1:T(8,128)(2,1)}), bf16[2048,1024]{0,1:T(8,128)(2,1)}) %all-gather.16.cloned.1.call-update) | async-done | bytes 4194320 | tf_op jit(solution)/shard_map/all_gather | solution.py:99
  177.4 10.0 %fusion.72 = f32[1024,1024]{1,0:T(8,128)} fusion(bf16[1024,2048]{1,0:T(8,128)(2,1)} %fusion.7, bf16[2048,1024]{0,1:T(8,128)(2,1)} %all-gather.16.cloned.1.call-done), kind=kOutput, calls=%fused_computation.155 | convolution fusion | flops 4294967296 | bytes 12582912 | tf_op jit(solution)/shard_map/dot_general | solution.py:46
  187.4 43.7 %all-gather.20.cloned.1.call-done = bf16[1,1024,2048]{2,1,0:T(8,128)(2,1)} async-done(((bf16[1,64,2048]{2,1,0:T(8,128)(2,1)}), bf16[1,1024,2048]{2,1,0:T(8,128)(2,1)}) %all-gather.20.cloned.1.call-update) | async-done | bytes 4194320 | tf_op jit(solution)/shard_map/all_gather | solution.py:100
  231.1 12.8 %convert_reduce_fusion.1 = (f32[1024]{0:T(1024)S(1)}, bf16[1024,1024]{1,0:T(8,128)(2,1)}) fusion(f32[1024,1024]{1,0:T(8,128)} %fusion.72, f32[1024]{0:T(1024)S(1)} %copy-done.33, bf16[1,1024,2048]{2,1,0:T(8,128)(2,1)} %all-gather.20.cloned.1.call-done, bf16[1024,4096]{1,0:T(8,128)(2,1)} %all-gather.12.cloned.1.call-done), kind=kOutput, calls=%fused_computation.32 | convolution fusion | flops 4323277824 | bytes 14688256 | tf_op jit(solution)/shard_map/dot_general | solution.py:46
  243.9 79.7 %all-reduce.15.cloned.1.call-done = (bf16[256,2048]{1,0:T(8,128)(2,1)}, bf16[2,128,2048]{2,1,0:T(8,128)(2,1)}) async-done(((bf16[256,2048]{1,0:T(8,128)(2,1)}, bf16[2,128,2048]{2,1,0:T(8,128)(2,1)}), (bf16[256,2048]{1,0:T(8,128)(2,1)}, bf16[2,128,2048]{2,1,0:T(8,128)(2,1)})) %all-reduce.15.cloned.1.call-update) | async-done | bytes 2097168 | tf_op jit(solution)/shard_map/psum | solution.py:101
  327.4 12.0 %multiply_reduce_fusion = (f32[4,1024]{1,0:T(4,128)S(1)}, f32[4,1024,1024]{1,2,0:T(8,128)}) fusion(f32[4,1024,1024]{1,2,0:T(8,128)} %copy-done.2, f32[4,1024]{1,0:T(4,128)S(1)} %fusion.58, pred[1024,1024]{0,1:T(8,128)(4,1)S(1)} %fusion.20, bf16[1024,4,64]{0,2,1:T(8,128)(2,1)S(1)} %bitcast.160, f32[1024,3,4,64]{0,3,2,1:T(8,128)} %bitcast.149), kind=kOutput, calls=%fused_computation.1 | convolution fusion | flops 557838336 | bytes 35684352 | tf_op jit(solution)/shard_map/qhd,khd->hqk/dot_general | solution.py:148
  339.4 12.2 %multiply_convert_fusion = bf16[4,1024,1024]{1,2,0:T(8,128)(2,1)S(1)} fusion(f32[4,1024,1024]{1,2,0:T(8,128)} %get-tuple-element.144, f32[4,1024,1024]{1,2,0:T(8,128)} %copy-done.2, f32[4,1024]{1,0:T(4,128)S(1)} %get-tuple-element.143, f32[4,1024]{1,0:T(4,128)S(1)} %fusion.58, pred[1024,1024]{0,1:T(8,128)(4,1)S(1)} %fusion.20), kind=kLoop, calls=%fused_computation | loop fusion | flops 25165824 | bytes 43024384 | tf_op jit(solution)/shard_map/convert_element_type | solution.py:150
  356.2 8.4 convolution_bitcast_fusion
  376.8 8.5 fusion.17
  389.0 10.8 %convolution_convert_fusion = bf16[1024,2048]{1,0:T(8,128)(2,1)} fusion(bf16[1024,4096]{1,0:T(8,128)(2,1)} %all-gather.12.cloned.1.call-done, f32[1024,1024]{1,0:T(8,128)} %fusion.72, f32[1024]{0:T(1024)S(1)} %copy-done.33), kind=kOutput, calls=%fused_computation.38 | convolution fusion | flops 4307550208 | bytes 12587008 | tf_op jit(solution)/shard_map/dot_general | solution.py:46
  399.9 7.7 convolution_convert_fusion.1
  418.4 10.1 %copy.131 = bf16[2048,1792]{1,0:T(8,128)(2,1)} copy(bf16[2048,1792]{0,1:T(8,128)(2,1)} %pad_maximum_fusion) | data formatting | bytes 14680064
  434.1 18.1 %reduce-scatter.7.cloned.1.call-done = bf16[128,2048]{1,0:T(8,128)(2,1)} async-done(((bf16[1024,2048]{1,0:T(8,128)(2,1)}), bf16[128,2048]{1,0:T(8,128)(2,1)}) %reduce-scatter.7.cloned.1.call-update) | async-done | bytes 524304 | tf_op jit(solution)/shard_map/reduce_scatter | solution.py:141
  455.9 77.8 %reduce-scatter.11.cloned.1.call-done = bf16[64,2048]{1,0:T(8,128)(2,1)} async-done(((bf16[1024,2048]{1,0:T(8,128)(2,1)}), bf16[64,2048]{1,0:T(8,128)(2,1)}) %reduce-scatter.11.cloned.1.call-update) | async-done | bytes 262160 | tf_op jit(solution)/shard_map/reduce_scatter | solution.py:170
  533.8 86.0 %reduce-scatter.13.cloned.1.call-done = bf16[128,1792]{1,0:T(8,128)(2,1)} async-done(((bf16[2048,1792]{1,0:T(8,128)(2,1)}), bf16[128,1792]{1,0:T(8,128)(2,1)}) %reduce-scatter.13.cloned.1.call-update) | async-done | bytes 458768 | tf_op jit(solution)/shard_map/reduce_scatter | solution.py:169
  623.6 6.3 all-to-all-start
  636.9 45.2 %all-reduce.13.cloned.1.call-done = bf16[128,2048]{1,0:T(8,128)(2,1)} async-done(((bf16[128,2048]{1,0:T(8,128)(2,1)}), bf16[128,2048]{1,0:T(8,128)(2,1)}) %all-reduce.13.cloned.1.call-update) | async-done | bytes 524304 | tf_op jit(solution)/shard_map/psum | solution.py:174
  684.2 142.7 %all-reduce.11.cloned.1.call-done = f32[16,1280]{1,0:T(8,128)} async-done(((f32[16,1280]{1,0:T(8,128)}), f32[16,1280]{1,0:T(8,128)}) %all-reduce.11.cloned.1.call-update) | async-done | bytes 81936 | tf_op jit(solution)/shard_map/psum | solution.py:202
  830.9 20.4 %all-gather.18.cloned.1.call-done = bf16[512,2048]{1,0:T(8,128)(2,1)} async-done(((bf16[64,2048]{1,0:T(8,128)(2,1)}), bf16[512,2048]{1,0:T(8,128)(2,1)}) %all-gather.18.cloned.1.call-update) | async-done | bytes 2097168 | tf_op jit(solution)/shard_map/all_gather | solution.py:176
  855.5 28.2 %all-gather.22.cloned.1.call-done = bf16[1024,1792]{1,0:T(8,128)(2,1)} async-done(((bf16[128,1792]{1,0:T(8,128)(2,1)}), bf16[1024,1792]{1,0:T(8,128)(2,1)}) %all-gather.22.cloned.1.call-update) | async-done | bytes 3670032 | tf_op jit(solution)/shard_map/all_gather | solution.py:175
  (223 shorter events, 148.6 us)
Async XLA Ops:
  7.2 12.8 %copy-start = (bf16[512,2048]{1,0:T(8,128)(2,1)S(1)}, bf16[512,2048]{1,0:T(8,128)(2,1)}, u32[]{:S(2)}) copy-start(bf16[512,2048]{1,0:T(8,128)(2,1)} %param.23) | copy-start | bytes 6291460
  7.2 56.8 %all-gather.12.cloned.1.call-start = ((), (), s32[]{:S(2)}) async-start(), calls=%async_computation.5 | async-start | bytes 9437184 | tf_op jit(solution)/shard_map/all_gather | solution.py:104
  9.7 108.2 %all-gather.14.cloned.1.call-start = ((), (), s32[]{:S(2)}) async-start(), calls=%async_computation.6 | async-start | bytes 3342336 | tf_op jit(solution)/shard_map/all_gather | solution.py:98
  9.8 34.4 %copy-start.40 = (s32[1,128]{1,0:T(1,128)S(1)}, s32[1,128]{1,0:T(1,128)}, u32[]{:S(2)}) copy-start(s32[1,128]{1,0:T(1,128)} %param.14) | copy-start | bytes 1540
  12.4 50.3 %copy-start.26 = (bf16[128,2048]{1,0:T(8,128)(2,1)S(1)}, bf16[128,2048]{1,0:T(8,128)(2,1)}, u32[]{:S(2)}) copy-start(bf16[128,2048]{1,0:T(8,128)(2,1)} %param.19) | copy-start | bytes 1572868
  14.1 163.3 %all-gather.16.cloned.1.call-start = ((), (), s32[]{:S(2)}) async-start(), calls=%async_computation.7 | async-start | bytes 4456448 | tf_op jit(solution)/shard_map/all_gather | solution.py:99
  19.9 211.2 %all-gather.20.cloned.1.call-start = ((), (), s32[]{:S(2)}) async-start(), calls=%async_computation.14 | async-start | bytes 4456448 | tf_op jit(solution)/shard_map/all_gather | solution.py:100
  20.7 302.9 %all-reduce.15.cloned.1.call-start = ((), (), s32[]{:S(2)}) async-start(), calls=%async_computation.17 | async-start | bytes 4194304 | tf_op jit(solution)/shard_map/psum | solution.py:101
  44.2 26.5 %copy-start.28 = (f32[2048]{0:T(1024)}, f32[2048]{0:T(1024)S(1)}, u32[]{:S(2)}) copy-start(f32[2048]{0:T(1024)S(1)} %get-tuple-element.136) | copy-start | bytes 24580
  143.5 87.6 %copy-start.33 = (f32[1024]{0:T(1024)S(1)}, f32[1024]{0:T(1024)}, u32[]{:S(2)}) copy-start(f32[1024]{0:T(1024)} %add.185) | copy-start | bytes 12292
  143.5 287.5 %reduce-scatter.9.cloned.1.call-start = ((), (), s32[]{:S(2)}) async-start(), calls=%async_computation.9 | async-start | bytes 4718592 | tf_op jit(solution)/shard_map/reduce_scatter | solution.py:158
  339.4 12.3 %copy-start.25 = (bf16[1024,4,16]{0,2,1:T(8,128)(2,1)S(1)}, bf16[1024,4,16]{0,2,1:T(8,128)(2,1)}, u32[]{:S(2)}) copy-start(bf16[1024,4,16]{0,2,1:T(8,128)(2,1)} %copy-done.24) | copy-start | bytes 393220
  376.8 75.4 %reduce-scatter.7.cloned.1.call-start = ((), (), s32[]{:S(2)}) async-start(), calls=%async_computation.8 | async-start | bytes 4718592 | tf_op jit(solution)/shard_map/reduce_scatter | solution.py:141
  388.8 144.9 %reduce-scatter.11.cloned.1.call-start = ((), (), s32[]{:S(2)}) async-start(), calls=%async_computation.12 | async-start | bytes 4456448 | tf_op jit(solution)/shard_map/reduce_scatter | solution.py:170
  399.8 219.9 %reduce-scatter.13.cloned.1.call-start = ((), (), s32[]{:S(2)}) async-start(), calls=%async_computation.16 | async-start | bytes 7798784 | tf_op jit(solution)/shard_map/reduce_scatter | solution.py:169
  428.5 23.7 %copy-start.8 = (bf16[1,128,2048]{2,1,0:T(8,128)(2,1)S(1)}, bf16[1,128,2048]{2,1,0:T(8,128)(2,1)}, u32[]{:S(2)}) copy-start(bf16[1,128,2048]{2,1,0:T(8,128)(2,1)} %param.25) | copy-start | bytes 1572868
  428.5 23.7 %copy-start.31 = (f32[2048]{0:T(1024)S(1)}, f32[2048]{0:T(1024)}, u32[]{:S(2)}) copy-start(f32[2048]{0:T(1024)} %get-tuple-element.133) | copy-start | bytes 24580
  428.5 23.7 %copy-start.32 = (f32[2048]{0:T(1024)S(1)}, f32[2048]{0:T(1024)}, u32[]{:S(2)}) copy-start(f32[2048]{0:T(1024)} %get-tuple-element.134) | copy-start | bytes 24580
  428.6 253.6 %all-reduce.13.cloned.1.call-start = ((), (), s32[]{:S(2)}) async-start(), calls=%async_computation.11 | async-start | bytes 1048576 | tf_op jit(solution)/shard_map/psum | solution.py:174
  430.9 396.0 %all-reduce.11.cloned.1.call-start = ((), (), s32[]{:S(2)}) async-start(), calls=%async_computation.10 | async-start | bytes 163840 | tf_op jit(solution)/shard_map/psum | solution.py:202
  455.9 395.5 %all-gather.18.cloned.1.call-start = ((), (), s32[]{:S(2)}) async-start(), calls=%async_computation.13 | async-start | bytes 2359296 | tf_op jit(solution)/shard_map/all_gather | solution.py:176
  533.7 350.0 %all-gather.22.cloned.1.call-start = ((), (), s32[]{:S(2)}) async-start(), calls=%async_computation.15 | async-start | bytes 4128768 | tf_op jit(solution)/shard_map/all_gather | solution.py:175
  623.6 10.9 %all-to-all-start = ((f32[8,1,512]{2,1,0:T(1,128)}), f32[8,1,512]{2,1,0:T(1,128)S(1)}, u32[]{:S(2)}, u32[]{:S(2)}) async-start(f32[8,1,512]{2,1,0:T(1,128)} %reshape.381), calls=%async_computation.2 | async-start | bytes 32768 | tf_op jit(solution)/shard_map/all_to_all | solution.py:207
  828.2 89.7 %copy-start.41 = (f32[128]{0:T(128)}, f32[128]{0:T(128)S(1)}, u32[]{:S(2)}) copy-start(f32[128]{0:T(128)S(1)} %get-tuple-element.174) | copy-start | bytes 1540
  (36 other events, 201.7 us)
Sparse Core Ops, SparseCore 0:
  10.3 53.5 all-gather.11
  66.6 51.1 all-gather.13
  120.5 56.8 all-gather.15
  179.4 51.6 all-gather.19
  234.9 88.7 all-reduce.14
  376.9 35.8 reduce-scatter.8
  415.3 36.8 reduce-scatter.6
  455.9 77.7 reduce-scatter.10
  537.2 82.5 reduce-scatter.12
  622.6 59.4 all-reduce.12
  687.5 139.4 all-reduce.10
  828.6 22.7 all-gather.17
  853.1 30.5 all-gather.21

commit v2 on v1

v2 whole, which is shorter than its diff:
```python
from functools import partial
import math

import jax
import jax.numpy as jnp
from jax import lax
from jax.experimental import pallas as pl
from jax.experimental.pallas import tpu as pltpu
from jax.sharding import PartitionSpec as P

HEAD = 64
ROT_DIMS = 32
SEQ = 1024
WIDTH = 2048
HIDDEN = 8192
OWN_HEADS = 4
COLS = 256
UNITS = 1024

epsilon = 1e-05
masked_score = -1e30
f32 = jnp.float32
bf16 = jnp.bfloat16
MESH = pl.DeviceIdType.MESH
VM = pltpu.VMEM


def dot(a, b, ca, cb):
    return lax.dot_general(a, b, (((ca,), (cb,)), ((), ())), preferred_element_type=f32)


def place():
    c = lax.axis_index("ctx")
    f = lax.axis_index("fsdp")
    return c, f, c // 2, c % 2, f // 4, f % 4


def other_core():
    c, f, z, core, y, x = place()
    return (z * 2 + 1 - core, f)


def up1(i):
    return (i + 1) % 4


def down1(i):
    return (i + 3) % 4


def over(i):
    return (i + 2) % 4


class Copies:
    def __init__(self, send, recv):
        self.send, self.recv = send, recv
        self.started = []

    def start(self, k, src, dst, device):
        copy = pltpu.make_async_remote_copy(
            src_ref=src,
            dst_ref=dst,
            send_sem=self.send.at[k],
            recv_sem=self.recv.at[k],
            device_id=device,
            device_id_type=MESH,
        )
        copy.start()
        self.started.append(copy)

    def arrived(self, k, dst):
        pltpu.make_async_remote_copy(
            src_ref=dst,
            dst_ref=dst,
            send_sem=self.send.at[k],
            recv_sem=self.recv.at[k],
            device_id=other_core(),
            device_id_type=MESH,
        ).wait_recv()

    def sent(self):
        for copy in self.started:
            copy.wait_send()


def plane_gather(w, cuts, copies):
    c, f, z, core, y, x = place()
    r0, r1, r2, r3, r4 = cuts
    first, last = pl.ds(r0, r2 - r0), pl.ds(r2, r4 - r2)
    q0, q1, q2, q3 = (pl.ds(a, b - a) for a, b in zip(cuts[:-1], cuts[1:]))
    xu, xd, xo = up1(x), down1(x), over(x)
    yu, yd, yo = up1(y), down1(y), over(y)
    to_xu, to_xd = (c, y * 4 + xu), (c, y * 4 + xd)
    to_yu, to_yd = (c, yu * 4 + x), (c, yd * 4 + x)
    lo, hi = pl.ds(0, 2), pl.ds(2, 2)
    every = pl.ds(0, 4)

    def send(k, part, device):
        copies.start(k, w.at[part], w.at[part], device)

    def got(k, part):
        copies.arrived(k, w.at[part])

    send(0, (y, x, first), to_xu)
    send(1, (y, x, first), to_xd)
    send(2, (y, x, last), to_yu)
    send(3, (y, x, last), to_yd)
    yield
    got(0, (y, xd, first))
    send(4, (y, xd, q0), to_xu)
    got(1, (y, xu, first))
    send(5, (y, xu, q1), to_xd)
    got(2, (yd, x, last))
    send(6, (yd, x, q2), to_yu)
    got(3, (yu, x, last))
    send(7, (yu, x, q3), to_yd)
    yield
    got(4, (y, xo, q0))
    got(5, (y, xo, q1))
    send(8, (y, every, first), to_yu)
    send(9, (y, every, first), to_yd)
    got(6, (yo, x, q2))
    got(7, (yo, x, q3))
    send(10, (every, x, last), to_xu)
    send(11, (every, x, last), to_xd)
    yield
    got(8, (yd, every, first))
    send(12, (yd, lo, first), to_yu)
    got(9, (yu, every, first))
    send(13, (yu, hi, first), to_yd)
    got(10, (every, xd, last))
    send(14, (lo, xd, last), to_xu)
    got(11, (every, xu, last))
    send(15, (hi, xu, last), to_xd)
    yield
    got(12, (yo, lo, first))
    got(13, (yo, hi, first))
    got(14, (lo, xo, last))
    got(15, (hi, xo, last))
    yield


def line_gather(t, cuts, copies):
    c, f, z, core, y, x = place()
    r0, r1, r2 = cuts
    h0, h1 = pl.ds(r0, r1 - r0), pl.ds(r1, r2 - r1)
    zu, zd, zo = up1(z), down1(z), over(z)
    to_zu, to_zd, to_core = (zu * 2 + core, f), (zd * 2 + core, f), (z * 2 + 1 - core, f)
    other = 1 - core

    def send(k, part, device):
        copies.start(k, t.at[part], t.at[part], device)

    def got(k, part):
        copies.arrived(k, t.at[part])

    send(0, (z, core), to_zu)
    send(1, (z, core), to_zd)
    send(2, (z, core), to_core)
    yield
    got(0, (zd, core))
    send(3, (zd, core, h0), to_zu)
    got(1, (zu, core))
    send(4, (zu, core, h1), to_zd)
    send(5, (zd, core), to_core)
    send(6, (zu, core), to_core)
    yield
    got(3, (zo, core, h0))
    got(4, (zo, core, h1))
    send(7, (zo, core), to_core)
    yield
    got(2, (z, other))
    got(5, (zd, other))
    got(6, (zu, other))
    got(7, (zo, other))
    yield


def enter(owner_of_rows, rows_of_owner):
    c, f, z, core, y, x = place()
    barrier = pltpu.get_barrier_semaphore()
    for device in (
        (c, y * 4 + up1(x)),
        (c, y * 4 + down1(x)),
        (c, up1(y) * 4 + x),
        (c, down1(y) * 4 + x),
        (up1(z) * 2 + core, f),
        (down1(z) * 2 + core, f),
        (z * 2 + 1 - core, f),
    ):
        pl.semaphore_signal(barrier, inc=1, device_id=device, device_id_type=MESH)
    owner = c * 2 + f // 8
    if owner_of_rows:

        @pl.when(owner != f)
        def _():
            pl.semaphore_signal(barrier, inc=1, device_id=(c, owner), device_id_type=MESH)

    if rows_of_owner:
        for j in range(8):
            target = (f % 2) * 8 + j

            @pl.when((f // 2 == c) & (target != f))
            def _():
                pl.semaphore_signal(barrier, inc=1, device_id=(c, target), device_id_type=MESH)

    count = 7
    if owner_of_rows:
        count = count + jnp.where(f // 2 == c, jnp.where(f // 8 == f % 2, 7, 8), 0)
    if rows_of_owner:
        count = count + jnp.where(owner != f, 1, 0)
    pl.semaphore_wait(barrier, count)


CUTS1 = (0, 32, 64, 96, 144)
CUTS2 = (0, 16, 32, 48, 80)
CUTS3 = (0, 32, 64, 96, 128)


def turn(fields, cos, low_sin, high_sin):
    return (
        fields * cos + pltpu.roll(fields, 112, 1) * low_sin + pltpu.roll(fields, 16, 1) * high_sin
    )


def turn_back(grads, cos, low_sin, high_sin):
    return (
        grads * cos + pltpu.roll(grads * low_sin, 16, 1) + pltpu.roll(grads * high_sin, 112, 1)
    )


def halves_packed(a, b, odd, lane):
    moved_a, moved_b = pltpu.roll(a, 64, 1), pltpu.roll(b, 64, 1)
    return jnp.where(lane < 64, jnp.where(odd, moved_a, a), jnp.where(odd, b, moved_b))


def first_kernel(
    tokens,
    cotangent,
    qkv_weight,
    proj_weight,
    up_weight,
    down_weight,
    seg,
    vec,
    cos0,
    sin0,
    inv,
    n_out,
    w1_out,
    w2_out,
    w3_out,
    u_out,
    dproj_out,
    ctx_out,
    act_out,
    dhid_out,
    lse_out,
    w1,
    w2,
    w3,
    t,
    u,
    n,
    strips,
    vecs,
    tab,
    begin_col,
    q,
    k,
    v,
    dctx,
    dq,
    dk,
    dv,
    dproj,
    ctx_heads,
    ctx,
    act,
    dhid,
    lse,
    sem1,
    sem2,
    sem3,
    sem_t,
    sem_u,
    sem_p,
    sem_l,
    sem_o,
):
    c, f, z, core, y, x = place()
    lane = lax.broadcasted_iota(jnp.int32, (1, 128), 1)

    loads = [
        pltpu.make_async_copy(tokens, t.at[z, core, pl.ds(0, 128)], sem_l.at[0]),
        pltpu.make_async_copy(cotangent, u.at[z, core], sem_l.at[1]),
        pltpu.make_async_copy(
            down_weight.at[pl.ds(pl.multiple_of(c * 64, 64), 64)],
            w2.at[y, x, pl.ds(0, 64)],
            sem_l.at[2],
        ),
    ]
    for i in range(3):
        loads.append(
            pltpu.make_async_copy(
                qkv_weight.at[:, pl.ds(pl.multiple_of(i * WIDTH + c * COLS, 128), COLS)],
                w1.at[y, x, pl.ds(0, 128), pl.ds(i * COLS, COLS)],
                sem_l.at[3 + i],
            )
        )
    for copy in loads:
        copy.start()
    for i in range(16):
        pltpu.make_async_copy(
            up_weight.at[:, pl.ds(pl.multiple_of(i * 512 + (c // 2) * 128, 128), 128)],
            strips.at[i],
            sem_l.at[6],
        ).start()
    w1[y, x, 128:144, 0:128] = vec[...]
    w1[y, x, 128:144, 128:768] = jnp.zeros((16, 640), bf16)
    seg_rows = jnp.broadcast_to(seg[...].astype(f32), (16, 128)).astype(bf16)
    t[z, core, 128:144, 0:128] = seg_rows
    t[z, core, 128:144, 128:WIDTH] = jnp.zeros((16, WIDTH - 128), bf16)

    enter(True, False)

    copies1 = Copies(sem1.at[0], sem1.at[1])
    copies2 = Copies(sem2.at[0], sem2.at[1])
    copies3 = Copies(sem3.at[0], sem3.at[1])
    copies_t = Copies(sem_t.at[0], sem_t.at[1])
    copies_u = Copies(sem_u.at[0], sem_u.at[1])
    gather1 = plane_gather(w1, CUTS1, copies1)
    gather2 = plane_gather(w2, CUTS2, copies2)
    gather3 = plane_gather(w3, CUTS3, copies3)
    gather_t = line_gather(t, (0, 64, 144), copies_t)
    gather_u = line_gather(u, (0, 64, 128), copies_u)

    for i in (3, 4, 5):
        loads[i].wait()
    next(gather1)
    loads[0].wait()
    next(gather_t)

    owner = c * 2 + f // 8
    own_rows = f // 2 == c
    for j in range(8):
        target = (f % 2) * 8 + j
        rows = proj_weight.at[pl.ds(16 * j, 16)]

        @pl.when(own_rows & (target != f))
        def _():
            pltpu.make_async_remote_copy(
                src_ref=rows,
                dst_ref=w2.at[target // 4, target % 4, pl.ds(64, 16)],
                send_sem=sem_p.at[0, j],
                recv_sem=sem_p.at[1, 0],
                device_id=(c, target),
                device_id_type=MESH,
            ).start()

        @pl.when(own_rows & (target == f))
        def _():
            local = pltpu.make_async_copy(
                rows, w2.at[target // 4, target % 4, pl.ds(64, 16)], sem_p.at[1, 1]
            )
            local.start()
            local.wait()

    pltpu.make_async_copy(strips, strips, sem_l.at[6]).wait()
    odd = core == 1
    for m in range(8):
        packed = halves_packed(
            strips[2 * m].astype(f32), strips[2 * m + 1].astype(f32), odd, lane
        )
        w3[y, x, :, 128 * m : 128 * m + 128] = packed.astype(bf16)

    next(gather1)
    loads[2].wait()

    @pl.when(owner != f)
    def _():
        own = w2.at[y, x, pl.ds(64, 16)]
        pltpu.make_async_remote_copy(
            src_ref=own,
            dst_ref=own,
            send_sem=sem_p.at[0, 0],
            recv_sem=sem_p.at[1, 0],
            device_id=other_core(),
            device_id_type=MESH,
        ).wait_recv()

    next(gather_t)
    loads[1].wait()
    next(gather_u)
    next(gather1)
    next(gather2)
    next(gather_t)
    next(gather1)
    next(gather2)
    next(gather_t)
    next(gather1)

    outs = []

    def put(src, dst):
        copy = pltpu.make_async_copy(src, dst, sem_o.at[len(outs)])
        copy.start()
        outs.append(copy)

    put(w1, w1_out)

    vecs[...] = w1[:, :, 128:144, 0:128].reshape(16, 16, 128).astype(f32)
    gain = jnp.concatenate([vecs[i, 0:1, :] for i in range(16)], axis=1)
    shift = jnp.concatenate([vecs[i, 1:2, :] for i in range(16)], axis=1)

    def bias_rows(which):
        parts = []
        for i in range(2):
            row = which * 16 + c * 2 + i
            parts.append(vecs[row // 3, pl.ds(4 + row % 3, 1), :])
        return jnp.concatenate(parts, axis=1)

    qkv_bias = jnp.concatenate([bias_rows(i) for i in range(3)], axis=1)
    up_parts = []
    for m in range(8):
        a = vecs[2 * m, pl.ds(7 + c // 2, 1), :]
        b = vecs[2 * m + 1, pl.ds(7 + c // 2, 1), :]
        up_parts.append(halves_packed(a, b, odd, lane))
    up_bias = jnp.concatenate(up_parts, axis=1)

    seg_all = jnp.concatenate(
        [t[b // 2, b % 2, 128:144, 0:128][0:1].astype(f32) for b in range(8)], axis=0
    )
    seg_cols = jnp.transpose(seg_all)
    firsts = [
        jnp.sum((seg_all < float(d)).astype(f32), keepdims=True) for d in range(1, 4)
    ]
    angles = [first * inv[...] for first in firsts]
    first_cos = [jnp.cos(angle) for angle in angles]
    first_sin = [jnp.sin(angle) for angle in angles]
    in_head = lane % 64
    for b in range(8):
        rows = pl.ds(b * 128, 128)
        own = seg_cols[:, b : b + 1]
        cb, sb = jnp.ones((128, 128), f32), jnp.zeros((128, 128), f32)
        first_position = jnp.zeros((128, 1), f32)
        for d in range(1, 4):
            here = own == float(d)
            cb = jnp.where(here, first_cos[d - 1], cb)
            sb = jnp.where(here, first_sin[d - 1], sb)
            first_position = jnp.where(here, firsts[d - 1], first_position)
        base_cos, base_sin = cos0[rows, :], sin0[rows, :]
        cos = base_cos * cb + base_sin * sb
        sin = base_sin * cb - base_cos * sb
        tab[0, rows, :] = cos
        tab[1, rows, :] = jnp.where(in_head < 16, -sin, 0.0)
        tab[2, rows, :] = jnp.where((in_head >= 16) & (in_head < 32), sin, 0.0)
        begin_col[rows, :] = first_position

    def norm_rows(i, carry):
        b, part = i // 4, i % 4
        src = pl.ds(pl.multiple_of(part * 32, 32), 32)
        values = t[b // 2, b % 2, src, :].astype(f32)
        average = jnp.mean(values, axis=-1, keepdims=True)
        centered = values - average
        variance = jnp.mean(centered * centered, axis=-1, keepdims=True)
        standard = centered * lax.rsqrt(variance + epsilon)
        n[pl.ds(pl.multiple_of(i * 32, 32), 32), :] = (standard * gain + shift).astype(bf16)
        return carry

    lax.fori_loop(0, 32, norm_rows, 0)
    put(n, n_out)
    next(gather2)
    next(gather3)
    next(gather_u)

    def project(m, carry):
        rows = pl.ds(pl.multiple_of(m * 256, 256), 256)
        left = n[rows, :]
        tables = [tab[i, rows, :] for i in range(3)]
        for which in range(3):
            columns = pl.ds(which * COLS, COLS)
            right = w1[:, :, pl.ds(0, 128), columns].reshape(WIDTH, COLS)
            fields = dot(left, right, 1, 0) + qkv_bias[:, which * COLS : (which + 1) * COLS]
            for pair in range(2):
                both = fields[:, pair * 128 : pair * 128 + 128]
                if which < 2:
                    both = turn(both, *tables)
                if which == 0:
                    both = both * 0.125
                both = both.astype(bf16)
                target = (q, k, v)[which]
                target[2 * pair, rows, :] = both[:, :64]
                target[2 * pair + 1, rows, :] = both[:, 64:]
        return carry

    lax.fori_loop(0, 4, project, 0)
    next(gather2)
    next(gather3)
    next(gather_u)
    next(gather2)
    next(gather_u)
    put(w2, w2_out)
    put(u, u_out)

    def context_grad(m, carry):
        rows = pl.ds(pl.multiple_of(m * 256, 256), 256)
        left = u[m].reshape(256, WIDTH)
        right = w2[:, :, pl.ds(64, 16), :].reshape(COLS, WIDTH)
        grads = dot(left, right, 1, 1).astype(bf16)
        for head in range(4):
            dctx[head, rows, :] = grads[:, head * 64 : head * 64 + 64]
        return carry

    lax.fori_loop(0, 4, context_grad, 0)
    next(gather3)

    for block in (3, 2, 1, 0):
        reach = (block + 1) * 256
        rows = pl.ds(block * 256, 256)
        keys = pl.ds(0, reach)
        begins = begin_col[rows, :]
        key_index = lax.broadcasted_iota(jnp.int32, (1, reach), 1).astype(f32)
        row_index = (
            lax.broadcasted_iota(jnp.int32, (256, 1), 0) + block * 256
        ).astype(f32)

        def attend(head, carry, block=block, rows=rows, keys=keys, begins=begins):
            qh, kh, vh, dh = q[head, rows, :], k[head, keys, :], v[head, keys, :], dctx[head, rows, :]
            scores = dot(qh, kh, 1, 1)
            allowed = (key_index >= begins) & (key_index <= row_index)
            scores = jnp.where(allowed, scores, masked_score)
            highest = jnp.max(scores, axis=1, keepdims=True)
            weights = jnp.exp(scores - highest)
            total = jnp.sum(weights, axis=1, keepdims=True)
            probs = weights * (1.0 / total)
            log_sum = jnp.broadcast_to(highest + jnp.log(total), (256, 128))
            lse[pl.ds(head, 1), rows] = jnp.transpose(log_sum)[0:1, :]
            probs_low = probs.astype(bf16)
            ctx_heads[head, rows, :] = dot(probs_low, vh, 1, 0).astype(bf16)
            d_probs = dot(dh, vh, 1, 1)
            delta = jnp.sum(probs * d_probs, axis=1, keepdims=True)
            d_scores = (probs * (d_probs - delta)).astype(bf16)
            dq[head, rows, :] = dot(d_scores, kh, 1, 0)
            d_keys = dot(d_scores, qh, 0, 0)
            d_values = dot(probs_low, dh, 0, 0)
            if block == 3:
                dk[head, keys, :] = d_keys
                dv[head, keys, :] = d_values
            else:
                dk[head, keys, :] += d_keys
                dv[head, keys, :] += d_values
            return carry

        lax.fori_loop(0, 4, attend, 0)
        if block >= 2:
            next(gather3)
    put(w3, w3_out)

    def join(m, carry):
        rows = pl.ds(pl.multiple_of(m * 256, 256), 256)
        tables = [tab[i, rows, :] for i in range(3)]
        for pair in range(2):
            lanes = pl.ds(pair * 128, 128)
            ctx[rows, lanes] = jnp.concatenate(
                [ctx_heads[2 * pair, rows, :], ctx_heads[2 * pair + 1, rows, :]], axis=1
            )
            for which, source in ((0, dq), (1, dk), (2, dv)):
                both = jnp.concatenate(
                    [source[2 * pair, rows, :], source[2 * pair + 1, rows, :]], axis=1
                )
                if which == 0:
                    both = both * 0.125
                if which < 2:
                    both = turn_back(both, *tables)
                dproj[rows, pl.ds(which * COLS + pair * 128, 128)] = both.astype(bf16)
        return carry

    lax.fori_loop(0, 4, join, 0)
    put(dproj, dproj_out)
    put(ctx, ctx_out)
    put(lse, lse_out)

    for i in range(4):
        columns = pl.ds(i * 256, 256)
        bias = up_bias[:, i * 256 : (i + 1) * 256]

        def feed(m, carry, columns=columns, bias=bias, i=i):
            rows = pl.ds(pl.multiple_of(m * 256, 256), 256)
            right = w3[:, :, :, columns].reshape(WIDTH, 256)
            h = dot(n[rows, :], right, 1, 0) + bias
            d_act = dot(
                u[m].reshape(256, WIDTH), w2[i, :, pl.ds(0, 64), :].reshape(256, WIDTH), 1, 1
            )
            square = h * h
            tanh = jnp.tanh(0.7978845608028654 * (h + 0.044715 * square * h))
            half = 0.5 * (1.0 + tanh)
            slope = half + 0.5 * h * (1.0 - tanh * tanh) * (
                0.7978845608028654 * (1.0 + 3.0 * 0.044715 * square)
            )
            act[rows, columns] = (h * half).astype(bf16)
            dhid[rows, columns] = (d_act * slope).astype(bf16)
            return carry

        lax.fori_loop(0, 4, feed, 0)
    put(act, act_out)
    put(dhid, dhid_out)

    for copies in (copies1, copies2, copies3, copies_t, copies_u):
        copies.sent()
    for j in range(8):
        target = (f % 2) * 8 + j

        @pl.when(own_rows & (target != f))
        def _():
            pltpu.make_async_remote_copy(
                src_ref=proj_weight.at[pl.ds(16 * j, 16)],
                dst_ref=w2.at[target // 4, target % 4, pl.ds(64, 16)],
                send_sem=sem_p.at[0, j],
                recv_sem=sem_p.at[1, 0],
                device_id=(c, target),
                device_id_type=MESH,
            ).wait_send()

    for copy in outs:
        copy.wait()


def first_call(tokens, cotangent, qkv_weight, proj_weight, up_weight, down_weight, seg, vec):
    lanes = jnp.arange(128) % 64
    inverse = jnp.exp((lanes % 16).astype(f32) * (-math.log(10000.0) / (ROT_DIMS // 2)))
    inverse = jnp.where(lanes < ROT_DIMS, inverse, 0.0)[None, :]
    base = jnp.arange(SEQ, dtype=f32)[:, None] * inverse
    shapes = dict(
        n=((SEQ, WIDTH), bf16),
        w1=((4, 4, 144, 768), bf16),
        w2=((4, 4, 80, WIDTH), bf16),
        w3=((4, 4, 128, UNITS), bf16),
        u=((4, 2, 128, WIDTH), bf16),
        dproj=((SEQ, 768), bf16),
        ctx=((SEQ, COLS), bf16),
        act=((SEQ, UNITS), bf16),
        dhid=((SEQ, UNITS), bf16),
        lse=((8, SEQ), f32),
    )
    anyspace = pl.BlockSpec(memory_space=pl.ANY)
    vmem = pl.BlockSpec(memory_space=VM)
    return pl.pallas_call(
        first_kernel,
        out_shape=[jax.ShapeDtypeStruct(*s) for s in shapes.values()],
        in_specs=[anyspace] * 6 + [vmem] * 5,
        out_specs=[anyspace] * len(shapes),
        scratch_shapes=[
            VM(*shapes["w1"]),
            VM(*shapes["w2"]),
            VM(*shapes["w3"]),
            VM((4, 2, 144, WIDTH), bf16),
            VM(*shapes["u"]),
            VM(*shapes["n"]),
            VM((16, 128, 128), bf16),
            VM((16, 16, 128), f32),
            VM((3, SEQ, 128), f32),
            VM((SEQ, 1), f32),
            VM((4, SEQ, 64), bf16),
            VM((4, SEQ, 64), bf16),
            VM((4, SEQ, 64), bf16),
            VM((4, SEQ, 64), bf16),
            VM((4, SEQ, 64), f32),
            VM((4, SEQ, 64), f32),
            VM((4, SEQ, 64), f32),
            VM(*shapes["dproj"]),
            VM((4, SEQ, 64), bf16),
            VM(*shapes["ctx"]),
            VM(*shapes["act"]),
            VM(*shapes["dhid"]),
            VM(*shapes["lse"]),
            pltpu.SemaphoreType.DMA((2, 16)),
            pltpu.SemaphoreType.DMA((2, 16)),
            pltpu.SemaphoreType.DMA((2, 16)),
            pltpu.SemaphoreType.DMA((2, 8)),
            pltpu.SemaphoreType.DMA((2, 8)),
            pltpu.SemaphoreType.DMA((2, 8)),
            pltpu.SemaphoreType.DMA((7,)),
            pltpu.SemaphoreType.DMA((10,)),
        ],
        compiler_params=pltpu.CompilerParams(
            collective_id=1, has_side_effects=True, vmem_limit_bytes=60 * 1024 * 1024
        ),
        cost_estimate=pl.CostEstimate(
            flops=25 * 10**9, bytes_accessed=40 * 10**6, transcendentals=4 * 10**6
        ),
        name="first",
    )(
        tokens, cotangent, qkv_weight, proj_weight, up_weight, down_weight, seg, vec,
        jnp.cos(base), jnp.sin(base), inverse,
    )


def standardize(inputs):
    average = jnp.mean(inputs, axis=-1, keepdims=True)
    centered = inputs - average
    variance = jnp.mean(centered * centered, axis=-1, keepdims=True)
    return centered * lax.rsqrt(variance + epsilon)


def local(
    tokens,
    segments,
    ln_gain,
    ln_shift,
    qkv_weight,
    qkv_bias,
    proj_weight,
    proj_bias,
    up_weight,
    up_bias,
    down_weight,
    down_bias,
    cotangent,
):
    c, f, z, core, y, x = place()
    width, cols, shard, ring, shards, strip = WIDTH, COLS, 128, 8, 16, 64
    hidden_width = HIDDEN
    packed = jnp.concatenate([ln_gain, ln_shift, proj_bias, down_bias, qkv_bias, up_bias])
    vec = jnp.pad(packed.reshape(11, 128), ((0, 5), (0, 0)))
    normed, w1, w2, w3, u, d_projected, context, active, d_hidden, lse = first_call(
        tokens[0], cotangent[0], qkv_weight, proj_weight, up_weight, down_weight, segments, vec
    )
    vecs = w1[:, :, 128:, :128].reshape(16, 16, 128)
    gain = vecs[:, 0].reshape(width).astype(f32)
    proj_b = vecs[:, 2].reshape(width).astype(f32)
    down_b = vecs[:, 3].reshape(width).astype(f32)
    qkv_w = w1[:, :, :128].reshape(width, 3 * cols)
    up_w = w3.reshape(width, 1024)
    down_w = w2[:, :, :64].reshape(1024, width)
    proj_w = w2[:, :, 64:].reshape(cols, width)
    upstream = u.reshape(1024, width)
    logsum = lse[:4]
    seq = 1024
    inputs = tokens[0].astype(f32)
    out_part = dot(context, proj_w, 1, 0) + dot(active, down_w, 1, 0)
    out_sum = lax.psum_scatter(out_part.astype(bf16), "ctx", scatter_dimension=0, tiled=True)
    block_out = (inputs + out_sum.astype(f32) + proj_b + down_b).astype(bf16)
    d_normed = dot(d_projected, qkv_w, 1, 1) + dot(d_hidden, up_w, 1, 1)
    d_normed = lax.psum_scatter(d_normed.astype(bf16), "ctx", scatter_dimension=0, tiled=True)
    d_normed = d_normed.astype(f32)
    standard, standard_pull = jax.vjp(standardize, inputs)
    upstream_own = cotangent[0].astype(f32)
    token_grad = (upstream_own + standard_pull(d_normed * gain)[0]).astype(bf16)

    grad_down = dot(active, upstream, 0, 0).astype(bf16)
    grad_up = dot(normed, d_hidden, 0, 0).astype(bf16)
    grad_qkv = dot(normed, d_projected, 0, 0).astype(bf16)
    grad_proj = dot(context, upstream, 0, 0).astype(bf16)
    wide = jnp.concatenate([grad_qkv, grad_up], axis=1)
    wide = lax.psum_scatter(wide, "fsdp", scatter_dimension=0, tiled=True)
    grad_down = lax.psum_scatter(grad_down, "fsdp", scatter_dimension=0, tiled=True)
    grad_proj = lax.psum(grad_proj, "fsdp").reshape(cols // shard, shard, width)
    grad_proj = lax.dynamic_index_in_dim(grad_proj, f % (cols // shard), 0, False)
    grad_proj = jnp.where(c == f // (cols // shard), grad_proj, jnp.zeros((), bf16))
    proj_weight_grad = lax.psum(grad_proj, "ctx").astype(f32)
    wide = lax.all_gather(wide, "ctx", axis=0, tiled=False)
    down_weight_grad = lax.all_gather(grad_down, "ctx", axis=0, tiled=True).astype(f32)
    qkv_weight_grad = (
        jnp.transpose(wide[:, :, : 3 * cols].reshape(ring, shard, 3, cols), (1, 2, 0, 3))
        .reshape(shard, 3 * width)
        .astype(f32)
    )
    up_weight_grad = (
        jnp.transpose(wide[:, :, 3 * cols :].reshape(ring, shard, shards, strip), (1, 2, 0, 3))
        .reshape(shard, hidden_width)
        .astype(f32)
    )

    d_qkv_b = jnp.sum(d_projected.astype(f32), axis=0).reshape(3, 1, cols)
    d_up_b = jnp.sum(d_hidden.astype(f32), axis=0).reshape(shards, 1, strip)
    here = (jnp.arange(ring) == c)[None, :, None]
    d_out_b = jnp.sum(upstream_own, axis=0)
    vectors = jnp.concatenate(
        [
            jnp.sum(d_normed * standard, axis=0).reshape(shards, -1),
            jnp.sum(d_normed, axis=0).reshape(shards, -1),
            d_out_b.reshape(shards, -1),
            jnp.where(here, d_qkv_b, 0.0).reshape(shards, -1),
            jnp.where(here, d_up_b, 0.0).reshape(shards, -1),
        ],
        axis=1,
    )
    vectors = lax.psum(vectors, ("ctx", "fsdp"))
    vectors = lax.dynamic_index_in_dim(vectors, f, 0, False)
    return (
        block_out[None],
        token_grad[None],
        lax.all_to_all(
            logsum.reshape(1, 4, seq), "ctx", split_axis=2, concat_axis=1, tiled=True
        ),
        vectors[:shard],
        vectors[shard : 2 * shard],
        qkv_weight_grad,
        vectors[3 * shard : 6 * shard],
        proj_weight_grad,
        vectors[2 * shard : 3 * shard],
        up_weight_grad,
        vectors[6 * shard :],
        down_weight_grad,
        vectors[2 * shard : 3 * shard],
    )


def solution(mesh):
    in_specs = (
        P("fsdp", "ctx", None),
        P("fsdp", "ctx"),
        P("fsdp"),
        P("fsdp"),
        P("fsdp", None),
        P("fsdp"),
        P("fsdp", None),
        P("fsdp"),
        P("fsdp", None),
        P("fsdp"),
        P("fsdp", None),
        P("fsdp"),
        P("fsdp", "ctx", None),
    )
    out_specs = (
        P("fsdp", "ctx", None),
        P("fsdp", "ctx", None),
        P("fsdp", None, "ctx"),
        P("fsdp"),
        P("fsdp"),
        P("fsdp", None),
        P("fsdp"),
        P("fsdp", None),
        P("fsdp"),
        P("fsdp", None),
        P("fsdp"),
        P("fsdp", None),
        P("fsdp"),
    )
    return jax.shard_map(local, mesh=mesh, in_specs=in_specs, out_specs=out_specs, check_vma=False)
```

time: 931 us -> 709 us (0.76)
  waiting for transfers between devices: 625 us -> 422 us
  Pallas kernels: 0 us -> 127 us
  matrix products: 114 us -> 44.7 us
  blocking collectives: 37 us -> 0 us
  other arithmetic: 62.2 us -> 33.1 us
  local copies, waits for them, and re-layouts: 64.6 us -> 54.4 us
    pallas_call x0 -> x1, Pallas kernels: none -> 127 us  [first_call(): pl.pallas_call(first_kernel, out_shape=[jax.ShapeDtypeStruct(*s) for s in...]
    all_gather x4 -> x0, waiting for transfers between devices: 122 us -> none  [the longest x1 44 us: local(): lax.all_gather(own_qkv.reshape(shard, 3 * cols), 'fsdp', axis=0, tiled=True)]
    psum x1, waiting for transfers between devices: 79.7 us -> 23 us  [local(): grad_proj = lax.psum(grad_proj, 'fsdp').reshape(cols // shard, shard, width)]
    dot_general x12 -> x8, matrix products: 82.2 us -> 44.7 us  [dot(): lax.dot_general(a, b, (((ca,), (cb,)), ((), ())), preferred_element_type=...]
    all_gather x2 -> x0, blocking collectives: 37 us -> none  [the longest x1 21.4 us: local(): packed = lax.all_gather(packed, 'fsdp', axis=0, tiled=False)]
    dot_general x6 -> x0, matrix products: 32.2 us -> none  [the longest x1 12 us: local(): jnp.einsum('qhd,khd->hqk', d_context, values, preferred_element_type=f32)]
    reduce_scatter x1, waiting for transfers between devices: 18.1 us -> 0.03 us  [local(): lax.psum_scatter(out_part.astype(bf16), 'ctx', scatter_dimension=0, tiled...]
    convert_element_type x6 -> x1, other arithmetic: 16 us -> 0.02 us  [local(): gain = vecs[:, 0].reshape(width).astype(f32)]
  transfers between devices with their start and end apart: 14 -> 10, of which waited for: 13 -> 8; matrix products, arithmetic and copies ran while one was open for 16% -> 13% of each run, Pallas kernels for 0% -> 0%
where the time goes in v2:
time: 709 us; the launch traced here: 705 us
  waiting for transfers between devices  422 us (60%)
  Pallas kernels  127 us (18%)
  local copies, waits for them, and re-layouts  54.4 us (8%)
  matrix products  44.7 us (6%)
  other arithmetic  33.1 us (5%)
  between operations  16.1 us (2%)
  starting transfers between devices  7.24 us (1%)
    psum x1, waiting for transfers between devices, local(): vectors = lax.psum(vectors, ('ctx', 'fsdp'))  143 us
    pallas_call x1, Pallas kernels, first_call(): pl.pallas_call(first_kernel, out_shape=[jax.ShapeDtypeStruct(*s) for s in...  127 us
    reduce_scatter x1, waiting for transfers between devices, local(): wide = lax.psum_scatter(wide, 'fsdp', scatter_dimension=0, tiled=True)  86.7 us
    reduce_scatter x1, waiting for transfers between devices, local(): lax.psum_scatter(grad_down, 'fsdp', scatter_dimension=0, tiled=True)  72.1 us
    psum x1, waiting for transfers between devices, local(): proj_weight_grad = lax.psum(grad_proj, 'ctx').astype(f32)  44.8 us
    dot_general x8, matrix products, dot(): lax.dot_general(a, b, (((ca,), (cb,)), ((), ())), preferred_element_type=...  44.7 us
    unnamed x40, local copies, waits for them, and re-layouts  27.7 us
    all_gather x1, waiting for transfers between devices, local(): wide = lax.all_gather(wide, 'ctx', axis=0, tiled=False)  27.5 us
  transfers between devices with their start and end apart: 10, of which 8 were waited for; matrix products, arithmetic and copies ran while one was open for 13% of the time, Pallas kernels for 0%

profile of v2, /device:TPU:1, one launch (start us, length us, event | category | flops | bytes accessed | tf_op | source)
XLA Modules:
  0.0 704.5 jit_solution(16217169673833010189)
XLA Ops:
  17.0 126.6 %first.1 = (bf16[1024,2048]{1,0:T(8,128)(2,1)}, bf16[4,4,144,768]{3,2,1,0:T(8,128)(2,1)}, bf16[4,4,80,2048]{3,2,1,0:T(8,128)(2,1)}, bf16[4,4,128,1024]{3,2,1,0:T...) custom-call(bf16[128,2048]{1,0:T(8,128)(2,1)} %bitcast.79, ...), custom_call_target="tpu_custom_call" | custom-call | flops 24999999488 | bytes 40000000 | tf_op jit(solution)/shard_map/first/pallas_call | solution.py:649
  143.7 4.7 convolution_convert_fusion.3
  150.1 3.4 fusion.27
  153.5 6.1 add_convert_fusion
  164.0 4.5 fusion.26
  168.6 3.3 add_convert_fusion.1
  172.1 9.5 %convolution_convert_fusion = bf16[1024,2048]{1,0:T(8,128)(2,1)} fusion(bf16[1024,1024]{1,0:T(8,128)(2,1)} %get-tuple-element.25, bf16[1024,2048]{1,0:T(8,128)(2,1)} %bitcast.99), kind=kOutput, calls=%fused_computation.4 | convolution fusion | flops 4297064448 | bytes 10485760 | tf_op jit(solution)/shard_map/dot_general | solution.py:29
  181.7 8.0 %convolution_convert_fusion.2 = bf16[2048,768]{0,1:T(8,128)(2,1)} fusion(bf16[1024,2048]{1,0:T(8,128)(2,1)} %get-tuple-element.31, bf16[1024,768]{1,0:T(8,128)(2,1)} %get-tuple-element.27), kind=kOutput, calls=%fused_computation.6 | convolution fusion | flops 3222798336 | bytes 8912896 | tf_op jit(solution)/shard_map/dot_general | solution.py:29
  189.8 5.0 convolution_convert_fusion.1
  194.8 6.0 pad_maximum_fusion
  200.8 10.1 %copy.65 = bf16[2048,1792]{1,0:T(8,128)(2,1)} copy(bf16[2048,1792]{0,1:T(8,128)(2,1)} %pad_maximum_fusion) | data formatting | bytes 14680064
  214.8 23.0 %all-reduce.7.cloned.1.call-done = bf16[2,128,2048]{2,1,0:T(8,128)(2,1)} async-done(((bf16[2,128,2048]{2,1,0:T(8,128)(2,1)}), bf16[2,128,2048]{2,1,0:T(8,128)(2,1)}) %all-reduce.7.cloned.1.call-update) | async-done | bytes 1048592 | tf_op jit(solution)/shard_map/psum | solution.py:759
  246.8 72.1 %reduce-scatter.11.cloned.1.call-done = bf16[64,2048]{1,0:T(8,128)(2,1)} async-done(((bf16[1024,2048]{1,0:T(8,128)(2,1)}), bf16[64,2048]{1,0:T(8,128)(2,1)}) %reduce-scatter.11.cloned.1.call-update) | async-done | bytes 262160 | tf_op jit(solution)/shard_map/reduce_scatter | solution.py:758
  319.0 86.7 %reduce-scatter.13.cloned.1.call-done = bf16[128,1792]{1,0:T(8,128)(2,1)} async-done(((bf16[2048,1792]{1,0:T(8,128)(2,1)}), bf16[128,1792]{1,0:T(8,128)(2,1)}) %reduce-scatter.13.cloned.1.call-update) | async-done | bytes 458768 | tf_op jit(solution)/shard_map/reduce_scatter | solution.py:757
  409.5 6.2 all-to-all-start
  415.8 4.7 all-to-all-done
  422.8 44.8 %all-reduce.9.cloned.1.call-done = bf16[128,2048]{1,0:T(8,128)(2,1)} async-done(((bf16[128,2048]{1,0:T(8,128)(2,1)}), bf16[128,2048]{1,0:T(8,128)(2,1)}) %all-reduce.9.cloned.1.call-update) | async-done | bytes 524304 | tf_op jit(solution)/shard_map/psum | solution.py:762
  469.7 142.7 %all-reduce.5.cloned.1.call-done = f32[16,1280]{1,0:T(8,128)} async-done(((f32[16,1280]{1,0:T(8,128)}), f32[16,1280]{1,0:T(8,128)}) %all-reduce.5.cloned.1.call-update) | async-done | bytes 81936 | tf_op jit(solution)/shard_map/psum | solution.py:790
  616.4 20.7 %all-gather.4.cloned.1.call-done = bf16[512,2048]{1,0:T(8,128)(2,1)} async-done(((bf16[64,2048]{1,0:T(8,128)(2,1)}), bf16[512,2048]{1,0:T(8,128)(2,1)}) %all-gather.4.cloned.1.call-update) | async-done | bytes 2097168 | tf_op jit(solution)/shard_map/all_gather | solution.py:764
  637.1 4.1 convert_element_type.150
  641.2 27.5 %all-gather.6.cloned.1.call-done = bf16[1024,1792]{1,0:T(8,128)(2,1)} async-done(((bf16[128,1792]{1,0:T(8,128)(2,1)}), bf16[1024,1792]{1,0:T(8,128)(2,1)}) %all-gather.6.cloned.1.call-update) | async-done | bytes 3670032 | tf_op jit(solution)/shard_map/all_gather | solution.py:763
  680.7 5.3 copy.61
  686.0 4.7 copy.62
  690.7 5.6 copy.64
  (102 shorter events, 52.9 us)
Async XLA Ops:
  8.0 229.8 %all-reduce.7.cloned.1.call-start = ((), (), s32[]{:S(2)}) async-start(), calls=%async_computation.8 | async-start | bytes 2097152 | tf_op jit(solution)/shard_map/psum | solution.py:759
  143.7 5.0 copy-start.2
  148.4 91.3 %reduce-scatter.9.cloned.1.call-start = ((), (), s32[]{:S(2)}) async-start(), calls=%async_computation.6 | async-start | bytes 4718592 | tf_op jit(solution)/shard_map/reduce_scatter | solution.py:746
  148.7 1.4 copy-start.4
  150.1 3.5 copy-start.3
  150.1 3.5 copy-start.9
  159.7 83.2 %reduce-scatter.7.cloned.1.call-start = ((), (), s32[]{:S(2)}) async-start(), calls=%async_computation.5 | async-start | bytes 4718592 | tf_op jit(solution)/shard_map/reduce_scatter | solution.py:743
  161.2 2.9 copy-start.10
  164.0 4.5 copy-start.5
  171.9 147.0 %reduce-scatter.11.cloned.1.call-start = ((), (), s32[]{:S(2)}) async-start(), calls=%async_computation.10 | async-start | bytes 4456448 | tf_op jit(solution)/shard_map/reduce_scatter | solution.py:758
  181.7 224.1 %reduce-scatter.13.cloned.1.call-start = ((), (), s32[]{:S(2)}) async-start(), calls=%async_computation.13 | async-start | bytes 7798784 | tf_op jit(solution)/shard_map/reduce_scatter | solution.py:757
  181.7 8.1 %copy-start.11 = (bf16[1024,2048]{1,0:T(8,128)(2,1)S(1)}, bf16[1024,2048]{1,0:T(8,128)(2,1)}, u32[]{:S(2)}) copy-start(bf16[1024,2048]{1,0:T(8,128)(2,1)} %get-tuple-element.31) | copy-start | bytes 12582916
  210.9 3.8 copy-start
  210.9 256.7 %all-reduce.9.cloned.1.call-start = ((), (), s32[]{:S(2)}) async-start(), calls=%async_computation.9 | async-start | bytes 1048576 | tf_op jit(solution)/shard_map/psum | solution.py:762
  214.6 191.1 %copy-start.7 = (f32[8,1024]{1,0:T(8,128)S(1)}, f32[8,1024]{1,0:T(8,128)}, u32[]{:S(2)}) copy-start(f32[8,1024]{1,0:T(8,128)} %get-tuple-element.30) | copy-start | bytes 98308
  239.7 372.7 %all-reduce.5.cloned.1.call-start = ((), (), s32[]{:S(2)}) async-start(), calls=%async_computation.7 | async-start | bytes 163840 | tf_op jit(solution)/shard_map/psum | solution.py:790
  246.1 0.6 copy-start.6
  246.7 390.4 %all-gather.4.cloned.1.call-start = ((), (), s32[]{:S(2)}) async-start(), calls=%async_computation.11 | async-start | bytes 2359296 | tf_op jit(solution)/shard_map/all_gather | solution.py:764
  318.9 349.8 %all-gather.6.cloned.1.call-start = ((), (), s32[]{:S(2)}) async-start(), calls=%async_computation.12 | async-start | bytes 4128768 | tf_op jit(solution)/shard_map/all_gather | solution.py:763
  409.5 10.9 %all-to-all-start = ((f32[8,1,512]{2,1,0:T(1,128)}), f32[8,1,512]{2,1,0:T(1,128)S(1)}, u32[]{:S(2)}, u32[]{:S(2)}) async-start(f32[8,1,512]{2,1,0:T(1,128)} %reshape.237), calls=%async_computation.2 | async-start | bytes 32768 | tf_op jit(solution)/shard_map/all_to_all | solution.py:795
  613.7 82.6 %copy-start.8 = (f32[128]{0:T(128)}, f32[128]{0:T(128)S(1)}, u32[]{:S(2)}) copy-start(f32[128]{0:T(128)S(1)} %get-tuple-element.154) | copy-start | bytes 1540
  668.8 2.5 copy-start.1
Sparse Core Ops, SparseCore 0:
  148.6 89.1 all-reduce.6
Sparse Core Ops, SparseCore 1:
  159.8 39.0 reduce-scatter.8
  201.7 36.6 reduce-scatter.6
  241.6 77.3 reduce-scatter.10
  322.8 82.8 reduce-scatter.12
  408.7 58.9 all-reduce.8
  473.7 138.7 all-reduce.4
  614.0 23.0 all-gather.3
  638.7 30.0 all-gather.5

commit v3 on v2

--- a/solution.py
+++ b/solution.py
@@ -141,7 +141,7 @@
     yield
 
 
-def line_gather(t, cuts, copies):
+def line_gather(t, cuts, copies, own=None):
     c, f, z, core, y, x = place()
     r0, r1, r2 = cuts
     h0, h1 = pl.ds(r0, r1 - r0), pl.ds(r1, r2 - r1)
@@ -155,9 +155,11 @@
     def got(k, part):
         copies.arrived(k, t.at[part])
 
-    send(0, (z, core), to_zu)
-    send(1, (z, core), to_zd)
-    send(2, (z, core), to_core)
+    mine = t.at[z, core]
+    own = mine if own is None else own
+    copies.start(0, own, mine, to_zu)
+    copies.start(1, own, mine, to_zd)
+    copies.start(2, own, mine, to_core)
     yield
     got(0, (zd, core))
     send(3, (zd, core, h0), to_zu)
@@ -697,11 +699,581 @@
     )
 
 
-def standardize(inputs):
-    average = jnp.mean(inputs, axis=-1, keepdims=True)
-    centered = inputs - average
-    variance = jnp.mean(centered * centered, axis=-1, keepdims=True)
-    return centered * lax.rsqrt(variance + epsilon)
+def add_into(target, part, *others):
+    total = target[part].astype(f32)
+    for ref, piece in others:
+        total = total + ref[piece].astype(f32)
+    target[part] = total.astype(bf16)
+
+
+def plane_reduce(g, cuts, ra, rb, copies):
+    c, f, z, core, y, x = place()
+    r0, r1, r2, r3, r4 = cuts
+    first, last = pl.ds(r0, r2 - r0), pl.ds(r2, r4 - r2)
+    q0, q1, q2, q3 = (pl.ds(a, b - a) for a, b in zip(cuts[:-1], cuts[1:]))
+    s0, s1, s2, s3 = (pl.ds(0, b - a) for a, b in zip(cuts[:-1], cuts[1:]))
+    xu, xd, xo = up1(x), down1(x), over(x)
+    yu, yd, yo = up1(y), down1(y), over(y)
+    to_xu, to_xd = (c, y * 4 + xu), (c, y * 4 + xd)
+    to_yu, to_yd = (c, yu * 4 + x), (c, yd * 4 + x)
+    lo, hi, every = pl.ds(0, 2), pl.ds(2, 2), pl.ds(0, 4)
+    near, far = pl.ds(0, 2), pl.ds(2, 4)
+
+    def send(k, part, ref, piece, device):
+        copies.start(k, g.at[part], ref.at[piece], device)
+
+    def got(k, ref, piece):
+        copies.arrived(k, ref.at[piece])
+
+    send(0, (yo, lo, first), ra, (0, near), to_yu)
+    send(1, (yo, hi, first), ra, (1, near), to_yd)
+    send(2, (lo, xo, last), rb, (0, near), to_xu)
+    send(3, (hi, xo, last), rb, (1, near), to_xd)
+    yield
+    got(0, ra, (0, near))
+    add_into(g, (yu, lo, first), (ra, (0, near)))
+    send(4, (yu, every, first), ra, (0, far), to_yu)
+    got(1, ra, (1, near))
+    add_into(g, (yd, hi, first), (ra, (1, near)))
+    send(5, (yd, every, first), ra, (1, far), to_yd)
+    got(2, rb, (0, near))
+    add_into(g, (lo, xu, last), (rb, (0, near)))
+    send(6, (every, xu, last), rb, (0, far), to_xu)
+    got(3, rb, (1, near))
+    add_into(g, (hi, xd, last), (rb, (1, near)))
+    send(7, (every, xd, last), rb, (1, far), to_xd)
+    yield
+    got(4, ra, (0, far))
+    got(5, ra, (1, far))
+    add_into(g, (y, every, first), (ra, (0, far)), (ra, (1, far)))
+    send(8, (y, xo, q0), ra, (0, 6, s0), to_xu)
+    send(9, (y, xo, q1), ra, (1, 6, s1), to_xd)
+    got(6, rb, (0, far))
+    got(7, rb, (1, far))
+    add_into(g, (every, x, last), (rb, (0, far)), (rb, (1, far)))
+    send(10, (yo, x, q2), rb, (0, 6, s2), to_yu)
+    send(11, (yo, x, q3), rb, (1, 6, s3), to_yd)
+    yield
+    got(8, ra, (0, 6, s0))
+    add_into(g, (y, xu, q0), (ra, (0, 6, s0)))
+    send(12, (y, xu, first), ra, (0, 7), to_xu)
+    got(9, ra, (1, 6, s1))
+    add_into(g, (y, xd, q1), (ra, (1, 6, s1)))
+    send(13, (y, xd, first), ra, (1, 7), to_xd)
+    got(10, rb, (0, 6, s2))
+    add_into(g, (yu, x, q2), (rb, (0, 6, s2)))
+    send(14, (yu, x, last), rb, (0, 7), to_yu)
+    got(11, rb, (1, 6, s3))
+    add_into(g, (yd, x, q3), (rb, (1, 6, s3)))
+    send(15, (yd, x, last), rb, (1, 7), to_yd)
+    yield
+    got(12, ra, (0, 7))
+    got(13, ra, (1, 7))
+    add_into(g, (y, x, first), (ra, (0, 7)), (ra, (1, 7)))
+    got(14, rb, (0, 7))
+    got(15, rb, (1, 7))
+    add_into(g, (y, x, last), (rb, (0, 7)), (rb, (1, 7)))
+    yield
+
+
+def line_reduce(g, cuts, rc, r1, r2, copies):
+    c, f, z, core, y, x = place()
+    c0, c1, c2 = cuts
+    h0, h1 = pl.ds(c0, c1 - c0), pl.ds(c1, c2 - c1)
+    s0, s1 = pl.ds(0, c1 - c0), pl.ds(0, c2 - c1)
+    zu, zd, zo = up1(z), down1(z), over(z)
+    to_zu, to_zd, to_core = (zu * 2 + core, f), (zd * 2 + core, f), (z * 2 + 1 - core, f)
+    every = pl.ds(0, 4)
+    copies.start(0, g.at[every, 1 - core], rc, to_core)
+    yield
+    copies.arrived(0, rc)
+
+    def add_row(i, carry):
+        add_into(g, (i, core), (rc, (i,)))
+        return carry
+
+    lax.fori_loop(0, 4, add_row, 0)
+    copies.start(1, g.at[zo, core, h0], r1.at[0, s0], to_zu)
+    copies.start(2, g.at[zo, core, h1], r1.at[1, s1], to_zd)
+    yield
+    copies.arrived(1, r1.at[0, s0])
+    add_into(g, (zu, core, h0), (r1, (0, s0)))
+    copies.start(3, g.at[zu, core], r2.at[0], to_zu)
+    copies.arrived(2, r1.at[1, s1])
+    add_into(g, (zd, core, h1), (r1, (1, s1)))
+    copies.start(4, g.at[zd, core], r2.at[1], to_zd)
+    yield
+    copies.arrived(3, r2.at[0])
+    copies.arrived(4, r2.at[1])
+    yield
+
+
+def second_kernel(
+    n_in,
+    w1_in,
+    w2_in,
+    w3_in,
+    u_in,
+    dproj_in,
+    ctx_in,
+    act_in,
+    dhid_in,
+    tokens,
+    cotangent,
+    lse,
+    block_out,
+    token_grad,
+    lse_out,
+    gq_out,
+    gu_out,
+    gd_out,
+    gp_out,
+    w1,
+    w2,
+    w3,
+    n,
+    u,
+    dproj,
+    ctx,
+    act,
+    dhid,
+    own_tokens,
+    own_cot,
+    vecs,
+    vector_rows,
+    zo_buf,
+    zd_buf,
+    zo_rc,
+    zo_r1,
+    zo_r2,
+    zd_rc,
+    zd_r1,
+    zd_r2,
+    ra1,
+    rb1,
+    ra2,
+    rb2,
+    ra3,
+    rb3,
+    gp,
+    lse_own,
+    sem1,
+    sem2,
+    sem3,
+    sem_zo,
+    sem_zd,
+    sem_lq,
+    sem_lu,
+    sem_ld,
+    sem_p,
+    sem_b,
+    sem_l,
+    sem_o,
+):
+    c, f, z, core, y, x = place()
+    lane = lax.broadcasted_iota(jnp.int32, (1, 128), 1)
+    odd = core == 1
+    owner = c * 2 + f // 8
+    own_rows = f // 2 == c
+
+    pairs = (
+        (act_in, act),
+        (w2_in, w2),
+        (ctx_in, ctx),
+        (u_in, u),
+        (dproj_in, dproj),
+        (w1_in, w1),
+        (dhid_in, dhid),
+        (w3_in, w3),
+        (n_in, n),
+        (tokens, own_tokens),
+        (cotangent, own_cot),
+    )
+    loads = [pltpu.make_async_copy(a, b, sem_l.at[i]) for i, (a, b) in enumerate(pairs)]
+    for copy in loads:
+        copy.start()
+    enter(False, True)
+
+    copies1 = Copies(sem1.at[0], sem1.at[1])
+    copies2 = Copies(sem2.at[0], sem2.at[1])
+    copies3 = Copies(sem3.at[0], sem3.at[1])
+    copies_zo = Copies(sem_zo.at[0], sem_zo.at[1])
+    copies_zd = Copies(sem_zd.at[0], sem_zd.at[1])
+    copies_lq = Copies(sem_lq.at[0], sem_lq.at[1])
+    copies_lu = Copies(sem_lu.at[0], sem_lu.at[1])
+    copies_ld = Copies(sem_ld.at[0], sem_ld.at[1])
+    reduce1 = plane_reduce(w1, CUTS1, ra1, rb1, copies1)
+    reduce2 = plane_reduce(w2, CUTS2, ra2, rb2, copies2)
+    reduce3 = plane_reduce(w3, CUTS3, ra3, rb3, copies3)
+    reduce_o = line_reduce(zo_buf, (0, 64, 144), zo_rc, zo_r1, zo_r2, copies_zo)
+    reduce_d = line_reduce(zd_buf, (0, 64, 128), zd_rc, zd_r1, zd_r2, copies_zd)
+    gather_q = line_gather(gq_out, (0, 64, 144), copies_lq, w1.at[y, x])
+    gather_u = line_gather(gu_out, (0, 64, 128), copies_lu, w3.at[y, x])
+    gather_d = line_gather(gd_out, (0, 32, 64), copies_ld, w2.at[y, x, pl.ds(0, 64)])
+    outs = []
+
+    def put(src, dst):
+        copy = pltpu.make_async_copy(src, dst, sem_o.at[len(outs)])
+        copy.start()
+        outs.append(copy)
+
+    for b in range(8):
+        part = jnp.concatenate([lse[j : j + 1, b * 128 : b * 128 + 128] for j in range(4)], axis=1)
+        wide = jnp.concatenate([jnp.where(c % 4 == s, part, 0.0) for s in range(4)], axis=1)
+        high = wide.astype(bf16).astype(f32)
+        row = lax.broadcasted_iota(jnp.int32, (16, 1), 0)
+        both = jnp.where(row == c // 4, high, jnp.where(row == 2 + c // 4, wide - high, 0.0))
+        zo_buf[b // 2, b % 2, 128:144, :] = both.astype(bf16)
+
+    for i in range(3):
+        loads[i].wait()
+
+    def out_part(i, carry):
+        columns = pl.ds(pl.multiple_of(i * 512, 512), 512)
+        total = dot(act[...], w2[:, :, pl.ds(0, 64), columns].reshape(UNITS, 512), 1, 0)
+        total = total + dot(ctx[...], w2[:, :, pl.ds(64, 16), columns].reshape(COLS, 512), 1, 0)
+        zo_buf[:, :, pl.ds(0, 128), columns] = total.astype(bf16).reshape(4, 2, 128, 512)
+        return carry
+
+    lax.fori_loop(0, 4, out_part, 0)
+    next(reduce_o)
+    loads[3].wait()
+
+    def down_part(i, carry):
+        columns = pl.ds(pl.multiple_of(i * 512, 512), 512)
+        right = u[:, :, :, columns].reshape(SEQ, 512)
+        grads = dot(act[...], right, 0, 0).astype(bf16)
+        w2[:, :, pl.ds(0, 64), columns] = grads.reshape(4, 4, 64, 512)
+        grads = dot(ctx[...], right, 0, 0).astype(bf16)
+        w2[:, :, pl.ds(64, 16), columns] = grads.reshape(4, 4, 16, 512)
+        return carry
+
+    lax.fori_loop(0, 4, down_part, 0)
+    next(reduce2)
+    next(reduce_o)
+    for i in range(4, 8):
+        loads[i].wait()
+    vecs[...] = w1[:, :, 128:144, 0:128].reshape(16, 16, 128).astype(f32)
+    gain = jnp.concatenate([vecs[i, 0:1, :] for i in range(16)], axis=1)
+
+    def normed_part(i, carry):
+        columns = pl.ds(pl.multiple_of(i * 512, 512), 512)
+        total = dot(dproj[...], w1[i, :, pl.ds(0, 128), :].reshape(512, 768), 1, 1)
+        total = total + dot(dhid[...], w3[i].reshape(512, UNITS), 1, 1)
+        zd_buf[:, :, :, columns] = total.astype(bf16).reshape(4, 2, 128, 512)
+        return carry
+
+    lax.fori_loop(0, 2, normed_part, 0)
+    next(reduce2)
+    lax.fori_loop(2, 4, normed_part, 0)
+    next(reduce_d)
+    next(reduce_o)
+    loads[8].wait()
+
+    def up_part(i, carry):
+        columns = pl.ds(pl.multiple_of(i * 512, 512), 512)
+        grads = dot(n[:, columns], dhid[...], 0, 0).astype(bf16)
+        w3[i] = grads.reshape(4, 128, UNITS)
+        return carry
+
+    lax.fori_loop(0, 2, up_part, 0)
+    next(reduce2)
+    lax.fori_loop(2, 4, up_part, 0)
+    next(reduce3)
+    next(reduce_d)
+    next(reduce2)
+
+    def qkv_part(i, carry):
+        columns = pl.ds(pl.multiple_of(i * 512, 512), 512)
+        grads = dot(n[:, columns], dproj[...], 0, 0).astype(bf16)
+        w1[i, :, pl.ds(0, 128), :] = grads.reshape(4, 128, 768)
+        return carry
+
+    lax.fori_loop(0, 4, qkv_part, 0)
+    next(reduce3)
+    next(reduce_d)
+    next(reduce2)
+
+    next(gather_d)
+    put(w2.at[y, x, pl.ds(0, 64)], gd_out.at[z, core])
+    rows = w2.at[y, x, pl.ds(64, 16)]
+    for j in range(8):
+        slot = gp.at[pl.ds(16 * j, 16)]
+
+        @pl.when((f % 8 == j) & (owner != f))
+        def _():
+            pltpu.make_async_remote_copy(
+                src_ref=rows,
+                dst_ref=slot,
+                send_sem=sem_p.at[0, 0],
+                recv_sem=sem_p.at[1, j],
+                device_id=(c, owner),
+                device_id_type=MESH,
+            ).start()
+
+        @pl.when((f % 8 == j) & (owner == f))
+        def _():
+            local = pltpu.make_async_copy(rows, slot, sem_p.at[0, 1])
+            local.start()
+            local.wait()
+
+    loads[9].wait()
+    loads[10].wait()
+    next(reduce_o)
+    proj_bias = jnp.concatenate([vecs[i, 2:3, :] for i in range(16)], axis=1)
+    down_bias = jnp.concatenate([vecs[i, 3:4, :] for i in range(16)], axis=1)
+
+    def finish_out(i, carry):
+        part = pl.ds(pl.multiple_of(i * 32, 32), 32)
+        total = zo_buf[z, core, part, :].astype(f32)
+        total = total + zo_r2[0, part, :].astype(f32) + zo_r2[1, part, :].astype(f32)
+        total = own_tokens[part, :].astype(f32) + total + proj_bias + down_bias
+        zo_r2[0, part, :] = total.astype(bf16)
+        return carry
+
+    tail = pl.ds(128, 16)
+    sums = zo_buf[z, core, tail, :].astype(f32)
+    sums = sums + zo_r2[0, tail, :].astype(f32) + zo_r2[1, tail, :].astype(f32)
+    sums = sums[0:2, :] + sums[2:4, :]
+    for h in range(32):
+        lse_own[h : h + 1, :] = sums[h // 16 : h // 16 + 1, (h % 16) * 128 : (h % 16) * 128 + 128]
+    lax.fori_loop(0, 4, finish_out, 0)
+    put(zo_r2.at[0, pl.ds(0, 128)], block_out)
+    put(lse_own, lse_out)
+    next(reduce3)
+
+    next(reduce_d)
+    zero = jnp.zeros((1, WIDTH), f32)
+
+    def finish_grad(i, carry):
+        d_gain, d_shift, d_bias = carry
+        part = pl.ds(pl.multiple_of(i * 32, 32), 32)
+        grads = zd_buf[z, core, part, :].astype(f32)
+        grads = grads + zd_r2[0, part, :].astype(f32) + zd_r2[1, part, :].astype(f32)
+        values = own_tokens[part, :].astype(f32)
+        average = jnp.mean(values, axis=-1, keepdims=True)
+        centered = values - average
+        variance = jnp.mean(centered * centered, axis=-1, keepdims=True)
+        scale = lax.rsqrt(variance + epsilon)
+        standard = centered * scale
+        d_gain = d_gain + jnp.sum(grads * standard, axis=0, keepdims=True)
+        d_shift = d_shift + jnp.sum(grads, axis=0, keepdims=True)
+        scaled = grads * gain
+        inner = scaled - jnp.mean(scaled, axis=-1, keepdims=True)
+        inner = inner - standard * jnp.mean(scaled * standard, axis=-1, keepdims=True)
+        upstream = own_cot[part, :].astype(f32)
+        d_bias = d_bias + jnp.sum(upstream, axis=0, keepdims=True)
+        zd_r2[0, part, :] = (upstream + scale * inner).astype(bf16)
+        return d_gain, d_shift, d_bias
+
+    d_gain, d_shift, d_bias = lax.fori_loop(0, 4, finish_grad, (zero, zero, zero))
+    put(zd_r2.at[0], token_grad)
+
+    vector_rows[...] = jnp.zeros((16, 16, 128), f32)
+    for i in range(16):
+        lanes = slice(i * 128, i * 128 + 128)
+        vector_rows[i, 0:1, :] = d_gain[:, lanes]
+        vector_rows[i, 1:2, :] = d_shift[:, lanes]
+        vector_rows[i, 2:3, :] = d_bias[:, lanes]
+    ones = jnp.ones((8, SEQ), bf16)
+    d_qkv = dot(ones, dproj[...], 1, 0)[0:1, :]
+    d_up = dot(ones, dhid[...], 1, 0)[0:1, :]
+    for which in range(3):
+        for i in range(2):
+            row = which * 16 + c * 2 + i
+            start = which * COLS + i * 128
+            vector_rows[row // 3, pl.ds(3 + row % 3, 1), :] = d_qkv[:, start : start + 128]
+    for m in range(8):
+        both = d_up[:, m * 128 : m * 128 + 128]
+        moved = pltpu.roll(both, 64, 1)
+        mine = (lane >= 64) == odd
+        vector_rows[2 * m, pl.ds(6 + c // 2, 1), :] = jnp.where(
+            mine, jnp.where(odd, moved, both), 0.0
+        )
+        vector_rows[2 * m + 1, pl.ds(6 + c // 2, 1), :] = jnp.where(
+            mine, jnp.where(odd, both, moved), 0.0
+        )
+    w1[:, :, 128:144, 0:128] = vector_rows[...].reshape(4, 4, 16, 128).astype(bf16)
+    w1[:, :, 128:144, 128:768] = jnp.zeros((4, 4, 16, 640), bf16)
+    next(reduce1)
+    next(gather_d)
+    next(reduce3)
+    next(reduce1)
+
+    def trade(k, src, dst, device):
+        return pltpu.make_async_remote_copy(
+            src_ref=src,
+            dst_ref=dst,
+            send_sem=sem_b.at[0, k],
+            recv_sem=sem_b.at[1, k],
+            device_id=device,
+            device_id_type=MESH,
+        )
+
+    for j in range(8):
+
+        @pl.when(own_rows & ((f % 2) * 8 + j != f))
+        def _():
+            slot = gp.at[pl.ds(16 * j, 16)]
+            pltpu.make_async_remote_copy(
+                src_ref=slot,
+                dst_ref=slot,
+                send_sem=sem_p.at[0, 0],
+                recv_sem=sem_p.at[1, j],
+                device_id=other_core(),
+                device_id_type=MESH,
+            ).wait_recv()
+
+    mine = core == x // 2
+    turns = (z - y + 4) % 4
+    to_zu, to_zd = (up1(z) * 2 + core, f), (down1(z) * 2 + core, f)
+    to_core = other_core()
+    h0, h1 = gp.at[pl.ds(0, 64)], gp.at[pl.ds(64, 64)]
+
+    @pl.when(mine & (turns == 0))
+    def _():
+        trade(0, gp, gp, to_zu).start()
+        trade(1, gp, gp, to_zd).start()
+
+    @pl.when(mine & (turns == 1))
+    def _():
+        trade(0, gp, gp, to_core).wait_recv()
+        trade(2, h0, h0, to_zu).start()
+
+    @pl.when(mine & (turns == 3))
+    def _():
+        trade(1, gp, gp, to_core).wait_recv()
+        trade(3, h1, h1, to_zd).start()
+
+    next(gather_d)
+    next(reduce3)
+    next(gather_u)
+    put(w3.at[y, x], gu_out.at[z, core])
+    next(reduce1)
+
+    @pl.when(mine & (turns == 2))
+    def _():
+        trade(2, h0, h0, to_core).wait_recv()
+        trade(3, h1, h1, to_core).wait_recv()
+
+    @pl.when(mine)
+    def _():
+        trade(4, gp, gp, to_core).start()
+
+    next(gather_u)
+    next(reduce1)
+    next(gather_u)
+    next(reduce1)
+    next(gather_q)
+    put(w1.at[y, x], gq_out.at[z, core])
+
+    @pl.when(jnp.logical_not(mine))
+    def _():
+        trade(4, gp, gp, to_core).wait_recv()
+
+    put(gp, gp_out)
+    next(gather_q)
+    next(gather_d)
+    next(gather_u)
+    next(gather_q)
+    next(gather_q)
+
+    for copies in (
+        copies1, copies2, copies3, copies_zo, copies_zd, copies_lq, copies_lu, copies_ld
+    ):
+        copies.sent()
+
+    @pl.when(owner != f)
+    def _():
+        pltpu.make_async_remote_copy(
+            src_ref=rows,
+            dst_ref=gp.at[pl.ds(0, 16)],
+            send_sem=sem_p.at[0, 0],
+            recv_sem=sem_p.at[1, 0],
+            device_id=(c, owner),
+            device_id_type=MESH,
+        ).wait_send()
+
+    @pl.when(mine & (turns == 0))
+    def _():
+        trade(0, gp, gp, to_zu).wait_send()
+        trade(1, gp, gp, to_zd).wait_send()
+
+    @pl.when(mine & (turns == 1))
+    def _():
+        trade(2, h0, h0, to_zu).wait_send()
+
+    @pl.when(mine & (turns == 3))
+    def _():
+        trade(3, h1, h1, to_zd).wait_send()
+
+    @pl.when(mine)
+    def _():
+        trade(4, gp, gp, to_core).wait_send()
+
+    for copy in outs:
+        copy.wait()
+
+
+def second_call(n, w1, w2, w3, u, dproj, ctx, act, dhid, tokens, cotangent, lse):
+    anyspace = pl.BlockSpec(memory_space=pl.ANY)
+    vmem = pl.BlockSpec(memory_space=VM)
+    dma = pltpu.SemaphoreType.DMA
+    given = (w1, w2, w3, n, u, dproj, ctx, act, dhid, tokens, cotangent)
+    return pl.pallas_call(
+        second_kernel,
+        out_shape=[
+            jax.ShapeDtypeStruct((128, WIDTH), bf16),
+            jax.ShapeDtypeStruct((128, WIDTH), bf16),
+            jax.ShapeDtypeStruct((32, 128), f32),
+            jax.ShapeDtypeStruct((4, 2, 144, 768), bf16),
+            jax.ShapeDtypeStruct((4, 2, 128, UNITS), bf16),
+            jax.ShapeDtypeStruct((4, 2, 64, WIDTH), bf16),
+            jax.ShapeDtypeStruct((128, WIDTH), bf16),
+        ],
+        in_specs=[anyspace] * 11 + [vmem],
+        out_specs=[anyspace] * 7,
+        scratch_shapes=[VM(a.shape, a.dtype) for a in given]
+        + [
+            VM((16, 16, 128), f32),
+            VM((16, 16, 128), f32),
+            VM((4, 2, 144, WIDTH), bf16),
+            VM((4, 2, 128, WIDTH), bf16),
+            VM((4, 144, WIDTH), bf16),
+            VM((2, 80, WIDTH), bf16),
+            VM((2, 144, WIDTH), bf16),
+            VM((4, 128, WIDTH), bf16),
+            VM((2, 64, WIDTH), bf16),
+            VM((2, 128, WIDTH), bf16),
+            VM((2, 8, 64, 768), bf16),
+            VM((2, 8, 80, 768), bf16),
+            VM((2, 8, 32, WIDTH), bf16),
+            VM((2, 8, 48, WIDTH), bf16),
+            VM((2, 8, 64, UNITS), bf16),
+            VM((2, 8, 64, UNITS), bf16),
+            VM((128, WIDTH), bf16),
+            VM((32, 128), f32),
+            dma((2, 16)),
+            dma((2, 16)),
+            dma((2, 16)),
+            dma((2, 5)),
+            dma((2, 5)),
+            dma((2, 8)),
+            dma((2, 8)),
+            dma((2, 8)),
+            dma((2, 8)),
+            dma((2, 5)),
+            dma((11,)),
+            dma((7,)),
+        ],
+        compiler_params=pltpu.CompilerParams(
+            collective_id=2, has_side_effects=True, vmem_limit_bytes=62 * 1024 * 1024
+        ),
+        cost_estimate=pl.CostEstimate(
+            flops=26 * 10**9, bytes_accessed=60 * 10**6, transcendentals=0
+        ),
+        name="second",
+    )(n, w1, w2, w3, u, dproj, ctx, act, dhid, tokens, cotangent, lse)
 
 
 def local(
@@ -719,92 +1291,32 @@
     down_bias,
     cotangent,
 ):
-    c, f, z, core, y, x = place()
-    width, cols, shard, ring, shards, strip = WIDTH, COLS, 128, 8, 16, 64
-    hidden_width = HIDDEN
     packed = jnp.concatenate([ln_gain, ln_shift, proj_bias, down_bias, qkv_bias, up_bias])
     vec = jnp.pad(packed.reshape(11, 128), ((0, 5), (0, 0)))
-    normed, w1, w2, w3, u, d_projected, context, active, d_hidden, lse = first_call(
+    n, w1, w2, w3, u, dproj, ctx, act, dhid, lse = first_call(
         tokens[0], cotangent[0], qkv_weight, proj_weight, up_weight, down_weight, segments, vec
     )
-    vecs = w1[:, :, 128:, :128].reshape(16, 16, 128)
-    gain = vecs[:, 0].reshape(width).astype(f32)
-    proj_b = vecs[:, 2].reshape(width).astype(f32)
-    down_b = vecs[:, 3].reshape(width).astype(f32)
-    qkv_w = w1[:, :, :128].reshape(width, 3 * cols)
-    up_w = w3.reshape(width, 1024)
-    down_w = w2[:, :, :64].reshape(1024, width)
-    proj_w = w2[:, :, 64:].reshape(cols, width)
-    upstream = u.reshape(1024, width)
-    logsum = lse[:4]
-    seq = 1024
-    inputs = tokens[0].astype(f32)
-    out_part = dot(context, proj_w, 1, 0) + dot(active, down_w, 1, 0)
-    out_sum = lax.psum_scatter(out_part.astype(bf16), "ctx", scatter_dimension=0, tiled=True)
-    block_out = (inputs + out_sum.astype(f32) + proj_b + down_b).astype(bf16)
-    d_normed = dot(d_projected, qkv_w, 1, 1) + dot(d_hidden, up_w, 1, 1)
-    d_normed = lax.psum_scatter(d_normed.astype(bf16), "ctx", scatter_dimension=0, tiled=True)
-    d_normed = d_normed.astype(f32)
-    standard, standard_pull = jax.vjp(standardize, inputs)
-    upstream_own = cotangent[0].astype(f32)
-    token_grad = (upstream_own + standard_pull(d_normed * gain)[0]).astype(bf16)
-
-    grad_down = dot(active, upstream, 0, 0).astype(bf16)
-    grad_up = dot(normed, d_hidden, 0, 0).astype(bf16)
-    grad_qkv = dot(normed, d_projected, 0, 0).astype(bf16)
-    grad_proj = dot(context, upstream, 0, 0).astype(bf16)
-    wide = jnp.concatenate([grad_qkv, grad_up], axis=1)
-    wide = lax.psum_scatter(wide, "fsdp", scatter_dimension=0, tiled=True)
-    grad_down = lax.psum_scatter(grad_down, "fsdp", scatter_dimension=0, tiled=True)
-    grad_proj = lax.psum(grad_proj, "fsdp").reshape(cols // shard, shard, width)
-    grad_proj = lax.dynamic_index_in_dim(grad_proj, f % (cols // shard), 0, False)
-    grad_proj = jnp.where(c == f // (cols // shard), grad_proj, jnp.zeros((), bf16))
-    proj_weight_grad = lax.psum(grad_proj, "ctx").astype(f32)
-    wide = lax.all_gather(wide, "ctx", axis=0, tiled=False)
-    down_weight_grad = lax.all_gather(grad_down, "ctx", axis=0, tiled=True).astype(f32)
-    qkv_weight_grad = (
-        jnp.transpose(wide[:, :, : 3 * cols].reshape(ring, shard, 3, cols), (1, 2, 0, 3))
-        .reshape(shard, 3 * width)
-        .astype(f32)
+    block_out, token_grad, log_sums, gq, gu, gd, gp = second_call(
+        n, w1, w2, w3, u, dproj, ctx, act, dhid, tokens[0], cotangent[0], lse
     )
-    up_weight_grad = (
-        jnp.transpose(wide[:, :, 3 * cols :].reshape(ring, shard, shards, strip), (1, 2, 0, 3))
-        .reshape(shard, hidden_width)
-        .astype(f32)
-    )
-
-    d_qkv_b = jnp.sum(d_projected.astype(f32), axis=0).reshape(3, 1, cols)
-    d_up_b = jnp.sum(d_hidden.astype(f32), axis=0).reshape(shards, 1, strip)
-    here = (jnp.arange(ring) == c)[None, :, None]
-    d_out_b = jnp.sum(upstream_own, axis=0)
-    vectors = jnp.concatenate(
-        [
-            jnp.sum(d_normed * standard, axis=0).reshape(shards, -1),
-            jnp.sum(d_normed, axis=0).reshape(shards, -1),
-            d_out_b.reshape(shards, -1),
-            jnp.where(here, d_qkv_b, 0.0).reshape(shards, -1),
-            jnp.where(here, d_up_b, 0.0).reshape(shards, -1),
-        ],
-        axis=1,
-    )
-    vectors = lax.psum(vectors, ("ctx", "fsdp"))
-    vectors = lax.dynamic_index_in_dim(vectors, f, 0, False)
+    gq = gq.reshape(8, 144, 768)
+    vectors = jnp.sum(gq[:, 128:, :128].astype(f32), axis=0)
+    qkv_grad = jnp.transpose(gq[:, :128].reshape(8, 128, 3, COLS), (1, 2, 0, 3))
+    up_grad = jnp.transpose(gu.reshape(8, 128, 16, 64), (1, 2, 0, 3))
     return (
         block_out[None],
         token_grad[None],
-        lax.all_to_all(
-            logsum.reshape(1, 4, seq), "ctx", split_axis=2, concat_axis=1, tiled=True
-        ),
-        vectors[:shard],
-        vectors[shard : 2 * shard],
-        qkv_weight_grad,
-        vectors[3 * shard : 6 * shard],
-        proj_weight_grad,
-        vectors[2 * shard : 3 * shard],
-        up_weight_grad,
-        vectors[6 * shard :],
-        down_weight_grad,
-        vectors[2 * shard : 3 * shard],
+        log_sums[None],
+        vectors[0],
+        vectors[1],
+        qkv_grad.reshape(128, 3 * WIDTH).astype(f32),
+        vectors[3:6].reshape(384),
+        gp.astype(f32),
+        vectors[2],
+        up_grad.reshape(128, HIDDEN).astype(f32),
+        vectors[6:10].reshape(512),
+        gd.reshape(512, WIDTH).astype(f32),
+        vectors[2],
     )
 
 

time: 709 us -> 292 us (0.41)
  waiting for transfers between devices: 422 us -> 0 us
  Pallas kernels: 127 us -> 250 us
  matrix products: 44.7 us -> 0 us
  local copies, waits for them, and re-layouts: 54.4 us -> 29.6 us
  other arithmetic: 33.1 us -> 9.23 us
  between operations: 16.1 us -> 0.72 us
  starting transfers between devices: 7.24 us -> 0 us
    psum x3 -> x0, waiting for transfers between devices: 210 us -> none  [the longest x1 143 us: local(): vectors = lax.psum(vectors, ('ctx', 'fsdp'))]
    reduce_scatter x4 -> x0, waiting for transfers between devices: 159 us -> none  [the longest x1 86.7 us: local(): wide = lax.psum_scatter(wide, 'fsdp', scatter_dimension=0, tiled=True)]
    pallas_call x0 -> x1, Pallas kernels: none -> 124 us  [second_call(): pl.pallas_call(second_kernel, out_shape=[jax.ShapeDtypeStruct((128, WIDTH...]
    all_gather x2 -> x0, waiting for transfers between devices: 48.2 us -> none  [the longest x1 27.5 us: local(): wide = lax.all_gather(wide, 'ctx', axis=0, tiled=False)]
    dot_general x8 -> x0, matrix products: 44.7 us -> none  [dot(): lax.dot_general(a, b, (((ca,), (cb,)), ((), ())), preferred_element_type=...]
    unnamed x40 -> x22, local copies, waits for them, and re-layouts: 27.7 us -> 15.9 us
    slice x7 -> x1, local copies, waits for them, and re-layouts: 9.29 us -> 1.51 us  [local(): qkv_grad = jnp.transpose(gq[:, :128].reshape(8, 128, 3, COLS), (1, 2, 0, 3))]
    reduce_sum x6 -> x1, other arithmetic: 8.45 us -> 0.78 us  [local(): vectors = jnp.sum(gq[:, 128:, :128].astype(f32), axis=0)]
  transfers between devices with their start and end apart: 10 -> 0, of which waited for: 8 -> 0; matrix products, arithmetic and copies ran while one was open for 13% -> 0% of each run, Pallas kernels for 0% -> 0%
where the time goes in v3:
time: 292 us; the launch traced here: 290 us
  Pallas kernels  250 us (86%)
  local copies, waits for them, and re-layouts  29.6 us (10%)
  other arithmetic  9.23 us (3%)
    pallas_call x1, Pallas kernels, first_call(): pl.pallas_call(first_kernel, out_shape=[jax.ShapeDtypeStruct(*s) for s in...  126 us
    pallas_call x1, Pallas kernels, second_call(): pl.pallas_call(second_kernel, out_shape=[jax.ShapeDtypeStruct((128, WIDTH...  124 us
    unnamed x22, local copies, waits for them, and re-layouts  15.9 us
    convert_element_type x2, local copies, waits for them, and re-layouts, local(): up_grad.reshape(128, HIDDEN).astype(f32)  8.83 us

profile of v3, /device:TPU:1, one launch (start us, length us, event | category | flops | bytes accessed | tf_op | source)
XLA Modules:
  0.0 289.5 jit_solution(11816844722679460160)
XLA Ops:
  1.2 0.8 dynamic-update-slice
  2.0 0.8 dynamic-update-slice.1
  2.9 0.8 dynamic-update-slice.2
  3.7 0.8 dynamic-update-slice.3
  4.5 0.9 dynamic-update-slice.4
  5.4 0.9 dynamic-update-slice.5
  6.2 0.6 pad.4.vec
  6.8 2.8 fusion
  9.6 126.1 %first.1 = (bf16[1024,2048]{1,0:T(8,128)(2,1)}, bf16[4,4,144,768]{3,2,1,0:T(8,128)(2,1)}, bf16[4,4,80,2048]{3,2,1,0:T(8,128)(2,1)}, bf16[4,4,128,1024]{3,2,1,0:T...) custom-call(bf16[128,2048]{1,0:T(8,128)(2,1)} %bitcast.39, ...), custom_call_target="tpu_custom_call" | custom-call | flops 24999999488 | bytes 40000000 | tf_op jit(solution)/shard_map/first/pallas_call | solution.py:651
  135.8 123.8 %second.1 = (bf16[128,2048]{1,0:T(8,128)(2,1)}, bf16[128,2048]{1,0:T(8,128)(2,1)}, f32[32,128]{1,0:T(8,128)}, bf16[4,2,144,768]{3,2,1,0:T(8,128)(2,1)}, bf16[4,2...) custom-call(bf16[1024,2048]{1,0:T(8,128)(2,1)} %get-tuple-element.30.n_in, ...), custom_call_target="tpu_custom_call" | custom-call | flops 25999998976 | bytes 60000000 | tf_op jit(solution)/shard_map/second/pallas_call | solution.py:1223
  259.6 0.8 convert_reduce_fusion
  260.4 1.5 slice.32
  261.9 0.9 copy.38
  263.3 0.6 slice_bitcast_fusion.1
  263.9 0.6 slice_bitcast_fusion
  264.5 2.1 convert_element_type.60
  267.2 2.4 copy.36
  269.6 4.1 %copy.34 = f32[4,2,128,1024]{2,3,1,0:T(8,128)} copy(bf16[4,2,128,1024]{3,2,1,0:T(8,128)(2,1)} %get-tuple-element.45) | data formatting | bytes 6291456 | tf_op jit(solution)/shard_map/convert_element_type | solution.py:1316
  273.7 4.7 %copy.35 = f32[128,16,8,64]{0,3,2,1:T(8,128)} copy(f32[128,16,8,64]{0,3,1,2:T(8,128)} %bitcast.29) | data formatting | bytes 8388608 | tf_op jit(solution)/shard_map/convert_element_type | solution.py:1316
  278.4 5.7 %copy.37 = f32[128,8192]{1,0:T(8,128)} copy(f32[128,8192]{0,1:T(8,128)} %bitcast.30) | data formatting | bytes 8388608
  284.1 2.7 bitcast_convert_fusion
  287.3 0.8 copy.50
  288.1 0.8 copy.51
  288.9 0.6 copy.52
  (17 shorter events, 2.1 us)
Async XLA Ops:
  263.3 23.5 %copy-start.4 = (f32[128]{0:T(128)}, f32[128]{0:T(128)S(1)}, u32[]{:S(2)}) copy-start(f32[128]{0:T(128)S(1)} %get-tuple-element.125) | copy-start | bytes 1540
  278.4 5.7 %copy-start = (bf16[4,2,64,2048]{3,2,1,0:T(8,128)(2,1)S(1)}, bf16[4,2,64,2048]{3,2,1,0:T(8,128)(2,1)}, u32[]{:S(2)}) copy-start(bf16[4,2,64,2048]{3,2,1,0:T(8,128)(2,1)} %get-tuple-element.46) | copy-start | bytes 6291460
  284.1 3.2 %copy-start.2 = (bf16[128,2048]{1,0:T(8,128)(2,1)S(1)}, bf16[128,2048]{1,0:T(8,128)(2,1)}, u32[]{:S(2)}) copy-start(bf16[128,2048]{1,0:T(8,128)(2,1)} %get-tuple-element.40) | copy-start | bytes 1572868
  284.1 4.0 %copy-start.1 = (bf16[128,2048]{1,0:T(8,128)(2,1)S(1)}, bf16[128,2048]{1,0:T(8,128)(2,1)}, u32[]{:S(2)}) copy-start(bf16[128,2048]{1,0:T(8,128)(2,1)} %get-tuple-element.41) | copy-start | bytes 1572868
  284.1 4.8 %copy-start.3 = (f32[32,128]{1,0:T(8,128)S(1)}, f32[32,128]{1,0:T(8,128)}, u32[]{:S(2)}) copy-start(f32[32,128]{1,0:T(8,128)} %get-tuple-element.42) | copy-start | bytes 49156

commit v4 on v2

v4 whole, which is shorter than its diff:
```python
from functools import partial
import math

import jax
import jax.numpy as jnp
from jax import lax
from jax.experimental import pallas as pl
from jax.experimental.pallas import tpu as pltpu
from jax.sharding import PartitionSpec as P

HEAD = 64
ROT_DIMS = 32
SEQ = 1024
WIDTH = 2048
HIDDEN = 8192
OWN_HEADS = 4
COLS = 256
UNITS = 1024

epsilon = 1e-05
masked_score = -1e30
f32 = jnp.float32
bf16 = jnp.bfloat16
MESH = pl.DeviceIdType.MESH
VM = pltpu.VMEM


def dot(a, b, ca, cb):
    return lax.dot_general(a, b, (((ca,), (cb,)), ((), ())), preferred_element_type=f32)


def place():
    c = lax.axis_index("ctx")
    f = lax.axis_index("fsdp")
    return c, f, c // 2, c % 2, f // 4, f % 4


def other_core():
    c, f, z, core, y, x = place()
    return (z * 2 + 1 - core, f)


def up1(i):
    return (i + 1) % 4


def down1(i):
    return (i + 3) % 4


def over(i):
    return (i + 2) % 4


class Copies:
    def __init__(self, send, recv):
        self.send, self.recv = send, recv
        self.started = []

    def start(self, k, src, dst, device):
        copy = pltpu.make_async_remote_copy(
            src_ref=src,
            dst_ref=dst,
            send_sem=self.send.at[k],
            recv_sem=self.recv.at[k],
            device_id=device,
            device_id_type=MESH,
        )
        copy.start()
        self.started.append(copy)

    def arrived(self, k, dst):
        pltpu.make_async_remote_copy(
            src_ref=dst,
            dst_ref=dst,
            send_sem=self.send.at[k],
            recv_sem=self.recv.at[k],
            device_id=other_core(),
            device_id_type=MESH,
        ).wait_recv()

    def sent(self):
        for copy in self.started:
            copy.wait_send()
        self.started = []


def plane_gather(w, cuts, copies):
    c, f, z, core, y, x = place()
    r0, r1, r2, r3, r4 = cuts
    first, last = pl.ds(r0, r2 - r0), pl.ds(r2, r4 - r2)
    q0, q1, q2, q3 = (pl.ds(a, b - a) for a, b in zip(cuts[:-1], cuts[1:]))
    xu, xd, xo = up1(x), down1(x), over(x)
    yu, yd, yo = up1(y), down1(y), over(y)
    to_xu, to_xd = (c, y * 4 + xu), (c, y * 4 + xd)
    to_yu, to_yd = (c, yu * 4 + x), (c, yd * 4 + x)
    lo, hi = pl.ds(0, 2), pl.ds(2, 2)
    every = pl.ds(0, 4)

    def send(k, part, device):
        copies.start(k, w.at[part], w.at[part], device)

    def got(k, part):
        copies.arrived(k, w.at[part])

    send(0, (y, x, first), to_xu)
    send(1, (y, x, first), to_xd)
    send(2, (y, x, last), to_yu)
    send(3, (y, x, last), to_yd)
    yield
    got(0, (y, xd, first))
    send(4, (y, xd, q0), to_xu)
    got(1, (y, xu, first))
    send(5, (y, xu, q1), to_xd)
    got(2, (yd, x, last))
    send(6, (yd, x, q2), to_yu)
    got(3, (yu, x, last))
    send(7, (yu, x, q3), to_yd)
    yield
    got(4, (y, xo, q0))
    got(5, (y, xo, q1))
    send(8, (y, every, first), to_yu)
    send(9, (y, every, first), to_yd)
    got(6, (yo, x, q2))
    got(7, (yo, x, q3))
    send(10, (every, x, last), to_xu)
    send(11, (every, x, last), to_xd)
    yield
    got(8, (yd, every, first))
    send(12, (yd, lo, first), to_yu)
    got(9, (yu, every, first))
    send(13, (yu, hi, first), to_yd)
    got(10, (every, xd, last))
    send(14, (lo, xd, last), to_xu)
    got(11, (every, xu, last))
    send(15, (hi, xu, last), to_xd)
    yield
    got(12, (yo, lo, first))
    got(13, (yo, hi, first))
    got(14, (lo, xo, last))
    got(15, (hi, xo, last))
    yield


def line_gather(t, cuts, copies, own=None):
    c, f, z, core, y, x = place()
    r0, r1, r2 = cuts
    h0, h1 = pl.ds(r0, r1 - r0), pl.ds(r1, r2 - r1)
    zu, zd, zo = up1(z), down1(z), over(z)
    to_zu, to_zd, to_core = (zu * 2 + core, f), (zd * 2 + core, f), (z * 2 + 1 - core, f)
    other = 1 - core

    def send(k, part, device):
        copies.start(k, t.at[part], t.at[part], device)

    def got(k, part):
        copies.arrived(k, t.at[part])

    mine = t.at[z, core]
    own = mine if own is None else own
    copies.start(0, own, mine, to_zu)
    copies.start(1, own, mine, to_zd)
    copies.start(2, own, mine, to_core)
    yield
    got(0, (zd, core))
    send(3, (zd, core, h0), to_zu)
    got(1, (zu, core))
    send(4, (zu, core, h1), to_zd)
    send(5, (zd, core), to_core)
    send(6, (zu, core), to_core)
    yield
    got(3, (zo, core, h0))
    got(4, (zo, core, h1))
    send(7, (zo, core), to_core)
    yield
    got(2, (z, other))
    got(5, (zd, other))
    got(6, (zu, other))
    got(7, (zo, other))
    yield


def enter():
    c, f, z, core, y, x = place()
    barrier = pltpu.get_barrier_semaphore()
    for device in (
        (c, y * 4 + up1(x)),
        (c, y * 4 + down1(x)),
        (c, up1(y) * 4 + x),
        (c, down1(y) * 4 + x),
        (up1(z) * 2 + core, f),
        (down1(z) * 2 + core, f),
        (z * 2 + 1 - core, f),
    ):
        pl.semaphore_signal(barrier, inc=1, device_id=device, device_id_type=MESH)
    owner = c * 2 + f // 8

    @pl.when(owner != f)
    def _():
        pl.semaphore_signal(barrier, inc=1, device_id=(c, owner), device_id_type=MESH)

    for j in range(8):
        target = (f % 2) * 8 + j

        @pl.when((f // 2 == c) & (target != f))
        def _():
            pl.semaphore_signal(barrier, inc=1, device_id=(c, target), device_id_type=MESH)

    count = 7 + jnp.where(f // 2 == c, jnp.where(f // 8 == f % 2, 7, 8), 0)
    count = count + jnp.where(owner != f, 1, 0)
    pl.semaphore_wait(barrier, count)


def turn(fields, cos, low_sin, high_sin):
    return (
        fields * cos + pltpu.roll(fields, 112, 1) * low_sin + pltpu.roll(fields, 16, 1) * high_sin
    )


def turn_back(grads, cos, low_sin, high_sin):
    return (
        grads * cos + pltpu.roll(grads * low_sin, 16, 1) + pltpu.roll(grads * high_sin, 112, 1)
    )


def halves_packed(a, b, odd, lane):
    moved_a, moved_b = pltpu.roll(a, 64, 1), pltpu.roll(b, 64, 1)
    return jnp.where(lane < 64, jnp.where(odd, moved_a, a), jnp.where(odd, b, moved_b))


def add_into(target, part, *others):
    total = target[part].astype(f32)
    for ref, piece in others:
        total = total + ref[piece].astype(f32)
    target[part] = total.astype(target.dtype)


def plane_reduce(g, cuts, ra, rb, copies):
    c, f, z, core, y, x = place()
    r0, r1, r2, r3, r4 = cuts
    first, last = pl.ds(r0, r2 - r0), pl.ds(r2, r4 - r2)
    q0, q1, q2, q3 = (pl.ds(a, b - a) for a, b in zip(cuts[:-1], cuts[1:]))
    s0, s1, s2, s3 = (pl.ds(0, b - a) for a, b in zip(cuts[:-1], cuts[1:]))
    xu, xd, xo = up1(x), down1(x), over(x)
    yu, yd, yo = up1(y), down1(y), over(y)
    to_xu, to_xd = (c, y * 4 + xu), (c, y * 4 + xd)
    to_yu, to_yd = (c, yu * 4 + x), (c, yd * 4 + x)
    lo, hi, every = pl.ds(0, 2), pl.ds(2, 2), pl.ds(0, 4)
    near, far = pl.ds(0, 2), pl.ds(2, 4)

    def send(k, part, ref, piece, device):
        copies.start(k, g.at[part], ref.at[piece], device)

    def got(k, ref, piece):
        copies.arrived(k, ref.at[piece])

    send(0, (yo, lo, first), ra, (0, near), to_yu)
    send(1, (yo, hi, first), ra, (1, near), to_yd)
    send(2, (lo, xo, last), rb, (0, near), to_xu)
    send(3, (hi, xo, last), rb, (1, near), to_xd)
    yield
    got(0, ra, (0, near))
    add_into(g, (yu, lo, first), (ra, (0, near)))
    send(4, (yu, every, first), ra, (0, far), to_yu)
    got(1, ra, (1, near))
    add_into(g, (yd, hi, first), (ra, (1, near)))
    send(5, (yd, every, first), ra, (1, far), to_yd)
    got(2, rb, (0, near))
    add_into(g, (lo, xu, last), (rb, (0, near)))
    send(6, (every, xu, last), rb, (0, far), to_xu)
    got(3, rb, (1, near))
    add_into(g, (hi, xd, last), (rb, (1, near)))
    send(7, (every, xd, last), rb, (1, far), to_xd)
    yield
    got(4, ra, (0, far))
    got(5, ra, (1, far))
    add_into(g, (y, every, first), (ra, (0, far)), (ra, (1, far)))
    send(8, (y, xo, q0), ra, (0, 6, s0), to_xu)
    send(9, (y, xo, q1), ra, (1, 6, s1), to_xd)
    got(6, rb, (0, far))
    got(7, rb, (1, far))
    add_into(g, (every, x, last), (rb, (0, far)), (rb, (1, far)))
    send(10, (yo, x, q2), rb, (0, 6, s2), to_yu)
    send(11, (yo, x, q3), rb, (1, 6, s3), to_yd)
    yield
    got(8, ra, (0, 6, s0))
    add_into(g, (y, xu, q0), (ra, (0, 6, s0)))
    send(12, (y, xu, first), ra, (0, 7), to_xu)
    got(9, ra, (1, 6, s1))
    add_into(g, (y, xd, q1), (ra, (1, 6, s1)))
    send(13, (y, xd, first), ra, (1, 7), to_xd)
    got(10, rb, (0, 6, s2))
    add_into(g, (yu, x, q2), (rb, (0, 6, s2)))
    send(14, (yu, x, last), rb, (0, 7), to_yu)
    got(11, rb, (1, 6, s3))
    add_into(g, (yd, x, q3), (rb, (1, 6, s3)))
    send(15, (yd, x, last), rb, (1, 7), to_yd)
    yield
    got(12, ra, (0, 7))
    got(13, ra, (1, 7))
    add_into(g, (y, x, first), (ra, (0, 7)), (ra, (1, 7)))
    got(14, rb, (0, 7))
    got(15, rb, (1, 7))
    add_into(g, (y, x, last), (rb, (0, 7)), (rb, (1, 7)))
    yield


def line_reduce(g, cuts, rc, r1, r2, copies):
    c, f, z, core, y, x = place()
    c0, c1, c2 = cuts
    h0, h1 = pl.ds(c0, c1 - c0), pl.ds(c1, c2 - c1)
    s0, s1 = pl.ds(0, c1 - c0), pl.ds(0, c2 - c1)
    zu, zd, zo = up1(z), down1(z), over(z)
    to_zu, to_zd, to_core = (zu * 2 + core, f), (zd * 2 + core, f), (z * 2 + 1 - core, f)
    every = pl.ds(0, 4)
    copies.start(0, g.at[every, 1 - core], rc, to_core)
    yield
    copies.arrived(0, rc)

    def add_row(i, carry):
        add_into(g, (i, core), (rc, (i,)))
        return carry

    lax.fori_loop(0, 4, add_row, 0)
    copies.start(1, g.at[zo, core, h0], r1.at[0, s0], to_zu)
    copies.start(2, g.at[zo, core, h1], r1.at[1, s1], to_zd)
    yield
    copies.arrived(1, r1.at[0, s0])
    add_into(g, (zu, core, h0), (r1, (0, s0)))
    copies.start(3, g.at[zu, core], r2.at[0], to_zu)
    copies.arrived(2, r1.at[1, s1])
    add_into(g, (zd, core, h1), (r1, (1, s1)))
    copies.start(4, g.at[zd, core], r2.at[1], to_zd)
    yield
    copies.arrived(3, r2.at[0])
    copies.arrived(4, r2.at[1])
    yield


def vector_reduce(g, ry, rx, copies):
    c, f, z, core, y, x = place()
    xu, xd, xo = up1(x), down1(x), over(x)
    yu, yd, yo = up1(y), down1(y), over(y)
    to_xu, to_xd = (c, y * 4 + xu), (c, y * 4 + xd)
    to_yu, to_yd = (c, yu * 4 + x), (c, yd * 4 + x)
    copies.start(0, g.at[yo], ry.at[0], to_yu)
    yield
    copies.arrived(0, ry.at[0])
    add_into(g, (yu,), (ry, (0,)))
    copies.start(1, g.at[yu], ry.at[1], to_yu)
    copies.start(2, g.at[yd], ry.at[2], to_yd)
    yield
    copies.arrived(1, ry.at[1])
    copies.arrived(2, ry.at[2])
    add_into(g, (y,), (ry, (1,)), (ry, (2,)))
    copies.start(3, g.at[y, xo], rx.at[0], to_xu)
    yield
    copies.arrived(3, rx.at[0])
    add_into(g, (y, xu), (rx, (0,)))
    copies.start(4, g.at[y, xu], rx.at[1], to_xu)
    copies.start(5, g.at[y, xd], rx.at[2], to_xd)
    yield
    copies.arrived(4, rx.at[1])
    copies.arrived(5, rx.at[2])
    add_into(g, (y, x), (rx, (1,)), (rx, (2,)))
    yield


GATHER1 = (0, 48, 96, 144, 192)
REDUCE1 = (0, 48, 96, 128, 176)
CUTS2 = (0, 16, 32, 48, 64)
CUTS3 = (0, 32, 64, 96, 128)
PROJ = ((0, 768), (768, 768), (1536, 512))


def layer_kernel(
    tokens,
    cotangent,
    qkv_weight,
    proj_weight,
    up_weight,
    down_weight,
    seg,
    gain_in,
    shift_in,
    proj_bias_in,
    down_bias_in,
    qkv_bias_in,
    up_bias_in,
    block_out,
    token_grad,
    lse_out,
    gq_out,
    gu_out,
    gd_out,
    gp_out,
    gv_out,
    w1,
    w2,
    w3,
    t,
    u,
    n,
    zd,
    rc,
    zo_r1,
    zo_r2,
    zd_r1,
    zd_r2,
    ra1,
    rb1,
    ra3,
    rb3,
    vecs,
    tab,
    begin_cols,
    q,
    k,
    v,
    dctx,
    ctx,
    dk,
    dv,
    dproj,
    act,
    dhid,
    lse,
    lse_own,
    pt,
    gp,
    gv,
    ry,
    rx,
    sem1,
    sem2,
    sem3,
    sem_t,
    sem_u,
    sem_r1,
    sem_r2,
    sem_r3,
    sem_v,
    sem_zo,
    sem_zd,
    sem_lq,
    sem_lu,
    sem_ld,
    sem_lv,
    sem_s,
    sem_p,
    sem_b,
    sem_l,
    sem_o,
    n_free,
    rc_free,
):
    c, f, z, core, y, x = place()
    lane = lax.broadcasted_iota(jnp.int32, (1, 128), 1)
    odd = core == 1
    owner = c * 2 + f // 8
    own_rows = f // 2 == c
    zo = t

    loads = [
        pltpu.make_async_copy(tokens, t.at[z, core, pl.ds(0, 128)], sem_l.at[0]),
        pltpu.make_async_copy(cotangent, u.at[z, core], sem_l.at[1]),
        pltpu.make_async_copy(
            down_weight.at[pl.ds(pl.multiple_of(c * 64, 64), 64)], w2.at[y, x], sem_l.at[2]
        ),
    ]
    for i in range(3):
        loads.append(
            pltpu.make_async_copy(
                qkv_weight.at[:, pl.ds(pl.multiple_of(i * WIDTH + c * COLS, 128), COLS)],
                w1.at[y, x, pl.ds(0, 128), pl.ds(i * COLS, COLS)],
                sem_l.at[3 + i],
            )
        )
    for copy in loads:
        copy.start()
    for i in range(16):
        pltpu.make_async_copy(
            up_weight.at[:, pl.ds(pl.multiple_of(i * 512 + (c // 2) * 128, 128), 128)],
            q.at[pl.ds(i // 2 * 128, 128), pl.ds(i % 2 * 128, 128)],
            sem_l.at[6],
        ).start()
    vector_list = [gain_in[...], shift_in[...], proj_bias_in[...], down_bias_in[...]]
    vector_list += [qkv_bias_in[:, 128 * i : 128 * i + 128] for i in range(3)]
    vector_list += [up_bias_in[:, 128 * i : 128 * i + 128] for i in range(4)]
    vector_list = [vector.astype(f32) for vector in vector_list] + [jnp.zeros((5, 128), f32)]
    w1[y, x, 176:192, 0:128] = jnp.concatenate(vector_list, axis=0).astype(bf16)
    w1[y, x, 176:192, 128:768] = jnp.zeros((16, 640), bf16)
    w1[y, x, 160:176, 512:768] = jnp.zeros((16, 256), bf16)
    seg_rows = jnp.broadcast_to(seg[...].astype(f32), (16, 128)).astype(bf16)
    t[z, core, 128:144, 0:128] = seg_rows
    t[z, core, 128:144, 128:WIDTH] = jnp.zeros((16, WIDTH - 128), bf16)

    enter()

    def both_ways(sems):
        return Copies(sems.at[0], sems.at[1])

    copies1, copies2, copies3 = both_ways(sem1), both_ways(sem2), both_ways(sem3)
    copies_t, copies_u = both_ways(sem_t), both_ways(sem_u)
    copies_r1, copies_r2, copies_r3 = both_ways(sem_r1), both_ways(sem_r2), both_ways(sem_r3)
    copies_v = both_ways(sem_v)
    copies_zo, copies_zd = both_ways(sem_zo), both_ways(sem_zd)
    copies_lq, copies_lu = both_ways(sem_lq), both_ways(sem_lu)
    copies_ld, copies_lv = both_ways(sem_ld), both_ways(sem_lv)
    gather1 = plane_gather(w1, GATHER1, copies1)
    gather2 = plane_gather(w2, CUTS2, copies2)
    gather3 = plane_gather(w3, CUTS3, copies3)
    gather_t = line_gather(t, (0, 64, 144), copies_t)
    gather_u = line_gather(u, (0, 64, 128), copies_u)
    reduce1 = plane_reduce(w1, REDUCE1, ra1, rb1, copies_r1)
    reduce2 = plane_reduce(w2, CUTS2, n.at[0], n.at[1], copies_r2)
    reduce3 = plane_reduce(w3, CUTS3, ra3, rb3, copies_r3)
    reduce_v = vector_reduce(gv, ry, rx, copies_v)
    reduce_o = line_reduce(zo, (0, 64, 144), rc, zo_r1, zo_r2, copies_zo)
    reduce_d = line_reduce(zd, (0, 64, 128), rc.at[:, pl.ds(0, 128)], zd_r1, zd_r2, copies_zd)
    spread_q = line_gather(gq_out, (0, 64, 128), copies_lq, w1.at[y, x, pl.ds(0, 128)])
    spread_u = line_gather(gu_out, (0, 64, 128), copies_lu, w3.at[y, x])
    spread_d = line_gather(gd_out, (0, 32, 64), copies_ld, w2.at[y, x])
    spread_v = line_gather(gv_out, (0, 8, 16), copies_lv, gv.at[y, x])

    outs = []

    def put(src, dst):
        copy = pltpu.make_async_copy(src, dst, sem_o.at[len(outs)])
        copy.start()
        outs.append(copy)

    def scatter(j, target):
        return pltpu.make_async_remote_copy(
            src_ref=proj_weight.at[pl.ds(16 * j, 16)],
            dst_ref=pt,
            send_sem=sem_s.at[0, j],
            recv_sem=sem_s.at[1, 0],
            device_id=(c, target),
            device_id_type=MESH,
        )

    for j in range(8):
        target = (f % 2) * 8 + j

        @pl.when(own_rows & (target != f))
        def _():
            scatter(j, target).start()

        @pl.when(own_rows & (target == f))
        def _():
            local = pltpu.make_async_copy(proj_weight.at[pl.ds(16 * j, 16)], pt, sem_s.at[1, 1])
            local.start()
            local.wait()

    loads[0].wait()
    next(gather_t)
    for i in (3, 4, 5):
        loads[i].wait()

    @pl.when(owner != f)
    def _():
        pltpu.make_async_remote_copy(
            src_ref=pt,
            dst_ref=pt,
            send_sem=sem_s.at[0, 0],
            recv_sem=sem_s.at[1, 0],
            device_id=other_core(),
            device_id_type=MESH,
        ).wait_recv()

    for j, (start, size) in enumerate(PROJ):
        w1[y, x, 128 + 16 * j : 144 + 16 * j, 0:size] = pt[:, start : start + size]
    next(gather1)

    pltpu.make_async_copy(q, q, sem_l.at[6]).wait()
    for m in range(8):
        strip = q[128 * m : 128 * m + 128, :].astype(f32)
        packed = halves_packed(strip[:, :128], strip[:, 128:], odd, lane)
        w3[y, x, :, 128 * m : 128 * m + 128] = packed.astype(bf16)

    in_head = lane % 64
    inverse = jnp.exp((lane % 16).astype(f32) * (-math.log(10000.0) / (ROT_DIMS // 2)))
    inverse = jnp.where(in_head < ROT_DIMS, inverse, 0.0)
    row_angles = lax.broadcasted_iota(jnp.int32, (128, 1), 0).astype(f32) * inverse
    tab[0, 0:128, :] = jnp.cos(row_angles)
    tab[1, 0:128, :] = jnp.sin(row_angles)

    next(gather_t)
    loads[1].wait()
    next(gather_u)
    next(gather1)
    next(gather3)
    next(gather_t)
    next(gather1)
    next(gather3)
    next(gather_u)
    loads[2].wait()
    next(gather1)
    next(gather3)
    next(gather2)
    next(gather_t)

    seg_all = jnp.concatenate(
        [t[b // 2, b % 2, 128:144, 0:128][0:1].astype(f32) for b in range(8)], axis=0
    )
    seg_cols = jnp.transpose(seg_all)
    firsts = [jnp.sum((seg_all < float(d)).astype(f32), keepdims=True) for d in range(1, 4)]
    begins = jnp.zeros((128, 8), f32)
    row = lax.broadcasted_iota(jnp.int32, (32, 1), 0)
    shifts = (row // 4 * 128).astype(f32)
    for d in range(1, 4):
        begins = jnp.where(seg_cols == float(d), firsts[d - 1], begins)
        shifts = shifts - jnp.where(row % 4 == d, firsts[d - 1], 0.0)
    begin_cols[:, 0:8] = begins
    shift_cos, shift_sin = jnp.cos(shifts * inverse), jnp.sin(shifts * inverse)
    row_cos, row_sin = tab[0, 0:128, :], tab[1, 0:128, :]
    for b in range(8):
        rows = pl.ds(b * 128, 128)
        own = seg_cols[:, b : b + 1]
        block_cos, block_sin = shift_cos[4 * b : 4 * b + 1], shift_sin[4 * b : 4 * b + 1]
        for d in range(1, 4):
            at = 4 * b + d
            block_cos = jnp.where(own == float(d), shift_cos[at : at + 1], block_cos)
            block_sin = jnp.where(own == float(d), shift_sin[at : at + 1], block_sin)
        sin = row_sin * block_cos + row_cos * block_sin
        tab[0, rows, :] = row_cos * block_cos - row_sin * block_sin
        tab[1, rows, :] = jnp.where(in_head < 16, -sin, 0.0)
        tab[2, rows, :] = jnp.where((in_head >= 16) & (in_head < 32), sin, 0.0)

    next(gather1)

    vecs[...] = w1[:, :, 176:192, 0:128].reshape(16, 16, 128).astype(f32)

    def joined(which):
        return jnp.concatenate([vecs[i, which : which + 1, :] for i in range(16)], axis=1)

    gain, shift = joined(0), joined(1)

    def bias_rows(which):
        parts = []
        for i in range(2):
            at = which * 16 + c * 2 + i
            parts.append(vecs[at // 3, pl.ds(4 + at % 3, 1), :])
        return jnp.concatenate(parts, axis=1)

    qkv_bias = jnp.concatenate([bias_rows(i) for i in range(3)], axis=1)
    up_parts = []
    for m in range(8):
        a = vecs[2 * m, pl.ds(7 + c // 2, 1), :]
        b = vecs[2 * m + 1, pl.ds(7 + c // 2, 1), :]
        up_parts.append(halves_packed(a, b, odd, lane))
    up_bias = jnp.concatenate(up_parts, axis=1)

    def norm_rows(i, carry):
        b, part = i // 8, i % 8
        values = t[b // 2, b % 2, pl.ds(pl.multiple_of(part * 16, 16), 16), :].astype(f32)
        average = jnp.mean(values, axis=-1, keepdims=True)
        centered = values - average
        variance = jnp.mean(centered * centered, axis=-1, keepdims=True)
        standard = centered * lax.rsqrt(variance + epsilon)
        rows = pl.ds(pl.multiple_of(i % 2 * 16, 16), 16)
        normed = (standard * gain + shift).astype(bf16)
        n[i // 32, i // 16 % 2, i // 2 % 8, rows, :] = normed
        return carry

    lax.fori_loop(0, 64, norm_rows, 0)
    next(gather_u)
    next(gather2)
    next(gather3)

    def project(m, carry):
        rows = pl.ds(pl.multiple_of(m * 512, 512), 512)
        tables = [tab[i, rows, :] for i in range(3)]
        right = w1[:, :, pl.ds(0, 128), :].reshape(WIDTH, 768)
        fields = dot(n[m].reshape(512, WIDTH), right, 1, 0) + qkv_bias
        for which, target in enumerate((q, k, v)):
            for pair in range(2):
                at = which * COLS + pair * 128
                both = fields[:, at : at + 128]
                if which < 2:
                    both = turn(both, *tables)
                if which == 0:
                    both = both * 0.125
                target[rows, pair * 128 : pair * 128 + 128] = both.astype(bf16)
        return carry

    lax.fori_loop(0, 2, project, 0)
    next(gather2)
    next(gather_u)

    grads = jnp.zeros((SEQ, COLS), f32)
    for j, (start, size) in enumerate(PROJ):
        left = u[:, :, :, pl.ds(start, size)].reshape(SEQ, size)
        right = w1[:, :, pl.ds(128 + 16 * j, 16), pl.ds(0, size)].reshape(COLS, size)
        grads = grads + dot(left, right, 1, 1)
    dctx[...] = grads.astype(bf16)

    for block in (3, 2, 1, 0):
        reach = (block + 1) * 256
        rows = pl.ds(block * 256, 256)
        keys = pl.ds(0, reach)
        begin = jnp.concatenate(
            [begin_cols[:, 2 * block + i : 2 * block + i + 1] for i in range(2)], axis=0
        )
        key_index = lax.broadcasted_iota(jnp.int32, (1, reach), 1).astype(f32)
        row_index = (lax.broadcasted_iota(jnp.int32, (256, 1), 0) + block * 256).astype(f32)

        def attend(pair, carry, block=block, rows=rows, keys=keys):
            lanes = pl.ds(pl.multiple_of(pair * 128, 128), 128)
            qp, kp, vp, dp = q[rows, lanes], k[keys, lanes], v[keys, lanes], dctx[rows, lanes]
            results = []
            for half in range(2):
                here = (lane >= 64) == (half == 1)
                qh = jnp.where(here, qp, jnp.zeros((), bf16))
                dh = jnp.where(here, dp, jnp.zeros((), bf16))
                scores = dot(qh, kp, 1, 1)
                allowed = (key_index >= begin) & (key_index <= row_index)
                scores = jnp.where(allowed, scores, masked_score)
                highest = jnp.max(scores, axis=1, keepdims=True)
                weights = jnp.exp(scores - highest)
                total = jnp.sum(weights, axis=1, keepdims=True)
                probs = weights * (1.0 / total)
                log_sum = jnp.broadcast_to(highest + jnp.log(total), (256, 128))
                lse[pl.ds(pair * 2 + half, 1), rows] = jnp.transpose(log_sum)[0:1, :]
                probs_low = probs.astype(bf16)
                d_probs = dot(dh, vp, 1, 1)
                delta = jnp.sum(probs * d_probs, axis=1, keepdims=True)
                d_scores = (probs * (d_probs - delta)).astype(bf16)
                results.append(
                    (
                        dot(probs_low, vp, 1, 0),
                        dot(d_scores, kp, 1, 0),
                        dot(d_scores, qp, 0, 0),
                        dot(probs_low, dp, 0, 0),
                    )
                )
            context, d_queries, d_keys, d_values = [
                jnp.where(lane < 64, a, b) for a, b in zip(*results)
            ]
            ctx[rows, lanes] = context.astype(bf16)
            tables = [tab[i, rows, :] for i in range(3)]
            dproj[rows, lanes] = turn_back(d_queries * 0.125, *tables).astype(bf16)
            if block == 3:
                dk[keys, lanes] = d_keys
                dv[keys, lanes] = d_values
            else:
                dk[keys, lanes] += d_keys
                dv[keys, lanes] += d_values
            return carry

        lax.fori_loop(0, 2, attend, 0)
        if block == 3:
            next(gather2)
        if block == 1:
            next(gather3)

    def join(m, carry):
        rows = pl.ds(pl.multiple_of(m * 256, 256), 256)
        tables = [tab[i, rows, :] for i in range(3)]
        for pair in range(2):
            lanes = pl.ds(pair * 128, 128)
            turned = turn_back(dk[rows, lanes], *tables)
            dproj[rows, pl.ds(COLS + pair * 128, 128)] = turned.astype(bf16)
            dproj[rows, pl.ds(2 * COLS + pair * 128, 128)] = dv[rows, lanes].astype(bf16)
        return carry

    lax.fori_loop(0, 4, join, 0)

    copies1.sent()
    copies_t.sent()

    def normed_part(i, carry):
        columns = pl.ds(pl.multiple_of(i * 512, 512), 512)
        total = dot(dproj[...], w1[i, :, pl.ds(0, 128), :].reshape(512, 768), 1, 1)
        zd[:, :, :, columns] = total.astype(bf16).reshape(4, 2, 128, 512)
        return carry

    lax.fori_loop(0, 4, normed_part, 0)

    def qkv_part(i, carry):
        columns = pl.ds(pl.multiple_of(i * 512, 512), 512)
        grads = dot(n[:, :, :, :, columns].reshape(SEQ, 512), dproj[...], 0, 0).astype(bf16)
        w1[i, :, pl.ds(0, 128), :] = grads.reshape(4, 128, 768)
        return carry

    lax.fori_loop(0, 4, qkv_part, 0)
    for j, (start, size) in enumerate(PROJ):
        columns = pl.ds(start, size)
        part = (slice(None), slice(None), pl.ds(128 + 16 * j, 16), pl.ds(0, size))
        total = dot(ctx[...], w1[part].reshape(COLS, size), 1, 0)
        zo[:, :, pl.ds(0, 128), columns] = total.astype(bf16).reshape(4, 2, 128, size)
        right = u[:, :, :, columns].reshape(SEQ, size)
        w1[part] = dot(ctx[...], right, 0, 0).astype(bf16).reshape(4, 4, 16, size)
    next(reduce1)

    for b in range(8):
        part = jnp.concatenate([lse[j : j + 1, b * 128 : b * 128 + 128] for j in range(4)], axis=1)
        wide = jnp.concatenate([jnp.where(c % 4 == s, part, 0.0) for s in range(4)], axis=1)
        high = wide.astype(bf16).astype(f32)
        at = lax.broadcasted_iota(jnp.int32, (16, 1), 0)
        both = jnp.where(at == c // 4, high, jnp.where(at == 2 + c // 4, wide - high, 0.0))
        zo[b // 2, b % 2, 128:144, :] = both.astype(bf16)

    def feed(i, carry):
        rows = pl.ds(pl.multiple_of(i // 2 * 512, 512), 512)
        columns = pl.ds(pl.multiple_of(i % 2 * 512, 512), 512)
        right = w3[:, :, :, columns].reshape(WIDTH, 512)
        bias = jnp.where(i % 2 == 0, up_bias[:, 0:512], up_bias[:, 512:1024])
        h = dot(n[i // 2].reshape(512, WIDTH), right, 1, 0) + bias
        square = h * h
        tanh = jnp.tanh(0.7978845608028654 * (h + 0.044715 * square * h))
        half = 0.5 * (1.0 + tanh)
        slope = half + 0.5 * h * (1.0 - tanh * tanh) * (
            0.7978845608028654 * (1.0 + 3.0 * 0.044715 * square)
        )
        act[rows, columns] = (h * half).astype(bf16)
        dhid[rows, columns] = slope.astype(bf16)
        return carry

    lax.fori_loop(0, 1, feed, 0)
    next(reduce1)
    lax.fori_loop(1, 3, feed, 0)
    next(reduce1)
    lax.fori_loop(3, 4, feed, 0)

    def feed_back(i, carry):
        rows = pl.ds(pl.multiple_of(i // 2 * 512, 512), 512)
        columns = pl.ds(pl.multiple_of(i % 2 * 512, 512), 512)
        left = u[pl.ds(i // 2 * 2, 2)].reshape(512, WIDTH)
        d_act = dot(left, w2[pl.ds(i % 2 * 2, 2)].reshape(512, WIDTH), 1, 1)
        dhid[rows, columns] = (d_act * dhid[rows, columns].astype(f32)).astype(bf16)
        return carry

    next(gather2)
    lax.fori_loop(0, 2, feed_back, 0)
    next(reduce1)
    lax.fori_loop(2, 4, feed_back, 0)

    def normed_more(i, carry):
        columns = pl.ds(pl.multiple_of(i * 512, 512), 512)
        total = dot(dhid[...], w3[i].reshape(512, UNITS), 1, 1).reshape(4, 2, 128, 512)
        total = total + zd[:, :, :, columns].astype(f32)
        zd[:, :, :, columns] = total.astype(bf16)
        return carry

    lax.fori_loop(0, 4, normed_more, 0)
    next(reduce_d)
    next(reduce1)

    next(spread_q)
    put(w1.at[y, x, pl.ds(0, 128)], gq_out.at[z, core])
    for j, (start, size) in enumerate(PROJ):
        pt[:, start : start + size] = w1[y, x, 128 + 16 * j : 144 + 16 * j, 0:size]

    def to_owner(j):
        return pltpu.make_async_remote_copy(
            src_ref=pt,
            dst_ref=gp.at[pl.ds(16 * j, 16)],
            send_sem=sem_p.at[0, 0],
            recv_sem=sem_p.at[1, j],
            device_id=(c, owner),
            device_id_type=MESH,
        )

    for j in range(8):

        @pl.when((f % 8 == j) & (owner != f))
        def _():
            to_owner(j).start()

        @pl.when((f % 8 == j) & (owner == f))
        def _():
            local = pltpu.make_async_copy(pt, gp.at[pl.ds(16 * j, 16)], sem_p.at[0, 1])
            local.start()
            local.wait()

    copies3.sent()

    def up_part(i, carry):
        columns = pl.ds(pl.multiple_of(i * 512, 512), 512)
        grads = dot(n[:, :, :, :, columns].reshape(SEQ, 512), dhid[...], 0, 0).astype(bf16)
        w3[i] = grads.reshape(4, 128, UNITS)
        return carry

    lax.fori_loop(0, 4, up_part, 0)
    for device in (
        (c, y * 4 + up1(x)),
        (c, y * 4 + down1(x)),
        (c, up1(y) * 4 + x),
        (c, down1(y) * 4 + x),
    ):
        pl.semaphore_signal(n_free, inc=1, device_id=device, device_id_type=MESH)
    next(reduce3)
    next(reduce_d)
    pl.semaphore_signal(rc_free, inc=1, device_id=other_core(), device_id_type=MESH)
    next(spread_q)

    def out_part(i, carry):
        columns = pl.ds(pl.multiple_of(i * 512, 512), 512)
        total = dot(act[...], w2[:, :, :, columns].reshape(UNITS, 512), 1, 0)
        total = total.reshape(4, 2, 128, 512) + zo[:, :, pl.ds(0, 128), columns].astype(f32)
        zo[:, :, pl.ds(0, 128), columns] = total.astype(bf16)
        return carry

    lax.fori_loop(0, 4, out_part, 0)
    pl.semaphore_wait(rc_free, 1)
    next(reduce_o)
    next(reduce3)
    next(reduce_d)
    next(spread_q)

    copies2.sent()

    def down_part(i, carry):
        columns = pl.ds(pl.multiple_of(i * 512, 512), 512)
        right = u[:, :, :, columns].reshape(SEQ, 512)
        w2[:, :, :, columns] = dot(act[...], right, 0, 0).astype(bf16).reshape(4, 4, 64, 512)
        return carry

    lax.fori_loop(0, 4, down_part, 0)
    copies_u.sent()
    own_tokens, own_cot = u.at[0, 0], u.at[0, 1]
    again = [
        pltpu.make_async_copy(tokens, own_tokens, sem_l.at[7]),
        pltpu.make_async_copy(cotangent, own_cot, sem_l.at[8]),
    ]
    for copy in again:
        copy.start()
    pl.semaphore_wait(n_free, 4)
    next(reduce3)
    next(reduce2)
    next(reduce_o)

    for copy in again:
        copy.wait()
    next(reduce_d)
    zero = jnp.zeros((1, WIDTH), f32)

    def finish_grad(i, carry):
        d_gain, d_shift, d_bias = carry
        part = pl.ds(pl.multiple_of(i * 16, 16), 16)
        grads = zd[z, core, part, :].astype(f32)
        grads = grads + zd_r2[0, part, :].astype(f32) + zd_r2[1, part, :].astype(f32)
        values = own_tokens[part, :].astype(f32)
        average = jnp.mean(values, axis=-1, keepdims=True)
        centered = values - average
        variance = jnp.mean(centered * centered, axis=-1, keepdims=True)
        scale = lax.rsqrt(variance + epsilon)
        standard = centered * scale
        d_gain = d_gain + jnp.sum(grads * standard, axis=0, keepdims=True)
        d_shift = d_shift + jnp.sum(grads, axis=0, keepdims=True)
        scaled = grads * gain
        inner = scaled - jnp.mean(scaled, axis=-1, keepdims=True)
        inner = inner - standard * jnp.mean(scaled * standard, axis=-1, keepdims=True)
        upstream = own_cot[part, :].astype(f32)
        d_bias = d_bias + jnp.sum(upstream, axis=0, keepdims=True)
        zd_r2[0, part, :] = (upstream + scale * inner).astype(bf16)
        return d_gain, d_shift, d_bias

    d_gain, d_shift, d_bias = lax.fori_loop(0, 8, finish_grad, (zero, zero, zero))
    put(zd_r2.at[0], token_grad)

    gv[...] = jnp.zeros((4, 4, 16, 128), f32)
    for i in range(16):
        lanes = slice(i * 128, i * 128 + 128)
        gv[i // 4, i % 4, 0:1, :] = d_gain[:, lanes]
        gv[i // 4, i % 4, 1:2, :] = d_shift[:, lanes]
        gv[i // 4, i % 4, 2:3, :] = d_bias[:, lanes]
    ones = jnp.ones((8, SEQ), bf16)
    d_qkv = dot(ones, dproj[...], 1, 0)[0:1, :]
    d_up = dot(ones, dhid[...], 1, 0)[0:1, :]
    for which in range(3):
        for i in range(2):
            at = which * 16 + c * 2 + i
            start = which * COLS + i * 128
            target = at // 3
            gv[target // 4, target % 4, pl.ds(3 + at % 3, 1), :] = d_qkv[:, start : start + 128]
    for m in range(8):
        both = d_up[:, m * 128 : m * 128 + 128]
        moved = pltpu.roll(both, 64, 1)
        here = (lane >= 64) == odd
        for i, (even_place, odd_place) in enumerate(((both, moved), (moved, both))):
            at = 2 * m + i
            term = jnp.where(here, jnp.where(odd, odd_place, even_place), 0.0)
            gv[at // 4, at % 4, pl.ds(6 + c // 2, 1), :] = term
    next(reduce_v)

    def trade(k, src, dst, device):
        return pltpu.make_async_remote_copy(
            src_ref=src,
            dst_ref=dst,
            send_sem=sem_b.at[0, k],
            recv_sem=sem_b.at[1, k],
            device_id=device,
            device_id_type=MESH,
        )

    for j in range(8):

        @pl.when(own_rows & ((f % 2) * 8 + j != f))
        def _():
            slot = gp.at[pl.ds(16 * j, 16)]
            pltpu.make_async_remote_copy(
                src_ref=slot,
                dst_ref=slot,
                send_sem=sem_p.at[0, 0],
                recv_sem=sem_p.at[1, j],
                device_id=other_core(),
                device_id_type=MESH,
            ).wait_recv()

    mine = core == x // 2
    turns = (z - y + 4) % 4
    to_zu, to_zd = (up1(z) * 2 + core, f), (down1(z) * 2 + core, f)
    to_core = other_core()
    h0, h1 = gp.at[pl.ds(0, 64)], gp.at[pl.ds(64, 64)]

    @pl.when(mine & (turns == 0))
    def _():
        trade(0, gp, gp, to_zu).start()
        trade(1, gp, gp, to_zd).start()

    @pl.when(mine & (turns == 1))
    def _():
        trade(0, gp, gp, to_core).wait_recv()
        trade(2, h0, h0, to_zu).start()

    @pl.when(mine & (turns == 3))
    def _():
        trade(1, gp, gp, to_core).wait_recv()
        trade(3, h1, h1, to_zd).start()

    next(spread_q)
    next(reduce_o)
    next(reduce_v)
    next(reduce3)
    next(reduce2)
    next(reduce_v)

    @pl.when(mine & (turns == 2))
    def _():
        trade(2, h0, h0, to_core).wait_recv()
        trade(3, h1, h1, to_core).wait_recv()

    @pl.when(mine)
    def _():
        trade(4, gp, gp, to_core).start()

    next(reduce_o)
    proj_bias, down_bias = joined(2), joined(3)

    def finish_out(i, carry):
        part = pl.ds(pl.multiple_of(i * 16, 16), 16)
        total = zo[z, core, part, :].astype(f32)
        total = total + zo_r2[0, part, :].astype(f32) + zo_r2[1, part, :].astype(f32)
        total = own_tokens[part, :].astype(f32) + total + proj_bias + down_bias
        zo_r2[0, part, :] = total.astype(bf16)
        return carry

    tail = pl.ds(128, 16)
    sums = zo[z, core, tail, :].astype(f32)
    sums = sums + zo_r2[0, tail, :].astype(f32) + zo_r2[1, tail, :].astype(f32)
    sums = sums[0:2, :] + sums[2:4, :]
    for h in range(32):
        lse_own[h : h + 1, :] = sums[h // 16 : h // 16 + 1, (h % 16) * 128 : (h % 16) * 128 + 128]
    lax.fori_loop(0, 8, finish_out, 0)
    put(zo_r2.at[0, pl.ds(0, 128)], block_out)
    put(lse_own, lse_out)

    next(reduce_v)
    next(reduce3)
    next(spread_u)
    put(w3.at[y, x], gu_out.at[z, core])
    next(reduce2)
    next(reduce_v)
    next(spread_v)
    put(gv.at[y, x], gv_out.at[z, core])
    next(spread_u)
    next(reduce2)
    next(spread_v)
    next(spread_u)
    next(reduce2)
    next(spread_d)
    put(w2.at[y, x], gd_out.at[z, core])

    @pl.when(jnp.logical_not(mine))
    def _():
        trade(4, gp, gp, to_core).wait_recv()

    put(gp, gp_out)
    next(spread_v)
    next(spread_d)
    next(spread_u)
    next(spread_v)
    next(spread_d)
    next(spread_d)

    for copies in (
        copies_r1, copies_r2, copies_r3, copies_v, copies_zo, copies_zd,
        copies_lq, copies_lu, copies_ld, copies_lv,
    ):
        copies.sent()
    for j in range(8):
        target = (f % 2) * 8 + j

        @pl.when(own_rows & (target != f))
        def _():
            scatter(j, target).wait_send()

    @pl.when(owner != f)
    def _():
        to_owner(0).wait_send()

    @pl.when(mine & (turns == 0))
    def _():
        trade(0, gp, gp, to_zu).wait_send()
        trade(1, gp, gp, to_zd).wait_send()

    @pl.when(mine & (turns == 1))
    def _():
        trade(2, h0, h0, to_zu).wait_send()

    @pl.when(mine & (turns == 3))
    def _():
        trade(3, h1, h1, to_zd).wait_send()

    @pl.when(mine)
    def _():
        trade(4, gp, gp, to_core).wait_send()

    for copy in outs:
        copy.wait()


def layer_call(*operands):
    anyspace = pl.BlockSpec(memory_space=pl.ANY)
    vmem = pl.BlockSpec(memory_space=VM)
    dma = pltpu.SemaphoreType.DMA
    return pl.pallas_call(
        layer_kernel,
        out_shape=[
            jax.ShapeDtypeStruct((128, WIDTH), bf16),
            jax.ShapeDtypeStruct((128, WIDTH), bf16),
            jax.ShapeDtypeStruct((32, 128), f32),
            jax.ShapeDtypeStruct((4, 2, 128, 768), bf16),
            jax.ShapeDtypeStruct((4, 2, 128, UNITS), bf16),
            jax.ShapeDtypeStruct((4, 2, 64, WIDTH), bf16),
            jax.ShapeDtypeStruct((128, WIDTH), bf16),
            jax.ShapeDtypeStruct((4, 2, 16, 128), f32),
        ],
        in_specs=[anyspace] * 6 + [vmem] * 7,
        out_specs=[anyspace] * 8,
        scratch_shapes=[
            VM((4, 4, 192, 768), bf16),
            VM((4, 4, 64, WIDTH), bf16),
            VM((4, 4, 128, UNITS), bf16),
            VM((4, 2, 144, WIDTH), bf16),
            VM((4, 2, 128, WIDTH), bf16),
            VM((2, 2, 8, 32, WIDTH), bf16),
            VM((4, 2, 128, WIDTH), bf16),
            VM((4, 144, WIDTH), bf16),
            VM((2, 80, WIDTH), bf16),
            VM((2, 144, WIDTH), bf16),
            VM((2, 64, WIDTH), bf16),
            VM((2, 128, WIDTH), bf16),
            VM((2, 8, 96, 768), bf16),
            VM((2, 8, 80, 768), bf16),
            VM((2, 8, 64, UNITS), bf16),
            VM((2, 8, 64, UNITS), bf16),
            VM((16, 16, 128), f32),
            VM((3, SEQ, 128), f32),
            VM((128, 128), f32),
            VM((SEQ, COLS), bf16),
            VM((SEQ, COLS), bf16),
            VM((SEQ, COLS), bf16),
            VM((SEQ, COLS), bf16),
            VM((SEQ, COLS), bf16),
            VM((SEQ, COLS), f32),
            VM((SEQ, COLS), f32),
            VM((SEQ, 768), bf16),
            VM((SEQ, UNITS), bf16),
            VM((SEQ, UNITS), bf16),
            VM((8, SEQ), f32),
            VM((32, 128), f32),
            VM((16, WIDTH), bf16),
            VM((128, WIDTH), bf16),
            VM((4, 4, 16, 128), f32),
            VM((3, 4, 16, 128), f32),
            VM((3, 16, 128), f32),
            dma((2, 16)),
            dma((2, 16)),
            dma((2, 16)),
            dma((2, 8)),
            dma((2, 8)),
            dma((2, 16)),
            dma((2, 16)),
            dma((2, 16)),
            dma((2, 6)),
            dma((2, 5)),
            dma((2, 5)),
            dma((2, 8)),
            dma((2, 8)),
            dma((2, 8)),
            dma((2, 8)),
            dma((2, 8)),
            dma((2, 8)),
            dma((2, 5)),
            dma((9,)),
            dma((8,)),
            pltpu.SemaphoreType.REGULAR,
            pltpu.SemaphoreType.REGULAR,
        ],
        compiler_params=pltpu.CompilerParams(
            collective_id=1, has_side_effects=True, vmem_limit_bytes=62 * 1024 * 1024
        ),
        cost_estimate=pl.CostEstimate(
            flops=45 * 10**9, bytes_accessed=40 * 10**6, transcendentals=4 * 10**6
        ),
        name="layer",
    )(*operands)


def finish_kernel(gq, gu, gd, gp, gv, qkv_out, up_out, down_out, proj_out, vec_out):
    lane = lax.broadcasted_iota(jnp.int32, (1, 128), 1)
    for which in range(3):
        for c in range(8):
            part = gq[c, :, which * COLS : which * COLS + COLS]
            qkv_out[:, which * WIDTH + c * COLS : which * WIDTH + (c + 1) * COLS] = part.astype(f32)
    for pair in range(4):
        for m in range(8):
            a = gu[2 * pair, :, 128 * m : 128 * m + 128].astype(f32)
            b = gu[2 * pair + 1, :, 128 * m : 128 * m + 128].astype(f32)
            for odd in range(2):
                at = (2 * m + odd) * 512 + pair * 128
                up_out[:, at : at + 128] = halves_packed(a, b, odd == 1, lane)
    down_out[...] = gd[0].astype(f32)
    proj_out[...] = gp[...].astype(f32)
    vec_out[...] = jnp.sum(gv[...], axis=0)


def finish_call(gq, gu, gd, gp, gv):
    steps = 4
    rows = 128 // steps
    return pl.pallas_call(
        finish_kernel,
        grid=(steps,),
        out_shape=[
            jax.ShapeDtypeStruct((128, 3 * WIDTH), f32),
            jax.ShapeDtypeStruct((128, HIDDEN), f32),
            jax.ShapeDtypeStruct((512, WIDTH), f32),
            jax.ShapeDtypeStruct((128, WIDTH), f32),
            jax.ShapeDtypeStruct((16, 128), f32),
        ],
        in_specs=[
            pl.BlockSpec((8, rows, 768), lambda i: (0, i, 0)),
            pl.BlockSpec((8, rows, UNITS), lambda i: (0, i, 0)),
            pl.BlockSpec((1, 128, WIDTH), lambda i: (i, 0, 0)),
            pl.BlockSpec((rows, WIDTH), lambda i: (i, 0)),
            pl.BlockSpec((8, 16, 128), lambda i: (0, 0, 0)),
        ],
        out_specs=[
            pl.BlockSpec((rows, 3 * WIDTH), lambda i: (i, 0)),
            pl.BlockSpec((rows, HIDDEN), lambda i: (i, 0)),
            pl.BlockSpec((128, WIDTH), lambda i: (i, 0)),
            pl.BlockSpec((rows, WIDTH), lambda i: (i, 0)),
            pl.BlockSpec((16, 128), lambda i: (0, 0)),
        ],
        compiler_params=pltpu.CompilerParams(vmem_limit_bytes=40 * 1024 * 1024),
        cost_estimate=pl.CostEstimate(
            flops=10**6, bytes_accessed=20 * 10**6, transcendentals=0
        ),
        name="finish",
    )(gq, gu, gd, gp, gv)


def local(
    tokens,
    segments,
    ln_gain,
    ln_shift,
    qkv_weight,
    qkv_bias,
    proj_weight,
    proj_bias,
    up_weight,
    up_bias,
    down_weight,
    down_bias,
    cotangent,
):
    block_out, token_grad, log_sums, gq, gu, gd, gp, gv = layer_call(
        tokens[0],
        cotangent[0],
        qkv_weight,
        proj_weight,
        up_weight,
        down_weight,
        segments,
        ln_gain[None],
        ln_shift[None],
        proj_bias[None],
        down_bias[None],
        qkv_bias[None],
        up_bias[None],
    )
    qkv_grad, up_grad, down_grad, proj_grad, vectors = finish_call(
        gq.reshape(8, 128, 768),
        gu.reshape(8, 128, UNITS),
        gd.reshape(4, 128, WIDTH),
        gp,
        gv.reshape(8, 16, 128),
    )
    return (
        block_out[None],
        token_grad[None],
        log_sums[None],
        vectors[0],
        vectors[1],
        qkv_grad,
        vectors[3:6].reshape(384),
        proj_grad,
        vectors[2],
        up_grad,
        vectors[6:10].reshape(512),
        down_grad,
        vectors[2],
    )


def solution(mesh):
    in_specs = (
        P("fsdp", "ctx", None),
        P("fsdp", "ctx"),
        P("fsdp"),
        P("fsdp"),
        P("fsdp", None),
        P("fsdp"),
        P("fsdp", None),
        P("fsdp"),
        P("fsdp", None),
        P("fsdp"),
        P("fsdp", None),
        P("fsdp"),
        P("fsdp", "ctx", None),
    )
    out_specs = (
        P("fsdp", "ctx", None),
        P("fsdp", "ctx", None),
        P("fsdp", None, "ctx"),
        P("fsdp"),
        P("fsdp"),
        P("fsdp", None),
        P("fsdp"),
        P("fsdp", None),
        P("fsdp"),
        P("fsdp", None),
        P("fsdp"),
        P("fsdp", None),
        P("fsdp"),
    )
    return jax.shard_map(local, mesh=mesh, in_specs=in_specs, out_specs=out_specs, check_vma=False)
```

time: 709 us -> 256 us (0.36)
  waiting for transfers between devices: 422 us -> 0 us
  Pallas kernels: 127 us -> 241 us
  matrix products: 44.7 us -> 0 us
  local copies, waits for them, and re-layouts: 54.4 us -> 13.4 us
  other arithmetic: 33.1 us -> 0 us
  between operations: 16.1 us -> 0.67 us
  starting transfers between devices: 7.24 us -> 0 us
    psum x3 -> x0, waiting for transfers between devices: 210 us -> none  [the longest x1 143 us: local(): vectors = lax.psum(vectors, ('ctx', 'fsdp'))]
    reduce_scatter x4 -> x0, waiting for transfers between devices: 159 us -> none  [the longest x1 86.7 us: local(): wide = lax.psum_scatter(wide, 'fsdp', scatter_dimension=0, tiled=True)]
    pallas_call x1 -> x2, Pallas kernels: 127 us -> 241 us  [the longest x1 236 us: layer_call(): pl.pallas_call(layer_kernel, out_shape=[jax.ShapeDtypeStruct((128, WIDTH)...]
    all_gather x2 -> x0, waiting for transfers between devices: 48.2 us -> none  [the longest x1 27.5 us: local(): wide = lax.all_gather(wide, 'ctx', axis=0, tiled=False)]
    dot_general x8 -> x0, matrix products: 44.7 us -> none  [dot(): lax.dot_general(a, b, (((ca,), (cb,)), ((), ())), preferred_element_type=...]
    unnamed x40 -> x22, local copies, waits for them, and re-layouts: 27.7 us -> 9.18 us
    convert_element_type x4 -> x0, local copies, waits for them, and re-layouts: 14.5 us -> none  [the longest x2 10.1 us: local(): up_weight_grad = jnp.transpose(wide[:, :, 3 * cols:].reshape(ring, shard,...]
    convert_element_type x5 -> x0, other arithmetic: 10.7 us -> none  [the longest x1 4.13 us: local(): lax.all_gather(grad_down, 'ctx', axis=0, tiled=True).astype(f32)]
  transfers between devices with their start and end apart: 10 -> 0, of which waited for: 8 -> 0; matrix products, arithmetic and copies ran while one was open for 13% -> 0% of each run, Pallas kernels for 0% -> 0%
where the time goes in v4:
time: 256 us; the launch traced here: 255 us
  Pallas kernels  241 us (94%)
  local copies, waits for them, and re-layouts  13.4 us (5%)
    pallas_call x1, Pallas kernels, layer_call(): pl.pallas_call(layer_kernel, out_shape=[jax.ShapeDtypeStruct((128, WIDTH)...  236 us
    unnamed x22, local copies, waits for them, and re-layouts  9.18 us

profile of v4, /device:TPU:1, one launch (start us, length us, event | category | flops | bytes accessed | tf_op | source)
XLA Modules:
  0.0 255.3 jit_solution(17397148614336415519)
XLA Ops:
  0.6 1.2 broadcast_in_dim.31.qkv_bias_in
  1.9 1.3 broadcast_in_dim.32.up_bias_in
  3.1 236.3 %layer.1 = (bf16[128,2048]{1,0:T(8,128)(2,1)}, bf16[128,2048]{1,0:T(8,128)(2,1)}, f32[32,128]{1,0:T(8,128)}, bf16[4,2,128,768]{3,2,1,0:T(8,128)(2,1)}, bf16[4,2,...) custom-call(bf16[128,2048]{1,0:T(8,128)(2,1)} %bitcast.30, ...), custom_call_target="tpu_custom_call" | custom-call | flops 44999999488 | bytes 40000000 | tf_op jit(solution)/shard_map/layer/pallas_call | solution.py:1140
  239.5 0.0 copy-start
  239.5 1.6 copy-done
  241.1 0.0 copy-start.1
  241.1 1.6 copy-done.1
  242.7 0.0 copy-start.2
  242.7 1.4 copy-done.2
  244.1 0.0 copy-start.3
  244.1 1.0 copy-done.3
  245.1 0.8 copy-done.4
  246.0 5.0 %finish.1 = (f32[128,6144]{1,0:T(8,128)}, f32[128,8192]{1,0:T(8,128)}, f32[512,2048]{1,0:T(8,128)}, f32[128,2048]{1,0:T(8,128)}, f32[16,128]{1,0:T(8,128)S(1)}) custom-call(bf16[8,128,768]{2,1,0:T(8,128)(2,1)S(1)} %bitcast.25, bf16[8,128,1024]{2,1,0:T(8,128)(2,1)S(1)} %bitcast.23, bf16[4,128,2048]{2,1,0:T(8,128)(2,1)S(1)} %bitcast.24, ...), custom_call_target="tpu_custom_call" | custom-call | flops 1000000 | bytes 20000000 | tf_op jit(solution)/shard_map/finish/pallas_call | solution.py:1245
  250.9 0.5 slice_bitcast_fusion.2
  251.4 0.6 slice_bitcast_fusion.1
  252.0 0.6 slice_bitcast_fusion
  252.6 0.5 copy.30
  253.1 0.0 copy-done.6
  253.1 0.8 copy.31
  253.9 0.0 copy-done.5
  253.9 0.8 copy.32
  254.7 0.0 copy-done.7
  254.7 0.6 copy.33
  255.3 0.0 copy-done.8
  (5 shorter events, 0.0 us)
Async XLA Ops:
  239.5 1.6 copy-start
  241.1 1.6 copy-start.1
  242.7 1.4 copy-start.2
  244.1 1.0 copy-start.3
  245.1 0.8 copy-start.4
  246.0 7.2 %copy-start.6 = (bf16[128,2048]{1,0:T(8,128)(2,1)S(1)}, bf16[128,2048]{1,0:T(8,128)(2,1)}, u32[]{:S(2)}) copy-start(bf16[128,2048]{1,0:T(8,128)(2,1)} %get-tuple-element.26) | copy-start | bytes 1572868
  246.0 7.9 %copy-start.5 = (bf16[128,2048]{1,0:T(8,128)(2,1)S(1)}, bf16[128,2048]{1,0:T(8,128)(2,1)}, u32[]{:S(2)}) copy-start(bf16[128,2048]{1,0:T(8,128)(2,1)} %get-tuple-element.27) | copy-start | bytes 1572868
  250.9 3.8 %copy-start.7 = (f32[32,128]{1,0:T(8,128)S(1)}, f32[32,128]{1,0:T(8,128)}, u32[]{:S(2)}) copy-start(f32[32,128]{1,0:T(8,128)} %get-tuple-element.28) | copy-start | bytes 49156
  251.4 3.9 %copy-start.8 = (f32[128]{0:T(128)}, f32[128]{0:T(128)S(1)}, u32[]{:S(2)}) copy-start(f32[128]{0:T(128)S(1)} %get-tuple-element.89) | copy-start | bytes 1540
